TPU v7x, 128 devices: a whole 4x4x4 slice. The times are simulated.
128 devices in a mesh: seq: 16 (over y, z), head: 8 (over x, core).
Axes of the slice: x: 4, y: 4, z: 4, core: 2. Of those that a mesh axis runs over, the one named last changes fastest.
Arguments:
- queries: bfloat16 [16384, 4096], P('seq', 'head'), may hold values from -6 to 6
- keys: bfloat16 [16384, 4096], P('seq', 'head'), may hold values from -6 to 6
- values: bfloat16 [16384, 4096], P('seq', 'head'), may hold values from -6 to 6
- decay: float32 [16384, 4096], P('seq', 'head'), as said below
- beta: float32 [32, 16384], P('head', 'seq'), may hold values from 0.002 to 0.98
- wy_inverse: float32 [256, 64, 2048], P('seq', None, 'head')
- out_gate: bfloat16 [16384, 4096], P('seq', 'head'), may hold values from -6 to 6
- norm_gain: float32 [128], replicated, may hold values from 0.1 to 1.9
- out_proj: bfloat16 [4096, 2304], P('head'), may hold values from -0.125 to 0.125
- grad_out: bfloat16 [16384, 2304], P('seq', 'head'), may hold values from -6 to 6
- resets: int32 [16], P('seq'), may hold values from 0 to 16, as said below
Outputs:
- grad_queries: bfloat16 [16384, 4096], P('seq', 'head')
- grad_keys: bfloat16 [16384, 4096], P('seq', 'head')
- grad_values: bfloat16 [16384, 4096], P('seq', 'head')
- grad_decay: float32 [16384, 4096], P('seq', 'head')
- grad_beta: float32 [32, 16384], P('head', 'seq')
- grad_gate: bfloat16 [16384, 4096], P('seq', 'head')
Inputs may be any that keep to these rules, and one draw needn't show every extreme that they name: `resets`: 16 means that no document starts in that index of seq; the first value is 0 and the last is 16. Natural logarithms of decay factors, at most 0.
All inputs are finite; a program needn't handle non-finite values.
Results may differ from a plain program's by a relative error of at most 0.02.
Values may be sent and summed in bfloat16 or wider, within the bound.
No kernel may reach another device: no remote copies, remote signals or barrier semaphores. Data moves between devices by JAX's collectives and lax.ppermute only.
A program may use at most 192 MiB of HBM per device.

v0:
```python
import jax
import jax.numpy as jnp
from jax import lax
from jax.sharding import PartitionSpec as P

DK = 128
DV = 128
GROUP = 64


precise = lax.Precision.HIGHEST


def from_behind(x, axis, by):
    devices = lax.axis_size(axis)
    pairs = [(i, i + by) for i in range(devices) if 0 <= i + by < devices]
    return lax.ppermute(x, axis, pairs)


def to_blocks(array, heads, width):
    count = array.shape[0] // GROUP
    return array.reshape(count, GROUP, heads, width).transpose(0, 2, 1, 3)


def from_blocks(array):
    count, heads, length, width = array.shape
    return array.transpose(0, 2, 1, 3).reshape(count * length, heads * width)


def unit_rows(array, width, multiplier_term):
    rows = array.reshape(array.shape[0], -1, width)
    scale = lax.rsqrt(jnp.sum(rows * rows, axis=-1, keepdims=True) + 1e-06)
    return (rows * scale * multiplier_term).reshape(array.shape)


def low_product(form, left, right):
    return jnp.einsum(
        form,
        left.astype(jnp.bfloat16),
        right.astype(jnp.bfloat16),
        preferred_element_type=jnp.float32,
    )


def group_step(state, block):
    query_rows, key_rows, value_rows, gate_rows, beta_rows, wy_rows, keep_flag = block
    entry = state * keep_flag
    cumul = jnp.cumsum(gate_rows, axis=1)
    final = cumul[:, -1:, :]
    query_dec = query_rows * jnp.exp(cumul)
    key_dec = key_rows * jnp.exp(cumul)
    key_inv = key_rows * jnp.exp(-cumul)
    key_tail = key_rows * jnp.exp(final - cumul)
    lower = jnp.tril(jnp.ones((GROUP, GROUP), jnp.float32))
    predicted = jnp.einsum("hld,hdv->hlv", key_dec, entry, precision=precise)
    target = beta_rows[:, :, None] * (value_rows - predicted)
    update = low_product("hij,hjv->hiv", wy_rows, target)
    scores = low_product("hid,hjd->hij", query_dec, key_inv) * lower
    output = jnp.einsum("hld,hdv->hlv", query_dec, entry, precision=precise)
    output = output + low_product("hij,hjv->hiv", scores, update)
    carried = jnp.exp(final[:, 0, :])[:, :, None] * entry
    carried = carried + low_product("hld,hlv->hdv", key_tail, update)
    return (carried, output)


def core(query_unit, key_unit, value_f, decay, beta, wy_inverse, keep, state):
    heads = beta.shape[0]
    count = query_unit.shape[0] // GROUP
    blocks = (
        to_blocks(query_unit, heads, DK),
        to_blocks(key_unit, heads, DK),
        to_blocks(value_f, heads, DV),
        to_blocks(decay, heads, DK),
        beta.reshape(heads, count, GROUP).transpose(1, 0, 2),
        wy_inverse.reshape(count, GROUP, heads, GROUP).transpose(0, 2, 1, 3),
        keep,
    )
    final, outputs = lax.scan(jax.checkpoint(group_step), state, blocks)
    return (from_blocks(outputs), final)


def transition(key_unit, decay, beta, wy_inverse, keep):
    heads = beta.shape[0]
    count = key_unit.shape[0] // GROUP
    blocks = (
        to_blocks(key_unit, heads, DK),
        to_blocks(decay, heads, DK),
        beta.reshape(heads, count, GROUP).transpose(1, 0, 2),
        wy_inverse.reshape(count, GROUP, heads, GROUP).transpose(0, 2, 1, 3),
        keep,
    )
    identity = jnp.broadcast_to(jnp.eye(DK, dtype=jnp.float32), (heads, DK, DK))

    def advance(total, block):
        key_rows, gate_rows, beta_rows, wy_rows, keep_flag = block
        cumul = jnp.cumsum(gate_rows, axis=1)
        final = cumul[:, -1:, :]
        key_dec = key_rows * jnp.exp(cumul)
        key_tail = key_rows * jnp.exp(final - cumul)
        mixed = jnp.einsum(
            "hij,hjd->hid", wy_rows, beta_rows[:, :, None] * key_dec, precision=precise
        )
        matrix = identity * jnp.exp(final[:, 0, :])[:, :, None]
        matrix = (
            matrix - jnp.einsum("hld,hle->hde", key_tail, mixed, precision=precise)
        ) * keep_flag
        return (jnp.einsum("hij,hjk->hik", matrix, total, precision=precise), None)

    product, _ = lax.scan(advance, identity, blocks)
    return product


def gated_norm(output, gate, gain):
    rows = output.reshape(output.shape[0], -1, DV)
    scale = lax.rsqrt(jnp.mean(rows * rows, axis=-1, keepdims=True) + 1e-06)
    gates = jax.nn.sigmoid(gate.reshape(rows.shape))
    return (rows * scale * gain * gates).reshape(output.shape)


def apply_map(matrix, state):
    return jnp.einsum("hij,hjk->hik", matrix, state, precision=precise)


def per_device(
    queries, keys, values, decay, beta, wy_inverse, out_gate, norm_gain, out_proj, grad_out, resets
):
    tokens_here = queries.shape[0]
    heads = beta.shape[0]
    count = tokens_here // GROUP
    upstream = lax.dot_general(
        lax.all_gather(grad_out, "head", axis=1, tiled=True),
        out_proj,
        (((1,), (1,)), ((), ())),
        preferred_element_type=jnp.float32,
    )
    keep = (jnp.arange(count) != resets[0]).astype(jnp.float32)
    query_f = queries.astype(jnp.float32)
    key_f = keys.astype(jnp.float32)
    value_f = values.astype(jnp.float32)
    gate_f = out_gate.astype(jnp.float32)

    def normalize(query_in, key_in):
        return (unit_rows(query_in, DK, DK ** (-0.5)), unit_rows(key_in, DK, 1.0))

    (query_unit, key_unit), unit_pull = jax.vjp(normalize, query_f, key_f)
    empty = jnp.zeros((heads, DK, DV), jnp.float32)
    _, offset = core(query_unit, key_unit, value_f, decay, beta, wy_inverse, keep, empty)
    summary = transition(key_unit, decay, beta, wy_inverse, keep)

    def relay_forward(turn, carry):
        incoming = from_behind(carry[1].astype(jnp.bfloat16), "seq", 1).astype(jnp.float32)
        return (incoming, apply_map(summary, incoming) + offset)

    state_in, _ = lax.fori_loop(0, lax.axis_size("seq"), relay_forward, (empty, offset))

    def layer(query_in, key_in, value_in, gate_log, beta_in, gate_in, state):
        output, final = core(query_in, key_in, value_in, gate_log, beta_in, wy_inverse, keep, state)
        return (gated_norm(output, gate_in, norm_gain), final)

    (normed, final), pullback = jax.vjp(
        layer, query_unit, key_unit, value_f, decay, beta, gate_f, state_in
    )
    first = pullback((upstream, jnp.zeros_like(final)))
    residual = first[6]
    flipped = summary.transpose(0, 2, 1)

    def relay_back(turn, carry):
        incoming = from_behind(carry[1].astype(jnp.bfloat16), "seq", -1).astype(jnp.float32)
        return (incoming, apply_map(flipped, incoming) + residual)

    state_grad, _ = lax.fori_loop(0, lax.axis_size("seq"), relay_back, (empty, residual))
    second = pullback((jnp.zeros_like(normed), state_grad))
    totals = [first[slot] + second[slot] for slot in range(6)]
    grad_query, grad_key = unit_pull((totals[0], totals[1]))
    return (
        grad_query.astype(jnp.bfloat16),
        grad_key.astype(jnp.bfloat16),
        totals[2].astype(jnp.bfloat16),
        totals[3],
        totals[4],
        totals[5].astype(jnp.bfloat16),
    )


def solution(mesh):
    return jax.shard_map(
        per_device,
        mesh=mesh,
        in_specs=(
            P("seq", "head"),
            P("seq", "head"),
            P("seq", "head"),
            P("seq", "head"),
            P("head", "seq"),
            P("seq", None, "head"),
            P("seq", "head"),
            P(),
            P("head", None),
            P("seq", "head"),
            P("seq"),
        ),
        out_specs=(
            P("seq", "head"),
            P("seq", "head"),
            P("seq", "head"),
            P("seq", "head"),
            P("head", "seq"),
            P("seq", "head"),
        ),
        check_vma=False,
    )
```

profile of v0, /device:TPU:0, one launch (start us, length us, event | category | flops | bytes accessed | tf_op | source)
XLA Modules:
  0.0 1375.4 jit_solution(17905217658942099016)
XLA Ops:
  49.4 89.3 %while.115 = (s32[]{:T(128)}, f32[4,128,128]{2,1,0:T(8,128)S(1)}, f32[16,4,64,128]{3,2,1,0:T(8,128)}, f32[16]{0:T(128)S(1)}, f32[16,4,64,128]{3,2,1,0:T(8,128)},...) while((s32[]{:T(128)}, f32[4,128,128]{2,1,0:T(8,128)S(1)}, ...), condition=%wide.region_3.4_spmd.clone, body=%wide.region_1.3_spmd.clone.sunk | while | flops 65634304 | bytes 2181264 | solution.py:78
  139.4 90.5 %while.113 = (s32[]{:T(128)}, f32[4,128,128]{2,1,0:T(8,128)S(1)}, f32[16,4,64,128]{3,2,1,0:T(8,128)}, f32[16,4,64,128]{3,2,1,0:T(8,128)}, f32[16,4,64,64]{3,2,1,...) while((s32[]{:T(128)}, f32[4,128,128]{2,1,0:T(8,128)S(1)}, ...), condition=%wide.region_6.7_spmd.clone, body=%wide.region_4.6_spmd.clone.sunk | while | flops 178552832 | bytes 3097725 | solution.py:109
  237.8 149.5 %while.110 = (s32[]{:T(128)}, f32[4,128,128]{2,1,0:T(8,128)}, bf16[4,128,128]{2,1,0:T(8,128)(2,1)S(1)}, f32[4,128,128]{2,1,0:T(8,128)S(1)}, f32[4,128,128]{2,1,0:T(8,128)S(1)}, /*index=5*/s32[]{:T(128)}) while((s32[]{:T(128)}, f32[4,128,128]{2,1,0:T(8,128)}, bf16[4,128,128]{2,1,0:T(8,128)(2,1)S(1)}, f32[4,128,128]{2,1,0:T(8,128)S(1)}, ...), condition=%wide.region_8.9_spmd, body=%wide.region_7.8_spmd.sunk | while | flops 100859904 | bytes 1704045 | solution.py:154
  285.5 6.5 collective-permute-start
  295.5 6.5 collective-permute-start
  306.0 6.8 collective-permute-start
  317.3 6.7 collective-permute-start
  337.4 6.5 collective-permute-start
  347.4 6.5 collective-permute-start
  357.4 6.5 collective-permute-start
  367.4 6.5 collective-permute-start
  377.4 6.5 collective-permute-start
  388.9 180.5 %while.114 = (s32[]{:T(128)}, f32[4,128,128]{2,1,0:T(8,128)S(1)}, f32[16,4,64,128]{3,2,1,0:T(8,128)}, f32[16,4,128,128]{3,2,1,0:T(8,128)}, f32[16,4,64,128]{3,2,...) while((s32[]{:T(128)}, f32[4,128,128]{2,1,0:T(8,128)S(1)}, ...), condition=%wide.region_12.13_spmd.clone, body=%wide.region_10.12_spmd.clone.sunk | while | flops 124559360 | bytes 4396181 | solution.py:78
  607.1 264.7 %while.116 = (s32[]{:T(128)}, f32[4,128,128]{2,1,0:T(8,128)S(1)}, f32[16,4,64,128]{3,2,0,1:T(8,128)}, f32[16,4,64,128]{3,2,0,1:T(8,128)}, f32[16,4,64,128]{3,2,1...) while((s32[]{:T(128)}, f32[4,128,128]{2,1,0:T(8,128)S(1)}, ...), condition=%wide.region_21.22_spmd.clone, body=%wide.region_15.21_spmd.clone.sunk | while | flops 304668416 | bytes 13037335 | solution.py:78
  872.6 163.6 %while.111 = (s32[]{:T(128)}, f32[4,128,128]{2,1,0:T(8,128)}, bf16[4,128,128]{2,1,0:T(8,128)(2,1)S(1)}, f32[4,128,128]{2,1,0:T(8,128)S(1)}, f32[4,128,128]{2,1,0:T(8,128)S(1)}, /*index=5*/s32[]{:T(128)}) while((s32[]{:T(128)}, f32[4,128,128]{2,1,0:T(8,128)}, bf16[4,128,128]{2,1,0:T(8,128)(2,1)S(1)}, f32[4,128,128]{2,1,0:T(8,128)S(1)}, ...), condition=%wide.region_23.24_spmd, body=%wide.region_22.23_spmd.sunk | while | flops 100859904 | bytes 1704045 | solution.py:171
  873.9 8.4 collective-permute-done.1
  884.6 9.7 collective-permute-done.1
  896.6 8.7 collective-permute-done.1
  907.6 6.5 collective-permute-done.1
  916.4 7.5 collective-permute-done.1
  926.2 7.7 collective-permute-done.1
  936.2 7.7 collective-permute-done.1
  946.1 7.8 collective-permute-done.1
  956.2 9.3 collective-permute-done.1
  967.7 8.6 collective-permute-done.1
  978.6 7.4 collective-permute-done.1
  988.3 7.1 collective-permute-done.1
  997.7 7.6 collective-permute-done.1
  1007.6 7.7 collective-permute-done.1
  1017.6 7.7 collective-permute-done.1
  1027.5 7.7 collective-permute-done.1
  1042.5 271.2 %while.112 = (s32[]{:T(128)}, f32[4,128,128]{2,1,0:T(8,128)S(1)}, f32[16,4,64,128]{3,2,0,1:T(8,128)}, f32[16,4,64,128]{3,2,0,1:T(8,128)}, f32[16,4,64,128]{3,2,1...) while((s32[]{:T(128)}, f32[4,128,128]{2,1,0:T(8,128)S(1)}, ...), condition=%wide.region_31.32_spmd, body=%wide.region_25.31_spmd.sunk | while | flops 304602880 | bytes 12513029 | solution.py:78
  (1732 shorter events, 1165.7 us)
Async XLA Ops:
  7.2 573.3 %all-gather.2.cloned.1.call-start = ((), (), s32[]{:S(2)}) async-start(), calls=%async_computation | async-start | bytes 5308416 | tf_op jit(solution)/shard_map/all_gather | solution.py:131
  245.4 6.9 collective-permute-start
  253.3 6.9 collective-permute-start
  261.2 6.9 collective-permute-start
  269.0 6.9 collective-permute-start
  276.9 7.6 collective-permute-start
  285.5 9.0 collective-permute-start
  295.5 9.5 collective-permute-start
  306.0 10.3 collective-permute-start
  317.3 9.2 collective-permute-start
  327.5 8.9 collective-permute-start
  337.4 9.0 collective-permute-start
  347.4 9.0 collective-permute-start
  357.4 9.0 collective-permute-start
  367.4 9.0 collective-permute-start
  377.4 9.0 collective-permute-start
  872.6 9.7 collective-permute-start.1
  883.3 11.0 collective-permute-start.1
  895.3 10.0 collective-permute-start.1
  906.3 7.8 collective-permute-start.1
  915.1 8.8 collective-permute-start.1
  924.9 9.0 collective-permute-start.1
  934.9 9.0 collective-permute-start.1
  944.8 9.1 collective-permute-start.1
  954.9 10.6 collective-permute-start.1
  966.4 9.9 collective-permute-start.1
  977.3 8.7 collective-permute-start.1
  987.0 8.4 collective-permute-start.1
  996.4 8.9 collective-permute-start.1
  1006.3 9.0 collective-permute-start.1
  1016.3 9.0 collective-permute-start.1
  1026.2 9.0 collective-permute-start.1
  (20 other events, 629.6 us)
Sparse Core Ops, SparseCore 0:
  9.7 36.7 all-gather.1
where the time goes:
time: 1400 us; the launch traced here: 1380 us
  matrix products  545 us (39%)
  local copies, waits for them, and re-layouts  373 us (27%)
  waiting for transfers between devices  169 us (12%)
  other arithmetic  152 us (11%)
  starting transfers between devices  112 us (8%)
  between operations  15.3 us (1%)
    dot_general x128, matrix products, group_step(): predicted = jnp.einsum('hld,hdv->hlv', key_dec, entry, precision=precise)  198 us
    squeeze x240, local copies, waits for them, and re-layouts, core(): final, outputs = lax.scan(jax.checkpoint(group_step), state, blocks)  195 us
    dot_general x320, matrix products, low_product(): jnp.einsum(form, left.astype(jnp.bfloat16), right.astype(jnp.bfloat16), p...  169 us
    ppermute x32, waiting for transfers between devices, from_behind(): return lax.ppermute(x, axis, pairs)  169 us
    ppermute x32, starting transfers between devices, from_behind(): return lax.ppermute(x, axis, pairs)  112 us
    dot_general x80, matrix products, group_step(): output = jnp.einsum('hld,hdv->hlv', query_dec, entry, precision=precise)  101 us
    another operation x128, other arithmetic, group_step(): cumul = jnp.cumsum(gate_rows, axis=1)  49.2 us
    dynamic_slice x80, local copies, waits for them, and re-layouts, core(): final, outputs = lax.scan(jax.checkpoint(group_step), state, blocks)  47.9 us
  transfers between devices with their start and end apart: 33, of which 32 were waited for; matrix products, arithmetic and copies ran while one was open for 32% of the time, Pallas kernels for 0%

commit v1 on v0

v1 whole, which is shorter than its diff:
```python
import functools

import jax
import jax.numpy as jnp
from jax import lax
from jax.experimental import pallas as pl
from jax.experimental.pallas import tpu as pltpu
from jax.sharding import PartitionSpec as P

DK = 128
DV = 128
GROUP = 64
EPS = 1e-6
SCALE = DK**-0.5
STEP = 2
RING = 4

f32 = jnp.float32
bf16 = jnp.bfloat16


def nn(a, b):
    return lax.dot_general(a, b, (((1,), (0,)), ((), ())), preferred_element_type=f32)


def nt(a, b):
    return lax.dot_general(a, b, (((1,), (1,)), ((), ())), preferred_element_type=f32)


def tn(a, b):
    return lax.dot_general(a, b, (((0,), (0,)), ((), ())), preferred_element_type=f32)


def triangle(upper, dtype):
    row = lax.broadcasted_iota(jnp.int32, (GROUP, GROUP), 0)
    col = lax.broadcasted_iota(jnp.int32, (GROUP, GROUP), 1)
    return (row <= col if upper else row >= col).astype(dtype)


def sum_rows(weights, x):
    high = x.astype(bf16)
    low = (x - high.astype(f32)).astype(bf16)
    return nn(weights, jnp.concatenate([high, low], axis=0))


def twice(upper):
    t = triangle(upper, f32)
    return jnp.concatenate([t, t], axis=1).astype(bf16)


def inverse_norm(x):
    return lax.rsqrt(jnp.sum(x * x, axis=-1, keepdims=True) + EPS)


def cols(h):
    return slice(128 * h, 128 * h + 128)


def half(h):
    return slice(64 * h, 64 * h + 64)


def kernel_a1(
    heads, resets, k_ref, v_ref, d_ref, b_ref, w_ref,
    g_ref, wb_ref, kd_ref, kt_ref, y_ref, n_ref, pre_ref, mb_ref, state,
):
    step = pl.program_id(0)

    @pl.when(step == 0)
    def _():
        row = lax.broadcasted_iota(jnp.int32, (256, 128), 0)
        col = lax.broadcasted_iota(jnp.int32, (256, 128), 1)
        for h in range(heads):
            state[h] = (row == col + 128).astype(f32)

    weights = twice(False)
    for c in range(STEP):
        rows = half(c)
        keep = (step * STEP + c != resets[0]).astype(f32)
        gamma = sum_rows(weights, d_ref[rows, :])
        g_ref[rows, :] = gamma
        for h in range(heads):
            g = gamma[:, cols(h)]
            last = g[63:64, :]
            k = k_ref[rows, cols(h)].astype(f32)
            ku = k * inverse_norm(k)
            kd = (ku * jnp.exp(g)).astype(bf16)
            kt = (ku * jnp.exp(last - g)).astype(bf16)
            wb = (w_ref[c, :, half(h)] * b_ref[h : h + 1, half(c)]).astype(bf16)
            xy = nn(wb, jnp.concatenate([v_ref[rows, cols(h)], kd], axis=1)).astype(bf16)
            bn = tn(xy, kt)
            n = bn[128:].astype(bf16)
            r = state[h] * keep
            rb = r.astype(bf16)
            r = jnp.exp(last) * r - nn(rb, n)
            state[h, 0:128] = r[0:128] + bn[0:128]
            state[h, 128:256] = r[128:256]
            wb_ref[c, :, half(h)] = wb
            kd_ref[rows, cols(h)] = kd
            kt_ref[rows, cols(h)] = kt
            y_ref[rows, cols(h)] = xy[:, 128:]
            n_ref[c, h] = n
            pre_ref[c, h] = rb

    @pl.when(step == pl.num_programs(0) - 1)
    def _():
        mb_ref[...] = state[...].astype(bf16)


def kernel_a2(heads, q_ref, k_ref, g_ref, qd_ref, ki_ref, a_ref, at_ref):
    lower = triangle(False, f32)
    upper = triangle(True, f32)
    for c in range(STEP):
        rows = half(c)
        for h in range(heads):
            g = g_ref[rows, cols(h)]
            q = q_ref[rows, cols(h)].astype(f32)
            k = k_ref[rows, cols(h)].astype(f32)
            qd = (q * (inverse_norm(q) * SCALE) * jnp.exp(g)).astype(bf16)
            ki = (k * inverse_norm(k) * jnp.exp(-g)).astype(bf16)
            qd_ref[rows, cols(h)] = qd
            ki_ref[rows, cols(h)] = ki
            a_ref[c, :, half(h)] = (nt(qd, ki) * lower).astype(bf16)
            at_ref[c, :, half(h)] = (nt(ki, qd) * upper).astype(bf16)


def kernel_b(
    heads, v_ref, kd_ref, qd_ref, y_ref, wb_ref, a_ref, at_ref, pre_ref, gate_ref, up_ref, gain_ref, s_ref,
    e_ref, vp_ref, u_ref, do_ref, du_ref, dt_ref, dg_ref, r_ref, total,
):
    step = pl.program_id(0)

    @pl.when(step == 0)
    def _():
        total[...] = jnp.zeros_like(total)

    gain = gain_ref[...]
    for c in range(STEP):
        rows = half(c)
        for h in range(heads):
            m = pre_ref[c, h, 128:256]
            e = (pre_ref[c, h, 0:128].astype(f32) + nn(s_ref[h], m)).astype(bf16)
            e_ref[c, h] = e
            qd = qd_ref[rows, cols(h)]
            both = nt(jnp.concatenate([kd_ref[rows, cols(h)], qd], axis=0), e)
            vp = (v_ref[rows, cols(h)].astype(f32) - both[0:64]).astype(bf16)
            u = nn(wb_ref[c, :, half(h)], vp).astype(bf16)
            o = both[64:128] + nn(a_ref[c, :, half(h)], u)
            rms = lax.rsqrt(jnp.mean(o * o, axis=-1, keepdims=True) + EPS)
            sig = jax.nn.sigmoid(gate_ref[rows, cols(h)].astype(f32))
            w = up_ref[rows, cols(h)].astype(f32) * gain * sig
            on = o * rms
            won = w * on
            dg_ref[rows, cols(h)] = (won * (1.0 - sig)).astype(bf16)
            do = (rms * (w - on * jnp.mean(won, axis=-1, keepdims=True))).astype(bf16)
            du = nn(at_ref[c, :, half(h)], do).astype(bf16)
            dt = tn(
                jnp.concatenate([do, du], axis=0),
                jnp.concatenate([qd, -y_ref[rows, cols(h)]], axis=0),
            ).astype(bf16)
            total[h] += nt(dt, m)
            vp_ref[rows, cols(h)] = vp
            u_ref[rows, cols(h)] = u
            do_ref[rows, cols(h)] = do
            du_ref[rows, cols(h)] = du
            dt_ref[c, h] = dt

    @pl.when(step == pl.num_programs(0) - 1)
    def _():
        r_ref[...] = total[...].astype(bf16)


def kernel_c1(heads, q_ref, k_ref, g_ref, qd_ref, ki_ref, u_ref, do_ref, e_ref, dq_ref, dgam_ref, kk_ref):
    lower = triangle(False, f32)
    upper = triangle(True, f32)
    for c in range(STEP):
        rows = half(c)
        for h in range(heads):
            u = u_ref[rows, cols(h)]
            do = do_ref[rows, cols(h)]
            da = (nt(do, u) * lower).astype(bf16)
            dat = (nt(u, do) * upper).astype(bf16)
            g = g_ref[rows, cols(h)]
            dqu = (nn(do, e_ref[c, h]) + nn(da, ki_ref[rows, cols(h)])) * jnp.exp(g)
            dku = nn(dat, qd_ref[rows, cols(h)]) * jnp.exp(-g)
            q = q_ref[rows, cols(h)].astype(f32)
            k = k_ref[rows, cols(h)].astype(f32)
            rq = inverse_norm(q)
            qn = q * rq
            prod = qn * dqu
            along = jnp.sum(prod, axis=-1, keepdims=True)
            dq_ref[rows, cols(h)] = ((rq * SCALE) * (dqu - qn * along)).astype(bf16)
            dgam_ref[rows, cols(h)] = prod * SCALE - (k * inverse_norm(k)) * dku
            kk_ref[rows, cols(h)] = dku.astype(bf16)


def kernel_c2(
    heads, resets, k_ref, g_ref, b_ref, wb_ref, kt_ref, n_ref, e_ref, vp_ref, u_ref, du_ref, dt_ref,
    dgam_ref, kk_ref, gin_ref, dk_ref, dv_ref, dd_ref, db_ref, state,
):
    step = pl.program_id(0)
    place = pl.num_programs(0) - 1 - step

    @pl.when(step == 0)
    def _():
        state[...] = gin_ref[...].astype(f32)

    weights = twice(True)
    ones = jnp.ones((16, 128), bf16)
    for c in reversed(range(STEP)):
        rows = half(c)
        keep = (place * STEP + c != resets[0]).astype(f32)
        for h in range(heads):
            grad = state[h]
            gb = grad.astype(bf16)
            e = e_ref[c, h]
            u = u_ref[rows, cols(h)]
            g = g_ref[rows, cols(h)]
            last = g[63:64, :]
            lam = jnp.exp(last)
            state[h] = keep * (dt_ref[c, h].astype(f32) + lam * grad - nt(gb, n_ref[c, h]))
            du = (du_ref[rows, cols(h)].astype(f32) + nt(kt_ref[rows, cols(h)], gb)).astype(bf16)
            dv = tn(wb_ref[c, :, half(h)], du)
            dvb = dv.astype(bf16)
            dv_ref[rows, cols(h)] = dvb
            weighed = (dv * vp_ref[rows, cols(h)].astype(f32)).astype(bf16)
            db_ref[h : h + 1, half(c)] = nt(ones, weighed)[0:1] / b_ref[h : h + 1, half(c)]
            kdd = nn(dvb, e) * jnp.exp(g)
            ktt = nn(u, gb) * jnp.exp(last - g)
            k = k_ref[rows, cols(h)].astype(f32)
            rk = inverse_norm(k)
            ku = k * rk
            dku = kk_ref[rows, cols(h)].astype(f32) + ktt - kdd
            along = jnp.sum(ku * dku, axis=-1, keepdims=True)
            dk_ref[rows, cols(h)] = (rk * (dku - ku * along)).astype(bf16)
            kutt = ku * ktt
            dgam = dgam_ref[rows, cols(h)] - ku * kdd - kutt
            dlast = jnp.sum(kutt, axis=0, keepdims=True) + lam * jnp.sum(
                grad * e.astype(f32), axis=0, keepdims=True
            )
            dd_ref[rows, cols(h)] = sum_rows(weights, dgam) + dlast


def gather_slots(me, own, others, slots, part=slice(None)):
    slots[me] = own[:, part]
    for shift, other in enumerate(others, 1):
        slots[lax.rem(me + RING - shift, RING)] = other[:, part]


def kernel_f1(heads, place, own, p1, p2, p3, total_ref, slots):
    gather_slots(place[1], own, (p1, p2, p3), slots)
    for h in range(heads):
        r = slots[0, h].astype(f32)
        for z in range(1, RING):
            r = nn(r.astype(bf16), slots[z, h, 128:256])
            r = jnp.concatenate([r[0:128] + slots[z, h, 0:128].astype(f32), r[128:256]], axis=0)
        total_ref[h] = r.astype(bf16)
    return


def kernel_f2(heads, place, own, p1, p2, p3, zslots, s_ref, yslots):
    gather_slots(place[0], own, (p1, p2, p3), yslots)
    for h in range(heads):
        s = jnp.zeros((DV, DK), f32)
        for slots, me in ((yslots, place[0]), (zslots, place[1])):
            for i in range(RING - 1):
                moved = nn(s.astype(bf16), slots[i, h, 128:256]) + slots[i, h, 0:128].astype(f32)
                s = jnp.where(i < me, moved, s)
        s_ref[h] = s.astype(bf16)


def kernel_r1(heads, place, own, p1, p2, p3, zslots, total_ref, slots):
    gather_slots(place[1], own, (p1, p2, p3), slots)
    for h in range(heads):
        g = slots[RING - 1, h].astype(f32)
        for z in reversed(range(RING - 1)):
            g = nt(g.astype(bf16), zslots[z, h, 128:256]) + slots[z, h].astype(f32)
        total_ref[h] = g.astype(bf16)


def kernel_r2(heads, place, own, p1, p2, p3, zr, zslots, yslots, g_ref, yr):
    gather_slots(place[0], own, (p1, p2, p3), yr)
    for h in range(heads):
        g = jnp.zeros((DV, DK), f32)
        for grads, slots, me in ((yr, yslots, place[0]), (zr, zslots, place[1])):
            for i in reversed(range(1, RING)):
                moved = nt(g.astype(bf16), slots[i, h, 128:256]) + grads[i, h].astype(f32)
                g = jnp.where(i > me, moved, g)
        g_ref[h] = g.astype(bf16)


def permute(x, distance, outer):
    size = lax.axis_size("seq")
    if outer:
        pairs = [(i, (i + RING * distance) % size) for i in range(size)]
    else:
        pairs = [(i, i // RING * RING + (i + distance) % RING) for i in range(size)]
    return lax.ppermute(x, "seq", pairs)


def three(x, outer):
    return [permute(x, distance, outer) for distance in (1, 2, 3)]


SMEM = pl.BlockSpec(memory_space=pltpu.SMEM)
VMEM = pl.BlockSpec(memory_space=pltpu.VMEM)


def shape(dims, dtype):
    return jax.ShapeDtypeStruct(dims, dtype)


def call(body, name, heads, in_specs, out_specs, out_shape, scratch, grid, flops, *args):
    total = sum(a.size * a.dtype.itemsize for a in args)
    total += sum(o.size * o.dtype.itemsize for o in out_shape)
    return pl.pallas_call(
        functools.partial(body, heads),
        out_shape=out_shape,
        grid=grid,
        in_specs=in_specs,
        out_specs=out_specs,
        scratch_shapes=scratch,
        compiler_params=pltpu.CompilerParams(
            vmem_limit_bytes=40 * 2**20,
            **({"dimension_semantics": ("arbitrary",)} if grid else {}),
        ),
        cost_estimate=pl.CostEstimate(flops=flops, bytes_accessed=total, transcendentals=0),
        name=name,
    )(*args)


def per_device(
    queries, keys, values, decay, beta, wy_inverse, out_gate, norm_gain, out_proj, grad_out, resets
):
    tokens = queries.shape[0]
    heads = beta.shape[0]
    count = tokens // GROUP
    steps = count // STEP
    width = heads * 128
    index = lax.axis_index("seq")
    place = jnp.stack([index // RING, index % RING]).astype(jnp.int32)
    upstream = lax.dot_general(
        lax.all_gather(grad_out, "head", axis=1, tiled=True),
        out_proj,
        (((1,), (1,)), ((), ())),
        preferred_element_type=f32,
    ).astype(bf16)

    def specs(back):
        at = (lambda i: steps - 1 - i) if back else (lambda i: i)
        return dict(
            tok=pl.BlockSpec((STEP * GROUP, width), lambda i: (at(i), 0)),
            beta=pl.BlockSpec((heads, STEP * GROUP), lambda i: (0, at(i))),
            wy=pl.BlockSpec((STEP, GROUP, heads * GROUP), lambda i: (at(i), 0, 0)),
            state=pl.BlockSpec((STEP, heads, 128, 128), lambda i: (at(i), 0, 0, 0)),
            pair=pl.BlockSpec((STEP, heads, 256, 128), lambda i: (at(i), 0, 0, 0)),
            whole=pl.BlockSpec((heads, 128, 128), lambda i: (0, 0, 0)),
            whole2=pl.BlockSpec((heads, 256, 128), lambda i: (0, 0, 0)),
            gain=pl.BlockSpec((1, 128), lambda i: (0, 0)),
        )

    s = specs(False)
    tok_b = shape((tokens, width), bf16)
    tok_f = shape((tokens, width), f32)
    small_b = shape((count, GROUP, heads * GROUP), bf16)
    state_b = shape((count, heads, 128, 128), bf16)
    pair_b = shape((count, heads, 256, 128), bf16)
    one_b = shape((heads, 128, 128), bf16)
    two_b = shape((heads, 256, 128), bf16)
    unit = count * heads * 2 * 64 * 128 * 128

    gamma, wb, kd, kt, y, n, pre, mb = call(
        kernel_a1, "a1", heads,
        [SMEM, s["tok"], s["tok"], s["tok"], s["beta"], s["wy"]],
        [s["tok"], s["wy"], s["tok"], s["tok"], s["tok"], s["state"], s["pair"], s["whole2"]],
        [tok_f, small_b, tok_b, tok_b, tok_b, state_b, pair_b, two_b],
        [pltpu.VMEM((heads, 256, 128), f32)], (steps,), 8 * unit,
        resets, keys, values, decay, beta, wy_inverse,
    )
    zs = three(mb, False)
    qd, ki, a, at = call(
        kernel_a2, "a2", heads,
        [s["tok"], s["tok"], s["tok"]],
        [s["tok"], s["tok"], s["wy"], s["wy"]],
        [tok_b, tok_b, small_b, small_b],
        [], (steps,), 2 * unit, queries, keys, gamma,
    )
    slots_b = shape((RING, heads, 256, 128), bf16)
    group, zslots = call(
        kernel_f1, "f1", heads, [SMEM] + [VMEM] * 4, [VMEM, VMEM], [two_b, slots_b], [], (),
        unit // 4, place, mb, *zs,
    )
    ys = three(group, True)
    state_in, yslots = call(
        kernel_f2, "f2", heads, [SMEM] + [VMEM] * 5, [VMEM, VMEM], [one_b, slots_b], [], (),
        unit // 4, place, group, *ys, zslots,
    )
    e, vp, u, do, du, dt, dgate, r = call(
        kernel_b, "b", heads,
        [s["tok"], s["tok"], s["tok"], s["tok"], s["wy"], s["wy"], s["wy"], s["pair"], s["tok"], s["tok"], s["gain"], s["whole"]],
        [s["state"], s["tok"], s["tok"], s["tok"], s["tok"], s["state"], s["tok"], s["whole"]],
        [state_b, tok_b, tok_b, tok_b, tok_b, state_b, tok_b, one_b],
        [pltpu.VMEM((heads, 128, 128), f32)], (steps,), 12 * unit,
        values, kd, qd, y, wb, a, at, pre, out_gate, upstream, norm_gain.reshape(1, 128), state_in,
    )
    zr = three(r, False)
    dq, dgam, kk = call(
        kernel_c1, "c1", heads,
        [s["tok"]] * 7 + [s["state"]],
        [s["tok"], s["tok"], s["tok"]], [tok_b, tok_f, tok_b],
        [], (steps,), 4 * unit, queries, keys, gamma, qd, ki, u, do, e,
    )
    rslots_b = shape((RING, heads, 128, 128), bf16)
    rgroup, rslots = call(
        kernel_r1, "r1", heads, [SMEM] + [VMEM] * 5, [VMEM, VMEM], [one_b, rslots_b], [], (),
        unit // 4, place, r, *zr, zslots,
    )
    yr = three(rgroup, True)
    grad_in, _ = call(
        kernel_r2, "r2", heads, [SMEM] + [VMEM] * 7, [VMEM, VMEM], [one_b, rslots_b], [], (),
        unit // 4, place, rgroup, *yr, rslots, zslots, yslots,
    )
    t = specs(True)
    dk, dv, dd, db = call(
        kernel_c2, "c2", heads,
        [SMEM, t["tok"], t["tok"], t["beta"], t["wy"], t["tok"], t["state"], t["state"], t["tok"], t["tok"], t["tok"], t["state"], t["tok"], t["tok"], t["whole"]],
        [t["tok"], t["tok"], t["tok"], t["beta"]],
        [tok_b, tok_b, tok_f, shape((heads, tokens), f32)],
        [pltpu.VMEM((heads, 128, 128), f32)], (steps,), 10 * unit,
        resets, keys, gamma, beta, wb, kt, n, e, vp, u, du, dt, dgam, kk, grad_in,
    )
    return dq, dk, dv, dd, db, dgate


def solution(mesh):
    return jax.shard_map(
        per_device,
        mesh=mesh,
        in_specs=(
            P("seq", "head"),
            P("seq", "head"),
            P("seq", "head"),
            P("seq", "head"),
            P("head", "seq"),
            P("seq", None, "head"),
            P("seq", "head"),
            P(),
            P("head", None),
            P("seq", "head"),
            P("seq"),
        ),
        out_specs=(
            P("seq", "head"),
            P("seq", "head"),
            P("seq", "head"),
            P("seq", "head"),
            P("head", "seq"),
            P("seq", "head"),
        ),
        check_vma=False,
    )
```

time: 1400 us -> 227 us (0.16); the launches traced: 1380 us -> 226 us
  matrix products: 545 us -> 5.13 us
  local copies, waits for them, and re-layouts: 373 us -> 28 us
  other arithmetic: 152 us -> 0.07 us
  waiting for transfers between devices: 169 us -> 24.8 us
  Pallas kernels: 0 us -> 138 us
  starting transfers between devices: 112 us -> 14.6 us
    dot_general x608 -> x0, matrix products: 538 us -> none  [the longest x128 198 us: group_step(): predicted = jnp.einsum('hld,hdv->hlv', key_dec, entry, precision=precise)]
    squeeze x240 -> x0, local copies, waits for them, and re-layouts: 195 us -> none  [core(): final, outputs = lax.scan(jax.checkpoint(group_step), state, blocks)]
    ppermute x32 -> x12, waiting for transfers between devices: 169 us -> 24.1 us  [permute(): return lax.ppermute(x, 'seq', pairs)]
    pallas_call x0 -> x9, Pallas kernels: none -> 138 us  [call(): pl.pallas_call(functools.partial(body, heads), out_shape=out_shape, grid=...]
    ppermute x32 -> x12, starting transfers between devices: 112 us -> 14.5 us  [permute(): return lax.ppermute(x, 'seq', pairs)]
    another operation x160 -> x1, other arithmetic: 51.8 us -> 0.07 us  [per_device(): place = jnp.stack([index // RING, index % RING]).astype(jnp.int32)]
    dynamic_slice x80 -> x0, local copies, waits for them, and re-layouts: 47.9 us -> none  [core(): final, outputs = lax.scan(jax.checkpoint(group_step), state, blocks)]
    reduce_sum x69 -> x0, other arithmetic: 40.6 us -> none  [the longest x32 23.9 us: group_step(): carried = jnp.exp(final[:, 0, :])[:, :, None] * entry]
  transfers between devices with their start and end apart: 33 -> 13, of which waited for: 32 -> 6; matrix products, arithmetic and copies ran while one was open for 32% -> 0% of each run, Pallas kernels for 0% -> 18%
where the time goes in v1:
time: 227 us; the launch traced here: 226 us
  Pallas kernels  138 us (61%)
  local copies, waits for them, and re-layouts  28 us (12%)
  waiting for transfers between devices  24.8 us (11%)
  between operations  15.1 us (7%)
  starting transfers between devices  14.6 us (6%)
  matrix products  5.13 us (2%)
    pallas_call x9, Pallas kernels, call(): pl.pallas_call(functools.partial(body, heads), out_shape=out_shape, grid=...  138 us
    unnamed x98, local copies, waits for them, and re-layouts  28 us
    ppermute x12, waiting for transfers between devices, permute(): return lax.ppermute(x, 'seq', pairs)  24.1 us
    ppermute x12, starting transfers between devices, permute(): return lax.ppermute(x, 'seq', pairs)  14.5 us
    dot_general x1, matrix products, per_device(): lax.dot_general(lax.all_gather(grad_out, 'head', axis=1, tiled=True), out...  5.13 us
  transfers between devices with their start and end apart: 13, of which 6 were waited for; matrix products, arithmetic and copies ran while one was open for 0% of the time, Pallas kernels for 18%

profile of v1, /device:TPU:0, one launch (start us, length us, event | category | flops | bytes accessed | tf_op | source)
XLA Modules:
  0.0 225.6 jit_solution(15567648434380805231)
XLA Ops:
  8.6 1.2 copy-done.4
  9.8 1.2 copy-done.10
  11.0 1.6 copy-done.19
  12.6 1.2 copy-done.39
  14.6 20.3 %a1.1 = (f32[1024,512]{1,0:T(8,128)S(1)}, bf16[16,64,256]{2,1,0:T(8,128)(2,1)S(1)}, bf16[1024,512]{1,0:T(8,128)(2,1)S(1)}, bf16[1024,512]{1,0:T(8,128)(2,1)S(1)}...) custom-call(s32[1]{0:T(128)S(6)} %copy.17.resets, ...), custom_call_target="tpu_custom_call" | custom-call | flops 1073741824 | bytes 17580036 | tf_op jit(solution)/shard_map/a1/pallas_call | solution.py:316
  34.8 1.3 copy-done.1
  36.2 1.3 copy-done.14
  41.2 4.1 %collective-permute-start.2 = (bf16[4,256,128]{2,1,0:T(8,128)(2,1)}, bf16[4,256,128]{2,1,0:T(8,128)(2,1)}, u32[]{:S(2)}, u32[]{:S(2)}) collective-permute-start(bf16[4,256,128]{2,1,0:T(8,128)(2,1)} %get-tuple-element.49.own), channel_id=1, source_target_pairs={{0,24},{8,0},{16,8},{24,16},{32,56},{40,32},{48,40},{56,48},{64,88... | collective-permute-start | bytes 786440 | tf_op jit(solution)/shard_map/ppermute | solution.py:298
  45.4 1.3 collective-permute-start
  46.7 10.2 %collective-permute-done.2.p3 = bf16[4,256,128]{2,1,0:T(8,128)(2,1)} collective-permute-done((bf16[4,256,128]{2,1,0:T(8,128)(2,1)}, bf16[4,256,128]{2,1,0:T(8,128)(2,1)}, u32[]{:S(2)}, u32[]{:S(2)}) %collective-permute-start.2) | collective-permute-done | bytes 262176 | tf_op jit(solution)/shard_map/ppermute | solution.py:298
  56.9 3.4 %collective-permute-done.p1 = bf16[4,256,128]{2,1,0:T(8,128)(2,1)} collective-permute-done((bf16[4,256,128]{2,1,0:T(8,128)(2,1)}, bf16[4,256,128]{2,1,0:T(8,128)(2,1)}, u32[]{:S(2)}, u32[]{:S(2)}) %collective-permute-start) | collective-permute-done | bytes 262176 | tf_op jit(solution)/shard_map/ppermute | solution.py:298
  60.3 2.1 f1.1
  62.4 3.1 %collective-permute-start.5 = (bf16[4,256,128]{2,1,0:T(8,128)(2,1)S(1)}, bf16[4,256,128]{2,1,0:T(8,128)(2,1)S(1)}, u32[]{:S(2)}, u32[]{:S(2)}) collective-permute-start(bf16[4,256,128]{2,1,0:T(8,128)(2,1)S(1)} %get-tuple-element.50.own), channel_id=1, source_target_pairs={{0,96},{8,104},{16,112},{24,120},{32,0},{40,8},{48,16},{56,24},{64... | collective-permute-start | bytes 786440 | tf_op jit(solution)/shard_map/ppermute | solution.py:298
  67.1 1.6 copy-done.2
  68.7 1.2 copy-done.12
  69.9 3.6 %a2.1 = (bf16[1024,512]{1,0:T(8,128)(2,1)S(1)}, bf16[1024,512]{1,0:T(8,128)(2,1)S(1)}, bf16[16,64,256]{2,1,0:T(8,128)(2,1)S(1)}, bf16[16,64,256]{2,1,0:T(8,128)(2,1)S(1)}) custom-call(bf16[1024,512]{1,0:T(8,128)(2,1)S(1)} %copy-done.12, bf16[1024,512]{1,0:T(8,128)(2,1)S(1)} %copy-done.5, f32[1024,512]{1,0:T(8,128)S(1)} %copy-done.2), custom_call_target="tpu_custom_call" | custom-call | flops 268435456 | bytes 7340032 | tf_op jit(solution)/shard_map/a2/pallas_call | solution.py:316
  77.1 3.2 %collective-permute-done.3.p1 = bf16[4,256,128]{2,1,0:T(8,128)(2,1)S(1)} collective-permute-done((bf16[4,256,128]{2,1,0:T(8,128)(2,1)S(1)}, bf16[4,256,128]{2,1,0:T(8,128)(2,1)S(1)}, u32[]{:S(2)}, u32[]{:S(2)}) %collective-permute-start.3) | collective-permute-done | bytes 262176 | tf_op jit(solution)/shard_map/ppermute | solution.py:298
  80.2 2.8 %f2.1 = (bf16[4,128,128]{2,1,0:T(8,128)(2,1)S(1)}, bf16[4,4,256,128]{3,2,1,0:T(8,128)(2,1)S(1)}) custom-call(s32[2]{0:T(128)S(1)} %pad_add_fusion.place, bf16[4,256,128]{2,1,0:T(8,128)(2,1)S(1)} %get-tuple-element.50.own, bf16[4,256,128]{2,1,0:T(8,128)(2,1)S(1)} %collective-permute-done.3.p1, bf16[4,256,128]{2,1,0:T(8,128)(2,1)S(1)} %collective-permute-done.4.p2, ...), custom_call_target="tpu_custom_call" | custom-call | flops 33554432 | bytes 3276808 | tf_op jit(solution)/shard_map/f2/pallas_call | solution.py:316
  84.1 5.1 %convolution_convert_fusion.up_ref = bf16[1024,512]{1,0:T(8,128)(2,1)S(1)} fusion(bf16[1024,2304]{0,1:T(8,128)(2,1)} %all-gather.2.cloned.1.call-done, bf16[512,2304]{1,0:T(8,128)(2,1)S(1)} %copy-done), kind=kOutput, calls=%fused_computation | convolution fusion | flops 2416443392 | bytes 8126464 | tf_op jit(solution)/shard_map/dot_general | solution.py:342
  89.4 61.0 %b.1 = (bf16[16,4,128,128]{3,2,1,0:T(8,128)(2,1)S(1)}, bf16[1024,512]{1,0:T(8,128)(2,1)S(1)}, bf16[1024,512]{1,0:T(8,128)(2,1)S(1)}, bf16[1024,512]{1,0:T(8,128)...) custom-call(bf16[1024,512]{1,0:T(8,128)(2,1)S(1)} %copy-done.11, ...), custom_call_target="tpu_custom_call" | custom-call | flops 1610612736 | bytes 21758464 | tf_op jit(solution)/shard_map/b/pallas_call | solution.py:316
  153.3 1.4 collective-permute-start.6
  154.7 4.0 %collective-permute-done.8.p3 = bf16[4,128,128]{2,1,0:T(8,128)(2,1)S(1)} collective-permute-done((bf16[4,128,128]{2,1,0:T(8,128)(2,1)S(1)}, bf16[4,128,128]{2,1,0:T(8,128)(2,1)S(1)}, u32[]{:S(2)}, u32[]{:S(2)}) %collective-permute-start.8) | collective-permute-done | bytes 131104 | tf_op jit(solution)/shard_map/ppermute | solution.py:298
  158.7 1.3 collective-permute-done.7.p2
  160.0 2.1 collective-permute-done.6.p1
  162.1 1.4 r1.1
  164.3 1.3 collective-permute-start.9
  165.6 1.2 copy-done.34
  166.8 12.0 %c1.1 = (bf16[1024,512]{1,0:T(8,128)(2,1)}, f32[1024,512]{1,0:T(8,128)S(1)}, bf16[1024,512]{1,0:T(8,128)(2,1)S(1)}) custom-call(bf16[1024,512]{1,0:T(8,128)(2,1)S(1)} %copy-done.13, bf16[1024,512]{1,0:T(8,128)(2,1)S(1)} %copy-done.5, f32[1024,512]{1,0:T(8,128)S(1)} %copy-done.3, bf16[1024,512]{1,0:T(8,128)(2,1)S(1)} %copy-done.9, ...), custom_call_target="tpu_custom_call" | custom-call | flops 536870912 | bytes 14680064 | tf_op jit(solution)/shard_map/c1/pallas_call | solution.py:316
  179.9 1.6 copy-done.45
  181.4 3.1 %r2.1 = (bf16[4,128,128]{2,1,0:T(8,128)(2,1)S(1)}, bf16[4,4,128,128]{3,2,1,0:T(8,128)(2,1)}) custom-call(s32[2]{0:T(128)S(1)} %pad_add_fusion.place, bf16[4,128,128]{2,1,0:T(8,128)(2,1)S(1)} %get-tuple-element.65.own, bf16[4,128,128]{2,1,0:T(8,128)(2,1)S(1)} %collective-permute-done.9.p1, bf16[4,128,128]{2,1,0:T(8,128)(2,1)S(1)} %collective-permute-done.10.p2, ...), custom_call_target="tpu_custom_call" | custom-call | flops 33554432 | bytes 3801096 | tf_op jit(solution)/shard_map/r2/pallas_call | solution.py:316
  185.8 1.2 copy-done.36
  187.1 31.7 %c2.1 = (bf16[1024,512]{1,0:T(8,128)(2,1)}, bf16[1024,512]{1,0:T(8,128)(2,1)}, f32[1024,512]{1,0:T(8,128)}, f32[4,1024]{1,0:T(4,128)}) custom-call(s32[1]{0:T(128)S(6)} %copy.17.resets, bf16[1024,512]{1,0:T(8,128)(2,1)S(1)} %copy-done.5, f32[1024,512]{1,0:T(8,128)S(1)} %copy-done.3, f32[4,1024]{1,0:T(4,128)S(1)} %copy-done.47, ...), custom_call_target="tpu_custom_call" | custom-call | flops 1342177280 | bytes 21659652 | tf_op jit(solution)/shard_map/c2/pallas_call | solution.py:316
  (104 shorter events, 17.5 us)
Async XLA Ops:
  7.2 76.8 %copy-start = (bf16[512,2304]{1,0:T(8,128)(2,1)S(1)}, bf16[512,2304]{1,0:T(8,128)(2,1)}, u32[]{:S(2)}) copy-start(bf16[512,2304]{1,0:T(8,128)(2,1)} %param.19) | copy-start | bytes 7077892
  7.2 76.8 %all-gather.2.cloned.1.call-start = ((), (), s32[]{:S(2)}) async-start(), calls=%async_computation | async-start | bytes 5308416 | tf_op jit(solution)/shard_map/all_gather | solution.py:343
  14.5 52.5 %copy-start.5 = (bf16[1024,512]{1,0:T(8,128)(2,1)S(1)}, bf16[1024,512]{1,0:T(8,128)(2,1)}, u32[]{:S(2)}) copy-start(bf16[1024,512]{1,0:T(8,128)(2,1)} %k_ref.7) | copy-start | bytes 3145732
  41.2 15.6 %collective-permute-start.2 = (bf16[4,256,128]{2,1,0:T(8,128)(2,1)}, bf16[4,256,128]{2,1,0:T(8,128)(2,1)}, u32[]{:S(2)}, u32[]{:S(2)}) collective-permute-start(bf16[4,256,128]{2,1,0:T(8,128)(2,1)} %get-tuple-element.49.own), channel_id=1, source_target_pairs={{0,24},{8,0},{16,8},{24,16},{32,56},{40,32},{48,40},{56,48},{64,88... | collective-permute-start | bytes 786440 | tf_op jit(solution)/shard_map/ppermute | solution.py:298
  45.4 11.5 %collective-permute-start.1 = (bf16[4,256,128]{2,1,0:T(8,128)(2,1)}, bf16[4,256,128]{2,1,0:T(8,128)(2,1)}, u32[]{:S(2)}, u32[]{:S(2)}) collective-permute-start(bf16[4,256,128]{2,1,0:T(8,128)(2,1)} %get-tuple-element.49.own), channel_id=1, source_target_pairs={{0,16},{8,24},{16,0},{24,8},{32,48},{40,56},{48,32},{56,40},{64,80... | collective-permute-start | bytes 786440 | tf_op jit(solution)/shard_map/ppermute | solution.py:298
  45.4 14.9 %collective-permute-start = (bf16[4,256,128]{2,1,0:T(8,128)(2,1)}, bf16[4,256,128]{2,1,0:T(8,128)(2,1)}, u32[]{:S(2)}, u32[]{:S(2)}) collective-permute-start(bf16[4,256,128]{2,1,0:T(8,128)(2,1)} %get-tuple-element.49.own), channel_id=1, source_target_pairs={{0,8},{8,16},{16,24},{24,0},{32,40},{40,48},{48,56},{56,32},{64,72... | collective-permute-start | bytes 786440 | tf_op jit(solution)/shard_map/ppermute | solution.py:298
  62.4 17.8 %copy-start.6 = (bf16[4,4,256,128]{3,2,1,0:T(8,128)(2,1)}, bf16[4,4,256,128]{3,2,1,0:T(8,128)(2,1)S(1)}, u32[]{:S(2)}) copy-start(bf16[4,4,256,128]{3,2,1,0:T(8,128)(2,1)S(1)} %get-tuple-element.51.zslots) | copy-start | bytes 3145732
  62.4 14.7 %collective-permute-start.5 = (bf16[4,256,128]{2,1,0:T(8,128)(2,1)S(1)}, bf16[4,256,128]{2,1,0:T(8,128)(2,1)S(1)}, u32[]{:S(2)}, u32[]{:S(2)}) collective-permute-start(bf16[4,256,128]{2,1,0:T(8,128)(2,1)S(1)} %get-tuple-element.50.own), channel_id=1, source_target_pairs={{0,96},{8,104},{16,112},{24,120},{32,0},{40,8},{48,16},{56,24},{64... | collective-permute-start | bytes 786440 | tf_op jit(solution)/shard_map/ppermute | solution.py:298
  65.5 11.6 %collective-permute-start.4 = (bf16[4,256,128]{2,1,0:T(8,128)(2,1)S(1)}, bf16[4,256,128]{2,1,0:T(8,128)(2,1)S(1)}, u32[]{:S(2)}, u32[]{:S(2)}) collective-permute-start(bf16[4,256,128]{2,1,0:T(8,128)(2,1)S(1)} %get-tuple-element.50.own), channel_id=1, source_target_pairs={{0,64},{8,72},{16,80},{24,88},{32,96},{40,104},{48,112},{56,120},{... | collective-permute-start | bytes 786440 | tf_op jit(solution)/shard_map/ppermute | solution.py:298
  66.1 14.1 %collective-permute-start.3 = (bf16[4,256,128]{2,1,0:T(8,128)(2,1)S(1)}, bf16[4,256,128]{2,1,0:T(8,128)(2,1)S(1)}, u32[]{:S(2)}, u32[]{:S(2)}) collective-permute-start(bf16[4,256,128]{2,1,0:T(8,128)(2,1)S(1)} %get-tuple-element.50.own), channel_id=1, source_target_pairs={{0,32},{8,40},{16,48},{24,56},{32,64},{40,72},{48,80},{56,88},{64,... | collective-permute-start | bytes 786440 | tf_op jit(solution)/shard_map/ppermute | solution.py:298
  84.0 5.2 %copy-start.48 = (f32[128]{0:T(128)S(1)}, f32[128]{0:T(128)}, u32[]{:S(2)}) copy-start(f32[128]{0:T(128)} %param.18) | copy-start | bytes 1540
  84.0 5.2 %copy-start.9 = (bf16[1024,512]{1,0:T(8,128)(2,1)S(1)}, bf16[1024,512]{1,0:T(8,128)(2,1)}, u32[]{:S(2)}) copy-start(bf16[1024,512]{1,0:T(8,128)(2,1)} %copy-done.8) | copy-start | bytes 3145732
  84.0 5.2 %copy-start.11 = (bf16[1024,512]{1,0:T(8,128)(2,1)S(1)}, bf16[1024,512]{1,0:T(8,128)(2,1)}, u32[]{:S(2)}) copy-start(bf16[1024,512]{1,0:T(8,128)(2,1)} %v_ref.3) | copy-start | bytes 3145732
  84.0 5.2 %copy-start.18 = (bf16[16,64,256]{2,1,0:T(8,128)(2,1)S(1)}, bf16[16,64,256]{2,1,0:T(8,128)(2,1)}, u32[]{:S(2)}) copy-start(bf16[16,64,256]{2,1,0:T(8,128)(2,1)} %copy-done.17) | copy-start | bytes 1572868
  84.0 5.2 %copy-start.20 = (bf16[1024,512]{1,0:T(8,128)(2,1)S(1)}, bf16[1024,512]{1,0:T(8,128)(2,1)}, u32[]{:S(2)}) copy-start(bf16[1024,512]{1,0:T(8,128)(2,1)} %gate_ref.1) | copy-start | bytes 3145732
  84.1 5.2 %copy-start.24 = (bf16[1024,512]{1,0:T(8,128)(2,1)S(1)}, bf16[1024,512]{1,0:T(8,128)(2,1)}, u32[]{:S(2)}) copy-start(bf16[1024,512]{1,0:T(8,128)(2,1)} %copy-done.23) | copy-start | bytes 3145732
  84.1 5.2 %copy-start.26 = (bf16[1024,512]{1,0:T(8,128)(2,1)S(1)}, bf16[1024,512]{1,0:T(8,128)(2,1)}, u32[]{:S(2)}) copy-start(bf16[1024,512]{1,0:T(8,128)(2,1)} %copy-done.25) | copy-start | bytes 3145732
  89.3 72.7 %copy-start.7 = (bf16[4,4,256,128]{3,2,1,0:T(8,128)(2,1)S(1)}, bf16[4,4,256,128]{3,2,1,0:T(8,128)(2,1)}, u32[]{:S(2)}) copy-start(bf16[4,4,256,128]{3,2,1,0:T(8,128)(2,1)} %copy-done.6) | copy-start | bytes 3145732
  89.3 76.3 %copy-start.3 = (f32[1024,512]{1,0:T(8,128)S(1)}, f32[1024,512]{1,0:T(8,128)}, u32[]{:S(2)}) copy-start(f32[1024,512]{1,0:T(8,128)} %copy-done.1) | copy-start | bytes 6291460
  89.4 76.2 %copy-start.13 = (bf16[1024,512]{1,0:T(8,128)(2,1)S(1)}, bf16[1024,512]{1,0:T(8,128)(2,1)}, u32[]{:S(2)}) copy-start(bf16[1024,512]{1,0:T(8,128)(2,1)} %q_ref.3) | copy-start | bytes 3145732
  89.4 76.2 %copy-start.32 = (bf16[1024,512]{1,0:T(8,128)(2,1)S(1)}, bf16[1024,512]{1,0:T(8,128)(2,1)}, u32[]{:S(2)}) copy-start(bf16[1024,512]{1,0:T(8,128)(2,1)} %copy-done.31) | copy-start | bytes 3145732
  152.3 13.3 %copy-start.27 = (bf16[1024,512]{1,0:T(8,128)(2,1)}, bf16[1024,512]{1,0:T(8,128)(2,1)S(1)}, u32[]{:S(2)}) copy-start(bf16[1024,512]{1,0:T(8,128)(2,1)S(1)} %get-tuple-element.59.vp_ref) | copy-start | bytes 3145732
  152.3 6.4 %collective-permute-start.8 = (bf16[4,128,128]{2,1,0:T(8,128)(2,1)S(1)}, bf16[4,128,128]{2,1,0:T(8,128)(2,1)S(1)}, u32[]{:S(2)}, u32[]{:S(2)}) collective-permute-start(bf16[4,128,128]{2,1,0:T(8,128)(2,1)S(1)} %get-tuple-element.64.own), channel_id=1, source_target_pairs={{0,24},{8,0},{16,8},{24,16},{32,56},{40,32},{48,40},{56,48},{64,88... | collective-permute-start | bytes 393224 | tf_op jit(solution)/shard_map/ppermute | solution.py:298
  152.3 7.6 %collective-permute-start.7 = (bf16[4,128,128]{2,1,0:T(8,128)(2,1)S(1)}, bf16[4,128,128]{2,1,0:T(8,128)(2,1)S(1)}, u32[]{:S(2)}, u32[]{:S(2)}) collective-permute-start(bf16[4,128,128]{2,1,0:T(8,128)(2,1)S(1)} %get-tuple-element.64.own), channel_id=1, source_target_pairs={{0,16},{8,24},{16,0},{24,8},{32,48},{40,56},{48,32},{56,40},{64,80... | collective-permute-start | bytes 393224 | tf_op jit(solution)/shard_map/ppermute | solution.py:298
  153.3 8.8 %collective-permute-start.6 = (bf16[4,128,128]{2,1,0:T(8,128)(2,1)S(1)}, bf16[4,128,128]{2,1,0:T(8,128)(2,1)S(1)}, u32[]{:S(2)}, u32[]{:S(2)}) collective-permute-start(bf16[4,128,128]{2,1,0:T(8,128)(2,1)S(1)} %get-tuple-element.64.own), channel_id=1, source_target_pairs={{0,8},{8,16},{16,24},{24,0},{32,40},{40,48},{48,56},{56,32},{64,72... | collective-permute-start | bytes 393224 | tf_op jit(solution)/shard_map/ppermute | solution.py:298
  163.5 15.4 %copy-start.44 = (bf16[4,4,128,128]{3,2,1,0:T(8,128)(2,1)}, bf16[4,4,128,128]{3,2,1,0:T(8,128)(2,1)S(1)}, u32[]{:S(2)}) copy-start(bf16[4,4,128,128]{3,2,1,0:T(8,128)(2,1)S(1)} %get-tuple-element.66.zr) | copy-start | bytes 1572868
  163.5 16.3 %collective-permute-start.11 = (bf16[4,128,128]{2,1,0:T(8,128)(2,1)S(1)}, bf16[4,128,128]{2,1,0:T(8,128)(2,1)S(1)}, u32[]{:S(2)}, u32[]{:S(2)}) collective-permute-start(bf16[4,128,128]{2,1,0:T(8,128)(2,1)S(1)} %get-tuple-element.65.own), channel_id=1, source_target_pairs={{0,96},{8,104},{16,112},{24,120},{32,0},{40,8},{48,16},{56,24},{64... | collective-permute-start | bytes 393224 | tf_op jit(solution)/shard_map/ppermute | solution.py:298
  163.6 16.3 %collective-permute-start.10 = (bf16[4,128,128]{2,1,0:T(8,128)(2,1)S(1)}, bf16[4,128,128]{2,1,0:T(8,128)(2,1)S(1)}, u32[]{:S(2)}, u32[]{:S(2)}) collective-permute-start(bf16[4,128,128]{2,1,0:T(8,128)(2,1)S(1)} %get-tuple-element.65.own), channel_id=1, source_target_pairs={{0,64},{8,72},{16,80},{24,88},{32,96},{40,104},{48,112},{56,120},{... | collective-permute-start | bytes 393224 | tf_op jit(solution)/shard_map/ppermute | solution.py:298
  164.3 15.6 %collective-permute-start.9 = (bf16[4,128,128]{2,1,0:T(8,128)(2,1)S(1)}, bf16[4,128,128]{2,1,0:T(8,128)(2,1)S(1)}, u32[]{:S(2)}, u32[]{:S(2)}) collective-permute-start(bf16[4,128,128]{2,1,0:T(8,128)(2,1)S(1)} %get-tuple-element.65.own), channel_id=1, source_target_pairs={{0,32},{8,40},{16,48},{24,56},{32,64},{40,72},{48,80},{56,88},{64,... | collective-permute-start | bytes 393224 | tf_op jit(solution)/shard_map/ppermute | solution.py:298
  166.8 13.0 %copy-start.38 = (bf16[4,4,256,128]{3,2,1,0:T(8,128)(2,1)S(1)}, bf16[4,4,256,128]{3,2,1,0:T(8,128)(2,1)}, u32[]{:S(2)}) copy-start(bf16[4,4,256,128]{3,2,1,0:T(8,128)(2,1)} %copy-done.37) | copy-start | bytes 3145732
  166.8 17.7 %copy-start.28 = (bf16[1024,512]{1,0:T(8,128)(2,1)S(1)}, bf16[1024,512]{1,0:T(8,128)(2,1)}, u32[]{:S(2)}) copy-start(bf16[1024,512]{1,0:T(8,128)(2,1)} %copy-done.27) | copy-start | bytes 3145732
  166.8 17.7 %copy-start.47 = (f32[4,1024]{1,0:T(4,128)S(1)}, f32[4,1024]{1,0:T(4,128)}, u32[]{:S(2)}) copy-start(f32[4,1024]{1,0:T(4,128)} %b_ref.3) | copy-start | bytes 49156
  (30 other events, 52.7 us)
Sparse Core Ops, SparseCore 0:
  9.7 36.7 all-gather.1

commit v2 on v1

v2 whole, which is shorter than its diff:
```python
import functools

import jax
import jax.numpy as jnp
from jax import lax
from jax.experimental import pallas as pl
from jax.experimental.pallas import tpu as pltpu
from jax.sharding import PartitionSpec as P

DK = 128
DV = 128
GROUP = 64
EPS = 1e-6
SCALE = DK**-0.5
STEP = 4
UNITS = dict(a1=16, a2=16, b=16, c0=16, c1=16, c2=16)
RING = 4

f32 = jnp.float32
bf16 = jnp.bfloat16


def nn(a, b):
    return lax.dot_general(a, b, (((1,), (0,)), ((), ())), preferred_element_type=f32)


def nt(a, b):
    return lax.dot_general(a, b, (((1,), (1,)), ((), ())), preferred_element_type=f32)


def tn(a, b):
    return lax.dot_general(a, b, (((0,), (0,)), ((), ())), preferred_element_type=f32)


def triangle(upper, dtype):
    row = lax.broadcasted_iota(jnp.int32, (GROUP, GROUP), 0)
    col = lax.broadcasted_iota(jnp.int32, (GROUP, GROUP), 1)
    return (row <= col if upper else row >= col).astype(dtype)


def sum_rows(weights, x):
    high = x.astype(bf16)
    low = (x - high.astype(f32)).astype(bf16)
    return nn(weights, jnp.concatenate([high, low], axis=0))


def twice(upper):
    t = triangle(upper, f32)
    return jnp.concatenate([t, t], axis=1).astype(bf16)


def inverse_norm(x):
    return lax.rsqrt(jnp.sum(x * x, axis=-1, keepdims=True) + EPS)


def cols(h):
    return slice(128 * h, 128 * h + 128)


def half(h):
    return slice(64 * h, 64 * h + 64)


def units(heads, size):
    pairs = [(c, h) for c in range(STEP) for h in range(heads)]
    return [pairs[i : i + size] for i in range(0, len(pairs), size)]


def each(f, *lists):
    return [f(*xs) for xs in zip(*lists)]


def kernel_a1(
    heads, resets, k_ref, v_ref, d_ref, b_ref, w_ref,
    g_ref, wb_ref, kd_ref, kt_ref, y_ref, n_ref, pre_ref, mb_ref, state,
):
    step = pl.program_id(0)

    @pl.when(step == 0)
    def _():
        row = lax.broadcasted_iota(jnp.int32, (256, 128), 0)
        col = lax.broadcasted_iota(jnp.int32, (256, 128), 1)
        for h in range(heads):
            state[h] = (row == col + 128).astype(f32)

    weights = twice(False)
    gammas = [sum_rows(weights, d_ref[half(c), :]) for c in range(STEP)]
    for c in range(STEP):
        g_ref[half(c), :] = gammas[c]
    rs = [state[h] for h in range(heads)]
    for group in units(heads, UNITS["a1"]):
        gs = [gammas[c][:, cols(h)] for c, h in group]
        ks = [k_ref[half(c), cols(h)].astype(f32) for c, h in group]
        kus = each(lambda k: k * inverse_norm(k), ks)
        kds = each(lambda ku, g: (ku * jnp.exp(g)).astype(bf16), kus, gs)
        kts = each(lambda ku, g: (ku * jnp.exp(g[63:64, :] - g)).astype(bf16), kus, gs)
        wbs = [(w_ref[c, :, half(h)] * b_ref[h : h + 1, half(c)]).astype(bf16) for c, h in group]
        xys = [
            nn(wb, jnp.concatenate([v_ref[half(c), cols(h)], kd], axis=1)).astype(bf16)
            for wb, kd, (c, h) in zip(wbs, kds, group)
        ]
        bns = each(tn, xys, kts)
        ns = each(lambda bn: bn[128:].astype(bf16), bns)
        for (c, h), wb, kd, kt, xy, n in zip(group, wbs, kds, kts, xys, ns):
            wb_ref[c, :, half(h)] = wb
            kd_ref[half(c), cols(h)] = kd
            kt_ref[half(c), cols(h)] = kt
            y_ref[half(c), cols(h)] = xy[:, 128:]
            n_ref[c, h] = n
        for (c, h), bn, n, g in zip(group, bns, ns, gs):
            keep = (step * STEP + c != resets[0]).astype(f32)
            r = rs[h] * keep
            rb = r.astype(bf16)
            pre_ref[c, h] = rb
            r = jnp.exp(g[63:64, :]) * r - nn(rb, n)
            rs[h] = jnp.concatenate([r[0:128] + bn[0:128], r[128:256]], axis=0)
    for h in range(heads):
        state[h] = rs[h]

    @pl.when(step == pl.num_programs(0) - 1)
    def _():
        for h in range(heads):
            mb_ref[h] = rs[h].astype(bf16)


def kernel_a2(heads, q_ref, k_ref, g_ref, qd_ref, ki_ref, a_ref, at_ref):
    lower = triangle(False, f32)
    upper = triangle(True, f32)
    for group in units(heads, UNITS["a2"]):
        gs = [g_ref[half(c), cols(h)] for c, h in group]
        qs = [q_ref[half(c), cols(h)].astype(f32) for c, h in group]
        ks = [k_ref[half(c), cols(h)].astype(f32) for c, h in group]
        qds = each(lambda q, g: (q * (inverse_norm(q) * SCALE) * jnp.exp(g)).astype(bf16), qs, gs)
        kis = each(lambda k, g: (k * inverse_norm(k) * jnp.exp(-g)).astype(bf16), ks, gs)
        als = each(lambda qd, ki: (nt(qd, ki) * lower).astype(bf16), qds, kis)
        ats = each(lambda qd, ki: (nt(ki, qd) * upper).astype(bf16), qds, kis)
        for (c, h), qd, ki, a, at in zip(group, qds, kis, als, ats):
            qd_ref[half(c), cols(h)] = qd
            ki_ref[half(c), cols(h)] = ki
            a_ref[c, :, half(h)] = a
            at_ref[c, :, half(h)] = at


def kernel_b(
    heads, v_ref, kd_ref, qd_ref, y_ref, wb_ref, a_ref, at_ref, pre_ref, gate_ref, up_ref, gain_ref, s_ref,
    e_ref, vp_ref, u_ref, do_ref, du_ref, dt_ref, dg_ref, r_ref, total,
):
    step = pl.program_id(0)

    @pl.when(step == 0)
    def _():
        total[...] = jnp.zeros_like(total)

    gain = gain_ref[...]
    sums = [total[h] for h in range(heads)]
    for group in units(heads, UNITS["b"]):
        es = [
            (pre_ref[c, h, 0:128].astype(f32) + nn(s_ref[h], pre_ref[c, h, 128:256])).astype(bf16)
            for c, h in group
        ]
        boths = [
            nt(jnp.concatenate([kd_ref[half(c), cols(h)], qd_ref[half(c), cols(h)]], axis=0), e)
            for e, (c, h) in zip(es, group)
        ]
        vps = [
            (v_ref[half(c), cols(h)].astype(f32) - both[0:64]).astype(bf16)
            for both, (c, h) in zip(boths, group)
        ]
        us = [nn(wb_ref[c, :, half(h)], vp).astype(bf16) for vp, (c, h) in zip(vps, group)]
        os = [both[64:128] + nn(a_ref[c, :, half(h)], u) for both, u, (c, h) in zip(boths, us, group)]
        rmss = each(lambda o: lax.rsqrt(jnp.mean(o * o, axis=-1, keepdims=True) + EPS), os)
        sigs = [jax.nn.sigmoid(gate_ref[half(c), cols(h)].astype(f32)) for c, h in group]
        ws = [up_ref[half(c), cols(h)].astype(f32) * gain * sig for sig, (c, h) in zip(sigs, group)]
        ons = each(lambda o, rms: o * rms, os, rmss)
        wons = each(lambda w, on: w * on, ws, ons)
        dgs = each(lambda won, sig: (won * (1.0 - sig)).astype(bf16), wons, sigs)
        dos = each(
            lambda rms, w, on, won: (rms * (w - on * jnp.mean(won, axis=-1, keepdims=True))).astype(bf16),
            rmss, ws, ons, wons,
        )
        dus = [nn(at_ref[c, :, half(h)], do).astype(bf16) for do, (c, h) in zip(dos, group)]
        dts = [
            tn(
                jnp.concatenate([do, du], axis=0),
                jnp.concatenate([qd_ref[half(c), cols(h)], -y_ref[half(c), cols(h)]], axis=0),
            ).astype(bf16)
            for do, du, (c, h) in zip(dos, dus, group)
        ]
        for (c, h), dt in zip(group, dts):
            sums[h] = sums[h] + nt(dt, pre_ref[c, h, 128:256])
        for (c, h), e, vp, u, do, du, dt, dg in zip(group, es, vps, us, dos, dus, dts, dgs):
            e_ref[c, h] = e
            vp_ref[half(c), cols(h)] = vp
            u_ref[half(c), cols(h)] = u
            do_ref[half(c), cols(h)] = do
            du_ref[half(c), cols(h)] = du
            dt_ref[c, h] = dt
            dg_ref[half(c), cols(h)] = dg
    for h in range(heads):
        total[h] = sums[h]

    @pl.when(step == pl.num_programs(0) - 1)
    def _():
        for h in range(heads):
            r_ref[h] = sums[h].astype(bf16)


def kernel_c1(heads, q_ref, g_ref, ki_ref, u_ref, do_ref, e_ref, dq_ref, pq_ref):
    lower = triangle(False, f32)
    for group in units(heads, UNITS["c1"]):
        us = [u_ref[half(c), cols(h)] for c, h in group]
        dos = [do_ref[half(c), cols(h)] for c, h in group]
        das = each(lambda do, u: (nt(do, u) * lower).astype(bf16), dos, us)
        dqus = [
            (nn(do, e_ref[c, h]) + nn(da, ki_ref[half(c), cols(h)])) * jnp.exp(g_ref[half(c), cols(h)])
            for do, da, (c, h) in zip(dos, das, group)
        ]
        qs = [q_ref[half(c), cols(h)].astype(f32) for c, h in group]
        rqs = each(lambda q: inverse_norm(q), qs)
        qns = each(lambda q, rq: q * rq, qs, rqs)
        prods = each(lambda qn, dqu: qn * dqu, qns, dqus)
        dqs = each(
            lambda rq, dqu, qn, prod: (
                (rq * SCALE) * (dqu - qn * jnp.sum(prod, axis=-1, keepdims=True))
            ).astype(bf16),
            rqs, dqus, qns, prods,
        )
        for (c, h), dq, prod in zip(group, dqs, prods):
            dq_ref[half(c), cols(h)] = dq
            pq_ref[half(c), cols(h)] = prod * SCALE


def kernel_c0(heads, g_ref, qd_ref, u_ref, do_ref, kk_ref):
    upper = triangle(True, f32)
    for group in units(heads, UNITS["c0"]):
        us = [u_ref[half(c), cols(h)] for c, h in group]
        dos = [do_ref[half(c), cols(h)] for c, h in group]
        dats = each(lambda do, u: (nt(u, do) * upper).astype(bf16), dos, us)
        dkus = [
            nn(dat, qd_ref[half(c), cols(h)]) * jnp.exp(-g_ref[half(c), cols(h)])
            for dat, (c, h) in zip(dats, group)
        ]
        for (c, h), dku in zip(group, dkus):
            kk_ref[half(c), cols(h)] = dku.astype(bf16)


def kernel_c2(
    heads, resets, k_ref, g_ref, b_ref, wb_ref, kt_ref, n_ref, e_ref, vp_ref, u_ref, du_ref, dt_ref,
    pq_ref, kk_ref, gin_ref, dk_ref, dv_ref, dd_ref, db_ref, state,
):
    step = pl.program_id(0)
    place = pl.num_programs(0) - 1 - step

    @pl.when(step == 0)
    def _():
        state[...] = gin_ref[...].astype(f32)

    weights = twice(True)
    ones = jnp.ones((16, 128), bf16)
    grads = {}
    gbs = {}
    now = [state[h] for h in range(heads)]
    for c in reversed(range(STEP)):
        keep = (place * STEP + c != resets[0]).astype(f32)
        for h in range(heads):
            grads[c, h] = now[h]
            gbs[c, h] = now[h].astype(bf16)
        for h in range(heads):
            lam = jnp.exp(g_ref[64 * c + 63 : 64 * c + 64, cols(h)])
            now[h] = keep * (dt_ref[c, h].astype(f32) + lam * now[h] - nt(gbs[c, h], n_ref[c, h]))
    for h in range(heads):
        state[h] = now[h]
    for group in reversed(units(heads, UNITS["c2"])):
        gb = [gbs[p] for p in group]
        dus = [
            (du_ref[half(c), cols(h)].astype(f32) + nt(kt_ref[half(c), cols(h)], x)).astype(bf16)
            for x, (c, h) in zip(gb, group)
        ]
        dvs = [tn(wb_ref[c, :, half(h)], du) for du, (c, h) in zip(dus, group)]
        dvbs = each(lambda x: x.astype(bf16), dvs)
        gs = [g_ref[half(c), cols(h)] for c, h in group]
        ktts = [
            nn(u_ref[half(c), cols(h)], x) * jnp.exp(g[63:64, :] - g) for x, g, (c, h) in zip(gb, gs, group)
        ]
        kdds = [nn(dvb, e_ref[c, h]) * jnp.exp(g) for dvb, g, (c, h) in zip(dvbs, gs, group)]
        ks = [k_ref[half(c), cols(h)].astype(f32) for c, h in group]
        rks = each(inverse_norm, ks)
        kus = each(lambda k, rk: k * rk, ks, rks)
        sums = [kk_ref[half(c), cols(h)].astype(f32) + ktt for ktt, (c, h) in zip(ktts, group)]
        dkus = each(lambda x, kdd: x - kdd, sums, kdds)
        dks = each(
            lambda rk, dku, ku: (rk * (dku - ku * jnp.sum(ku * dku, axis=-1, keepdims=True))).astype(bf16),
            rks, dkus, kus,
        )
        kutts = each(lambda ku, ktt: ku * ktt, kus, ktts)
        dgams = [
            pq_ref[half(c), cols(h)] - ku * (x + kdd) for ku, kdd, x, (c, h) in zip(kus, kdds, sums, group)
        ]
        dlasts = [
            jnp.sum(kutt, axis=0, keepdims=True)
            + jnp.exp(g[63:64, :]) * jnp.sum(grads[c, h] * e_ref[c, h].astype(f32), axis=0, keepdims=True)
            for kutt, g, (c, h) in zip(kutts, gs, group)
        ]
        dds = each(lambda dgam, dlast: sum_rows(weights, dgam) + dlast, dgams, dlasts)
        dbs = [
            nt(ones, (dv * vp_ref[half(c), cols(h)].astype(f32)).astype(bf16))[0:1]
            for dv, (c, h) in zip(dvs, group)
        ]
        for (c, h), dvb, dk, dd, db in zip(group, dvbs, dks, dds, dbs):
            dv_ref[half(c), cols(h)] = dvb
            dk_ref[half(c), cols(h)] = dk
            dd_ref[half(c), cols(h)] = dd
            db_ref[h : h + 1, half(c)] = db / b_ref[h : h + 1, half(c)]


def gather_slots(me, own, others, slots):
    slots[me] = own[...]
    for shift, other in enumerate(others, 1):
        slots[lax.rem(me + RING - shift, RING)] = other[...]


def identity_pair():
    row = lax.broadcasted_iota(jnp.int32, (256, 128), 0)
    col = lax.broadcasted_iota(jnp.int32, (256, 128), 1)
    return (row == col + 128).astype(f32)


def after(pair, r):
    moved = nn(r.astype(bf16), pair[128:256])
    return jnp.concatenate([moved[0:128] + pair[0:128].astype(f32), moved[128:256]], axis=0)


def kernel_f1(heads, place, own, p1, p2, p3, total_ref, before_ref, slots):
    me = place[1]
    gather_slots(me, own, (p1, p2, p3), slots)
    start = identity_pair()
    rs = [slots[0, h].astype(f32) for h in range(heads)]
    befores = [jnp.where(me == 0, start, r) for r in rs]
    for z in range(1, RING):
        befores = [jnp.where(z < me, after(slots[z, h], r), b) for h, (r, b) in enumerate(zip(rs, befores))]
        rs = [after(slots[z, h], r) for h, r in enumerate(rs)]
    for h in range(heads):
        total_ref[h] = rs[h].astype(bf16)
        before_ref[h] = befores[h].astype(bf16)


def kernel_f2(heads, place, own, p1, p2, p3, before, s_ref, slots):
    me = place[0]
    gather_slots(me, own, (p1, p2, p3), slots)
    ss = [jnp.where(me > 0, slots[0, h, 0:128].astype(f32), 0.0) for h in range(heads)]
    for i in range(1, RING - 1):
        moved = [
            nn(s.astype(bf16), slots[i, h, 128:256]) + slots[i, h, 0:128].astype(f32) for h, s in enumerate(ss)
        ]
        ss = [jnp.where(i < me, m, s) for m, s in zip(moved, ss)]
    ss = [nn(s.astype(bf16), before[h, 128:256]) + before[h, 0:128].astype(f32) for h, s in enumerate(ss)]
    for h in range(heads):
        s_ref[h] = ss[h].astype(bf16)


def kernel_m(heads, place, zslots, m_ref):
    me = place[1]
    row = lax.broadcasted_iota(jnp.int32, (128, 128), 0)
    col = lax.broadcasted_iota(jnp.int32, (128, 128), 1)
    ms = [jnp.where(me < RING - 1, zslots[RING - 1, h, 128:256].astype(f32), (row == col).astype(f32)) for h in range(heads)]
    for i in reversed(range(1, RING - 1)):
        moved = [nn(zslots[i, h, 128:256], m.astype(bf16)) for h, m in enumerate(ms)]
        ms = [jnp.where(i > me, x, m) for x, m in zip(moved, ms)]
    for h in range(heads):
        m_ref[h] = ms[h].astype(bf16)


def kernel_r1(heads, place, own, p1, p2, p3, zslots, total_ref, later_ref, slots):
    me = place[1]
    gather_slots(me, own, (p1, p2, p3), slots)
    gs = [slots[RING - 1, h].astype(f32) for h in range(heads)]
    laters = [jnp.where(me < RING - 1, g, 0.0) for g in gs]
    for z in reversed(range(RING - 1)):
        gs = [nt(g.astype(bf16), zslots[z, h, 128:256]) + slots[z, h].astype(f32) for h, g in enumerate(gs)]
        laters = [jnp.where(z > me, g, x) for g, x in zip(gs, laters)]
    for h in range(heads):
        total_ref[h] = gs[h].astype(bf16)
        later_ref[h] = laters[h].astype(bf16)


def kernel_r2(heads, place, own, p1, p2, p3, later, later_m, yslots, g_ref, slots):
    me = place[0]
    gather_slots(me, own, (p1, p2, p3), slots)
    gs = [jnp.where(me < RING - 1, slots[RING - 1, h].astype(f32), 0.0) for h in range(heads)]
    for i in reversed(range(1, RING - 1)):
        moved = [nt(g.astype(bf16), yslots[i, h, 128:256]) + slots[i, h].astype(f32) for h, g in enumerate(gs)]
        gs = [jnp.where(i > me, m, g) for m, g in zip(moved, gs)]
    for h in range(heads):
        g_ref[h] = (nt(gs[h].astype(bf16), later_m[h]) + later[h].astype(f32)).astype(bf16)


def permute(x, distance, outer):
    size = lax.axis_size("seq")
    if outer:
        pairs = [(i, (i + RING * distance) % size) for i in range(size)]
    else:
        pairs = [(i, i // RING * RING + (i + distance) % RING) for i in range(size)]
    return lax.ppermute(x, "seq", pairs)


def three(x, outer):
    return [permute(x, distance, outer) for distance in (1, 2, 3)]


VMEM_LIMIT = 60 * 2**20
SMEM = pl.BlockSpec(memory_space=pltpu.SMEM)
VMEM = pl.BlockSpec(memory_space=pltpu.VMEM)


def shape(dims, dtype):
    return jax.ShapeDtypeStruct(dims, dtype)


def call(body, name, heads, in_specs, out_specs, out_shape, scratch, grid, flops, *args):
    total = sum(a.size * a.dtype.itemsize for a in args)
    total += sum(o.size * o.dtype.itemsize for o in out_shape)
    return pl.pallas_call(
        functools.partial(body, heads),
        out_shape=out_shape,
        grid=grid,
        in_specs=in_specs,
        out_specs=out_specs,
        scratch_shapes=scratch,
        compiler_params=pltpu.CompilerParams(
            vmem_limit_bytes=VMEM_LIMIT,
            **({"dimension_semantics": ("arbitrary",)} if grid else {}),
        ),
        cost_estimate=pl.CostEstimate(flops=flops, bytes_accessed=total, transcendentals=0),
        name=name,
    )(*args)


def per_device(
    queries, keys, values, decay, beta, wy_inverse, out_gate, norm_gain, out_proj, grad_out, resets
):
    tokens = queries.shape[0]
    heads = beta.shape[0]
    count = tokens // GROUP
    steps = count // STEP
    width = heads * 128
    index = lax.axis_index("seq")
    place = jnp.stack([index // RING, index % RING]).astype(jnp.int32)
    gathered = lax.all_gather(grad_out, "head", axis=1, tiled=True)

    def specs(back):
        at = (lambda i: steps - 1 - i) if back else (lambda i: i)
        return dict(
            tok=pl.BlockSpec((STEP * GROUP, width), lambda i: (at(i), 0)),
            beta=pl.BlockSpec((heads, STEP * GROUP), lambda i: (0, at(i))),
            wy=pl.BlockSpec((STEP, GROUP, heads * GROUP), lambda i: (at(i), 0, 0)),
            state=pl.BlockSpec((STEP, heads, 128, 128), lambda i: (at(i), 0, 0, 0)),
            pair=pl.BlockSpec((STEP, heads, 256, 128), lambda i: (at(i), 0, 0, 0)),
            whole=pl.BlockSpec((heads, 128, 128), lambda i: (0, 0, 0)),
            whole2=pl.BlockSpec((heads, 256, 128), lambda i: (0, 0, 0)),
            gain=pl.BlockSpec((1, 128), lambda i: (0, 0)),
        )

    s = specs(False)
    tok_b = shape((tokens, width), bf16)
    tok_f = shape((tokens, width), f32)
    small_b = shape((count, GROUP, heads * GROUP), bf16)
    state_b = shape((count, heads, 128, 128), bf16)
    pair_b = shape((count, heads, 256, 128), bf16)
    one_b = shape((heads, 128, 128), bf16)
    two_b = shape((heads, 256, 128), bf16)
    unit = count * heads * 2 * 64 * 128 * 128

    gamma, wb, kd, kt, y, n, pre, mb = call(
        kernel_a1, "a1", heads,
        [SMEM, s["tok"], s["tok"], s["tok"], s["beta"], s["wy"]],
        [s["tok"], s["wy"], s["tok"], s["tok"], s["tok"], s["state"], s["pair"], s["whole2"]],
        [tok_f, small_b, tok_b, tok_b, tok_b, state_b, pair_b, two_b],
        [pltpu.VMEM((heads, 256, 128), f32)], (steps,), 8 * unit,
        resets, keys, values, decay, beta, wy_inverse,
    )
    zs = three(mb, False)
    qd, ki, a, at = call(
        kernel_a2, "a2", heads,
        [s["tok"], s["tok"], s["tok"]],
        [s["tok"], s["tok"], s["wy"], s["wy"]],
        [tok_b, tok_b, small_b, small_b],
        [], (steps,), 2 * unit, queries, keys, gamma,
    )
    zs, qd = lax.optimization_barrier((zs, qd))
    slots_b = shape((RING, heads, 256, 128), bf16)
    group, before, zslots = call(
        kernel_f1, "f1", heads, [SMEM] + [VMEM] * 4, [VMEM] * 3, [two_b, two_b, slots_b], [], (),
        unit // 4, place, mb, *zs,
    )
    ys = three(group, True)
    (later_m,) = call(kernel_m, "m", heads, [SMEM, VMEM], [VMEM], [one_b], [], (), unit // 8, place, zslots)
    upstream = lax.dot_general(
        gathered, out_proj, (((1,), (1,)), ((), ())), preferred_element_type=f32
    ).astype(bf16)
    ys, upstream, later_m = lax.optimization_barrier((ys, upstream, later_m))
    state_in, yslots = call(
        kernel_f2, "f2", heads, [SMEM] + [VMEM] * 5, [VMEM] * 2, [one_b, slots_b], [], (),
        unit // 4, place, group, *ys, before,
    )
    e, vp, u, do, du, dt, dgate, r = call(
        kernel_b, "b", heads,
        [s["tok"], s["tok"], s["tok"], s["tok"], s["wy"], s["wy"], s["wy"], s["pair"], s["tok"], s["tok"], s["gain"], s["whole"]],
        [s["state"], s["tok"], s["tok"], s["tok"], s["tok"], s["state"], s["tok"], s["whole"]],
        [state_b, tok_b, tok_b, tok_b, tok_b, state_b, tok_b, one_b],
        [pltpu.VMEM((heads, 128, 128), f32)], (steps,), 12 * unit,
        values, kd, qd, y, wb, a, at, pre, out_gate, upstream, norm_gain.reshape(1, 128), state_in,
    )
    zr = three(r, False)
    (kk,) = call(
        kernel_c0, "c0", heads, [s["tok"]] * 4, [s["tok"]], [tok_b], [], (steps,), 2 * unit, gamma, qd, u, do,
    )
    zr, kk = lax.optimization_barrier((zr, kk))
    rslots_b = shape((RING, heads, 128, 128), bf16)
    rgroup, later, _ = call(
        kernel_r1, "r1", heads, [SMEM] + [VMEM] * 5, [VMEM] * 3, [one_b, one_b, rslots_b], [], (),
        unit // 4, place, r, *zr, zslots,
    )
    yr = three(rgroup, True)
    dq, pq = call(
        kernel_c1, "c1", heads,
        [s["tok"]] * 5 + [s["state"]],
        [s["tok"], s["tok"]], [tok_b, tok_f],
        [], (steps,), 4 * unit, queries, gamma, ki, u, do, e,
    )
    yr, pq = lax.optimization_barrier((yr, pq))
    grad_in, _ = call(
        kernel_r2, "r2", heads, [SMEM] + [VMEM] * 7, [VMEM] * 2, [one_b, rslots_b], [], (),
        unit // 4, place, rgroup, *yr, later, later_m, yslots,
    )
    t = specs(True)
    dk, dv, dd, db = call(
        kernel_c2, "c2", heads,
        [SMEM, t["tok"], t["tok"], t["beta"], t["wy"], t["tok"], t["state"], t["state"], t["tok"], t["tok"], t["tok"], t["state"], t["tok"], t["tok"], t["whole"]],
        [t["tok"], t["tok"], t["tok"], t["beta"]],
        [tok_b, tok_b, tok_f, shape((heads, tokens), f32)],
        [pltpu.VMEM((heads, 128, 128), f32)], (steps,), 10 * unit,
        resets, keys, gamma, beta, wb, kt, n, e, vp, u, du, dt, pq, kk, grad_in,
    )
    return dq, dk, dv, dd, db, dgate


def solution(mesh):
    return jax.shard_map(
        per_device,
        mesh=mesh,
        in_specs=(
            P("seq", "head"),
            P("seq", "head"),
            P("seq", "head"),
            P("seq", "head"),
            P("head", "seq"),
            P("seq", None, "head"),
            P("seq", "head"),
            P(),
            P("head", None),
            P("seq", "head"),
            P("seq"),
        ),
        out_specs=(
            P("seq", "head"),
            P("seq", "head"),
            P("seq", "head"),
            P("seq", "head"),
            P("head", "seq"),
            P("seq", "head"),
        ),
        check_vma=False,
    )
```

time: 227 us -> 122 us (0.54)
  Pallas kernels: 138 us -> 64.1 us
  local copies, waits for them, and re-layouts: 28 us -> 2.76 us
  waiting for transfers between devices: 24.8 us -> 17.9 us
    pallas_call x9 -> x11, Pallas kernels: 138 us -> 64.1 us  [call(): pl.pallas_call(functools.partial(body, heads), out_shape=out_shape, grid=...]
    unnamed x98 -> x26, local copies, waits for them, and re-layouts: 28 us -> 2.76 us
    ppermute x12, waiting for transfers between devices: 24.1 us -> 17.2 us  [permute(): return lax.ppermute(x, 'seq', pairs)]
  transfers between devices with their start and end apart: 13 -> 13, of which waited for: 6 -> 7; matrix products, arithmetic and copies ran while one was open for 0% -> 5% of each run, Pallas kernels for 18% -> 26%
where the time goes in v2:
time: 122 us; the launch traced here: 121 us
  Pallas kernels  64.1 us (53%)
  waiting for transfers between devices  17.9 us (15%)
  between operations  14.8 us (12%)
  starting transfers between devices  14.5 us (12%)
  matrix products  5.97 us (5%)
  local copies, waits for them, and re-layouts  2.76 us (2%)
    pallas_call x11, Pallas kernels, call(): pl.pallas_call(functools.partial(body, heads), out_shape=out_shape, grid=...  64.1 us
    ppermute x12, waiting for transfers between devices, permute(): return lax.ppermute(x, 'seq', pairs)  17.2 us
    ppermute x12, starting transfers between devices, permute(): return lax.ppermute(x, 'seq', pairs)  14.5 us
    dot_general x1, matrix products, per_device(): lax.dot_general(gathered, out_proj, (((1,), (1,)), ((), ())), preferred_e...  5.97 us
    unnamed x26, local copies, waits for them, and re-layouts  2.76 us
  transfers between devices with their start and end apart: 13, of which 7 were waited for; matrix products, arithmetic and copies ran while one was open for 5% of the time, Pallas kernels for 26%

profile of v2, /device:TPU:0, one launch (start us, length us, event | category | flops | bytes accessed | tf_op | source)
XLA Modules:
  0.0 120.6 jit_solution(5409826937103727375)
XLA Ops:
  7.2 0.7 all-gather.2.cloned.1.call-update
  8.6 10.1 %a1.1 = (f32[1024,512]{1,0:T(8,128)}, bf16[16,64,256]{2,1,0:T(8,128)(2,1)}, bf16[1024,512]{1,0:T(8,128)(2,1)}, bf16[1024,512]{1,0:T(8,128)(2,1)}, bf16[1024,512]...) custom-call(s32[1]{0:T(128)S(6)} %copy.17.resets, ...), custom_call_target="tpu_custom_call" | custom-call | flops 1073741824 | bytes 17580036 | tf_op jit(solution)/shard_map/a1/pallas_call | solution.py:422
  18.7 4.2 %collective-permute-start.2 = (bf16[4,256,128]{2,1,0:T(8,128)(2,1)}, bf16[4,256,128]{2,1,0:T(8,128)(2,1)S(1)}, u32[]{:S(2)}, u32[]{:S(2)}) collective-permute-start(bf16[4,256,128]{2,1,0:T(8,128)(2,1)} %get-tuple-element.60.own), channel_id=1, source_target_pairs={{0,24},{8,0},{16,8},{24,16},{32,56},{40,32},{48,40},{56,48},{64,88... | collective-permute-start | bytes 786440 | tf_op jit(solution)/shard_map/ppermute | solution.py:403
  22.9 1.3 %collective-permute-start = (bf16[4,256,128]{2,1,0:T(8,128)(2,1)}, bf16[4,256,128]{2,1,0:T(8,128)(2,1)S(1)}, u32[]{:S(2)}, u32[]{:S(2)}) collective-permute-start(bf16[4,256,128]{2,1,0:T(8,128)(2,1)} %get-tuple-element.60.own), channel_id=1, source_target_pairs={{0,8},{8,16},{16,24},{24,0},{32,40},{40,48},{48,56},{56,32},{64,72... | collective-permute-start | bytes 786440 | tf_op jit(solution)/shard_map/ppermute | solution.py:403
  24.1 5.4 %a2.1 = (bf16[1024,512]{1,0:T(8,128)(2,1)}, bf16[1024,512]{1,0:T(8,128)(2,1)}, bf16[16,64,256]{2,1,0:T(8,128)(2,1)}, bf16[16,64,256]{2,1,0:T(8,128)(2,1)}) custom-call(bf16[1024,512]{1,0:T(8,128)(2,1)} %q_ref.3, bf16[1024,512]{1,0:T(8,128)(2,1)} %k_ref.5, f32[1024,512]{1,0:T(8,128)} %get-tuple-element.57.g_ref), custom_call_target="tpu_custom_call" | custom-call | flops 268435456 | bytes 7340032 | tf_op jit(solution)/shard_map/a2/pallas_call | solution.py:422
  30.1 4.3 %collective-permute-done.2.p3 = bf16[4,256,128]{2,1,0:T(8,128)(2,1)S(1)} collective-permute-done((bf16[4,256,128]{2,1,0:T(8,128)(2,1)}, bf16[4,256,128]{2,1,0:T(8,128)(2,1)S(1)}, u32[]{:S(2)}, u32[]{:S(2)}) %collective-permute-start.2) | collective-permute-done | bytes 262176 | tf_op jit(solution)/shard_map/ppermute | solution.py:403
  34.4 3.3 %collective-permute-done.p1 = bf16[4,256,128]{2,1,0:T(8,128)(2,1)S(1)} collective-permute-done((bf16[4,256,128]{2,1,0:T(8,128)(2,1)}, bf16[4,256,128]{2,1,0:T(8,128)(2,1)S(1)}, u32[]{:S(2)}, u32[]{:S(2)}) %collective-permute-start) | collective-permute-done | bytes 262176 | tf_op jit(solution)/shard_map/ppermute | solution.py:403
  37.7 0.7 copy-done.6
  38.4 2.9 %f1.1 = (bf16[4,256,128]{2,1,0:T(8,128)(2,1)}, bf16[4,256,128]{2,1,0:T(8,128)(2,1)}, bf16[4,4,256,128]{3,2,1,0:T(8,128)(2,1)}) custom-call(s32[2]{0:T(128)} %pad_add_fusion.place, bf16[4,256,128]{2,1,0:T(8,128)(2,1)} %get-tuple-element.60.own, bf16[4,256,128]{2,1,0:T(8,128)(2,1)} %copy-done.6, bf16[4,256,128]{2,1,0:T(8,128)(2,1)} %copy-done.5, ...), custom_call_target="tpu_custom_call" | custom-call | flops 33554432 | bytes 2621448 | tf_op jit(solution)/shard_map/f1/pallas_call | solution.py:422
  41.3 3.0 %collective-permute-start.5 = (bf16[4,256,128]{2,1,0:T(8,128)(2,1)}, bf16[4,256,128]{2,1,0:T(8,128)(2,1)S(1)}, u32[]{:S(2)}, u32[]{:S(2)}) collective-permute-start(bf16[4,256,128]{2,1,0:T(8,128)(2,1)} %get-tuple-element.71.own), channel_id=1, source_target_pairs={{0,96},{8,104},{16,112},{24,120},{32,0},{40,8},{48,16},{56,24},{64... | collective-permute-start | bytes 786440 | tf_op jit(solution)/shard_map/ppermute | solution.py:403
  44.3 0.6 collective-permute-start.4
  45.0 1.0 collective-permute-start.3
  45.9 2.2 %m.1.later_m = bf16[4,128,128]{2,1,0:T(8,128)(2,1)} custom-call(s32[2]{0:T(128)} %pad_add_fusion.place, bf16[4,4,256,128]{3,2,1,0:T(8,128)(2,1)} %get-tuple-element.72.zslots), custom_call_target="tpu_custom_call" | custom-call | flops 16777216 | bytes 1179656 | tf_op jit(solution)/shard_map/m/pallas_call | solution.py:422
  48.2 6.0 %convolution_convert_fusion.up_ref = bf16[1024,512]{1,0:T(8,128)(2,1)} fusion(bf16[1024,2304]{0,1:T(8,128)(2,1)} %all-gather.2.cloned.1.call-done, bf16[512,2304]{1,0:T(8,128)(2,1)S(1)} %copy-done), kind=kOutput, calls=%fused_computation | convolution fusion | flops 2416443392 | bytes 8126464 | tf_op jit(solution)/shard_map/dot_general | solution.py:497
  54.1 1.7 %collective-permute-done.5.p3 = bf16[4,256,128]{2,1,0:T(8,128)(2,1)S(1)} collective-permute-done((bf16[4,256,128]{2,1,0:T(8,128)(2,1)}, bf16[4,256,128]{2,1,0:T(8,128)(2,1)S(1)}, u32[]{:S(2)}, u32[]{:S(2)}) %collective-permute-start.5) | collective-permute-done | bytes 262176 | tf_op jit(solution)/shard_map/ppermute | solution.py:403
  55.8 3.6 %collective-permute-done.3.p1 = bf16[4,256,128]{2,1,0:T(8,128)(2,1)S(1)} collective-permute-done((bf16[4,256,128]{2,1,0:T(8,128)(2,1)}, bf16[4,256,128]{2,1,0:T(8,128)(2,1)S(1)}, u32[]{:S(2)}, u32[]{:S(2)}) %collective-permute-start.3) | collective-permute-done | bytes 262176 | tf_op jit(solution)/shard_map/ppermute | solution.py:403
  59.4 0.7 copy-done.3
  60.1 2.5 %f2.1 = (bf16[4,128,128]{2,1,0:T(8,128)(2,1)}, bf16[4,4,256,128]{3,2,1,0:T(8,128)(2,1)}) custom-call(s32[2]{0:T(128)} %pad_add_fusion.place, bf16[4,256,128]{2,1,0:T(8,128)(2,1)} %get-tuple-element.71.own, bf16[4,256,128]{2,1,0:T(8,128)(2,1)} %copy-done.3, bf16[4,256,128]{2,1,0:T(8,128)(2,1)} %copy-done.2, bf16[4,256,128]{2,1,0:T(8,128)(2,1)} %copy-done.1, ...), custom_call_target="tpu_custom_call" | custom-call | flops 33554432 | bytes 2490376 | tf_op jit(solution)/shard_map/f2/pallas_call | solution.py:422
  62.6 12.7 %b.1 = (bf16[16,4,128,128]{3,2,1,0:T(8,128)(2,1)}, bf16[1024,512]{1,0:T(8,128)(2,1)}, bf16[1024,512]{1,0:T(8,128)(2,1)}, bf16[1024,512]{1,0:T(8,128)(2,1)}, bf16...) custom-call(bf16[1024,512]{1,0:T(8,128)(2,1)} %v_ref.3, ...), custom_call_target="tpu_custom_call" | custom-call | flops 1610612736 | bytes 21758464 | tf_op jit(solution)/shard_map/b/pallas_call | solution.py:422
  75.3 1.0 collective-permute-start.7
  76.3 1.3 %collective-permute-start.6 = (bf16[4,128,128]{2,1,0:T(8,128)(2,1)}, bf16[4,128,128]{2,1,0:T(8,128)(2,1)S(1)}, u32[]{:S(2)}, u32[]{:S(2)}) collective-permute-start(bf16[4,128,128]{2,1,0:T(8,128)(2,1)} %get-tuple-element.88.own), channel_id=1, source_target_pairs={{0,8},{8,16},{16,24},{24,0},{32,40},{40,48},{48,56},{56,32},{64,72... | collective-permute-start | bytes 393224 | tf_op jit(solution)/shard_map/ppermute | solution.py:403
  77.6 4.8 %c0.1.kk_ref = bf16[1024,512]{1,0:T(8,128)(2,1)} custom-call(f32[1024,512]{1,0:T(8,128)} %get-tuple-element.57.g_ref, bf16[1024,512]{1,0:T(8,128)(2,1)} %get-tuple-element.62.qd_ref, bf16[1024,512]{1,0:T(8,128)(2,1)} %get-tuple-element.79.u_ref, bf16[1024,512]{1,0:T(8,128)(2,1)} %get-tuple-element.80.do_ref), custom_call_target="tpu_custom_call" | custom-call | flops 268435456 | bytes 6291456 | tf_op jit(solution)/shard_map/c0/pallas_call | solution.py:422
  82.5 0.9 collective-permute-done.7.p2
  83.4 2.0 %collective-permute-done.6.p1 = bf16[4,128,128]{2,1,0:T(8,128)(2,1)S(1)} collective-permute-done((bf16[4,128,128]{2,1,0:T(8,128)(2,1)}, bf16[4,128,128]{2,1,0:T(8,128)(2,1)S(1)}, u32[]{:S(2)}, u32[]{:S(2)}) %collective-permute-start.6) | collective-permute-done | bytes 131104 | tf_op jit(solution)/shard_map/ppermute | solution.py:403
  85.3 0.7 copy-done.9
  86.0 2.9 %r1.1 = (bf16[4,128,128]{2,1,0:T(8,128)(2,1)}, bf16[4,128,128]{2,1,0:T(8,128)(2,1)}, bf16[4,4,128,128]{3,2,1,0:T(8,128)(2,1)}) custom-call(s32[2]{0:T(128)} %pad_add_fusion.place, bf16[4,128,128]{2,1,0:T(8,128)(2,1)} %get-tuple-element.88.own, bf16[4,128,128]{2,1,0:T(8,128)(2,1)} %copy-done.9, bf16[4,128,128]{2,1,0:T(8,128)(2,1)} %copy-done.8, ...), custom_call_target="tpu_custom_call" | custom-call | flops 33554432 | bytes 2359304 | tf_op jit(solution)/shard_map/r1/pallas_call | solution.py:422
  89.5 1.4 %collective-permute-start.9 = (bf16[4,128,128]{2,1,0:T(8,128)(2,1)}, bf16[4,128,128]{2,1,0:T(8,128)(2,1)S(1)}, u32[]{:S(2)}, u32[]{:S(2)}) collective-permute-start(bf16[4,128,128]{2,1,0:T(8,128)(2,1)} %get-tuple-element.92.own), channel_id=1, source_target_pairs={{0,32},{8,40},{16,48},{24,56},{32,64},{40,72},{48,80},{56,88},{64,... | collective-permute-start | bytes 393224 | tf_op jit(solution)/shard_map/ppermute | solution.py:403
  90.9 6.4 %c1.1 = (bf16[1024,512]{1,0:T(8,128)(2,1)}, f32[1024,512]{1,0:T(8,128)}) custom-call(bf16[1024,512]{1,0:T(8,128)(2,1)} %q_ref.3, f32[1024,512]{1,0:T(8,128)} %get-tuple-element.57.g_ref, bf16[1024,512]{1,0:T(8,128)(2,1)} %get-tuple-element.58.ki_ref, bf16[1024,512]{1,0:T(8,128)(2,1)} %get-tuple-element.79.u_ref, bf16[1024,512]{1,0:T(8,128)(2,1)} %get-tuple-element.80.do_ref, ...), custom_call_target="tpu_custom_call" | custom-call | flops 536870912 | bytes 11534336 | tf_op jit(solution)/shard_map/c1/pallas_call | solution.py:422
  97.3 1.5 %collective-permute-done.9.p1 = bf16[4,128,128]{2,1,0:T(8,128)(2,1)S(1)} collective-permute-done((bf16[4,128,128]{2,1,0:T(8,128)(2,1)}, bf16[4,128,128]{2,1,0:T(8,128)(2,1)S(1)}, u32[]{:S(2)}, u32[]{:S(2)}) %collective-permute-start.9) | collective-permute-done | bytes 131104 | tf_op jit(solution)/shard_map/ppermute | solution.py:403
  98.8 0.6 copy-done.12
  99.5 2.7 %r2.1 = (bf16[4,128,128]{2,1,0:T(8,128)(2,1)}, bf16[4,4,128,128]{3,2,1,0:T(8,128)(2,1)}) custom-call(s32[2]{0:T(128)} %pad_add_fusion.place, bf16[4,128,128]{2,1,0:T(8,128)(2,1)} %get-tuple-element.92.own, bf16[4,128,128]{2,1,0:T(8,128)(2,1)} %copy-done.12, bf16[4,128,128]{2,1,0:T(8,128)(2,1)} %copy-done.11, bf16[4,128,128]{2,1,0:T(8,128)(2,1)} %copy-done.10, ...), custom_call_target="tpu_custom_call" | custom-call | flops 33554432 | bytes 2490376 | tf_op jit(solution)/shard_map/r2/pallas_call | solution.py:422
  102.2 11.5 %c2.1 = (bf16[1024,512]{1,0:T(8,128)(2,1)}, bf16[1024,512]{1,0:T(8,128)(2,1)}, f32[1024,512]{1,0:T(8,128)}, f32[4,1024]{1,0:T(4,128)}) custom-call(s32[1]{0:T(128)S(6)} %copy.17.resets, bf16[1024,512]{1,0:T(8,128)(2,1)} %k_ref.5, f32[1024,512]{1,0:T(8,128)} %get-tuple-element.57.g_ref, f32[4,1024]{1,0:T(4,128)} %b_ref.3, ...), custom_call_target="tpu_custom_call" | custom-call | flops 1342177280 | bytes 21659652 | tf_op jit(solution)/shard_map/c2/pallas_call | solution.py:422
  (34 shorter events, 1.3 us)
Async XLA Ops:
  7.2 41.0 %copy-start = (bf16[512,2304]{1,0:T(8,128)(2,1)S(1)}, bf16[512,2304]{1,0:T(8,128)(2,1)}, u32[]{:S(2)}) copy-start(bf16[512,2304]{1,0:T(8,128)(2,1)} %param.19) | copy-start | bytes 7077892
  7.2 41.0 %all-gather.2.cloned.1.call-start = ((), (), s32[]{:S(2)}) async-start(), calls=%async_computation | async-start | bytes 5308416 | tf_op jit(solution)/shard_map/all_gather | solution.py:448
  18.7 15.7 %collective-permute-start.2 = (bf16[4,256,128]{2,1,0:T(8,128)(2,1)}, bf16[4,256,128]{2,1,0:T(8,128)(2,1)S(1)}, u32[]{:S(2)}, u32[]{:S(2)}) collective-permute-start(bf16[4,256,128]{2,1,0:T(8,128)(2,1)} %get-tuple-element.60.own), channel_id=1, source_target_pairs={{0,24},{8,0},{16,8},{24,16},{32,56},{40,32},{48,40},{56,48},{64,88... | collective-permute-start | bytes 786440 | tf_op jit(solution)/shard_map/ppermute | solution.py:403
  22.9 11.5 %collective-permute-start.1 = (bf16[4,256,128]{2,1,0:T(8,128)(2,1)}, bf16[4,256,128]{2,1,0:T(8,128)(2,1)S(1)}, u32[]{:S(2)}, u32[]{:S(2)}) collective-permute-start(bf16[4,256,128]{2,1,0:T(8,128)(2,1)} %get-tuple-element.60.own), channel_id=1, source_target_pairs={{0,16},{8,24},{16,0},{24,8},{32,48},{40,56},{48,32},{56,40},{64,80... | collective-permute-start | bytes 786440 | tf_op jit(solution)/shard_map/ppermute | solution.py:403
  22.9 14.8 %collective-permute-start = (bf16[4,256,128]{2,1,0:T(8,128)(2,1)}, bf16[4,256,128]{2,1,0:T(8,128)(2,1)S(1)}, u32[]{:S(2)}, u32[]{:S(2)}) collective-permute-start(bf16[4,256,128]{2,1,0:T(8,128)(2,1)} %get-tuple-element.60.own), channel_id=1, source_target_pairs={{0,8},{8,16},{16,24},{24,0},{32,40},{40,48},{48,56},{56,32},{64,72... | collective-permute-start | bytes 786440 | tf_op jit(solution)/shard_map/ppermute | solution.py:403
  34.4 3.3 %copy-start.4 = (bf16[4,256,128]{2,1,0:T(8,128)(2,1)}, bf16[4,256,128]{2,1,0:T(8,128)(2,1)S(1)}, u32[]{:S(2)}) copy-start(bf16[4,256,128]{2,1,0:T(8,128)(2,1)S(1)} %collective-permute-done.2.p3) | copy-start | bytes 786436
  34.4 3.3 %copy-start.5 = (bf16[4,256,128]{2,1,0:T(8,128)(2,1)}, bf16[4,256,128]{2,1,0:T(8,128)(2,1)S(1)}, u32[]{:S(2)}) copy-start(bf16[4,256,128]{2,1,0:T(8,128)(2,1)S(1)} %collective-permute-done.1.p2) | copy-start | bytes 786436
  37.7 0.7 copy-start.6
  41.3 14.5 %collective-permute-start.5 = (bf16[4,256,128]{2,1,0:T(8,128)(2,1)}, bf16[4,256,128]{2,1,0:T(8,128)(2,1)S(1)}, u32[]{:S(2)}, u32[]{:S(2)}) collective-permute-start(bf16[4,256,128]{2,1,0:T(8,128)(2,1)} %get-tuple-element.71.own), channel_id=1, source_target_pairs={{0,96},{8,104},{16,112},{24,120},{32,0},{40,8},{48,16},{56,24},{64... | collective-permute-start | bytes 786440 | tf_op jit(solution)/shard_map/ppermute | solution.py:403
  44.3 11.5 %collective-permute-start.4 = (bf16[4,256,128]{2,1,0:T(8,128)(2,1)}, bf16[4,256,128]{2,1,0:T(8,128)(2,1)S(1)}, u32[]{:S(2)}, u32[]{:S(2)}) collective-permute-start(bf16[4,256,128]{2,1,0:T(8,128)(2,1)} %get-tuple-element.71.own), channel_id=1, source_target_pairs={{0,64},{8,72},{16,80},{24,88},{32,96},{40,104},{48,112},{56,120},{... | collective-permute-start | bytes 786440 | tf_op jit(solution)/shard_map/ppermute | solution.py:403
  45.0 14.4 %collective-permute-start.3 = (bf16[4,256,128]{2,1,0:T(8,128)(2,1)}, bf16[4,256,128]{2,1,0:T(8,128)(2,1)S(1)}, u32[]{:S(2)}, u32[]{:S(2)}) collective-permute-start(bf16[4,256,128]{2,1,0:T(8,128)(2,1)} %get-tuple-element.71.own), channel_id=1, source_target_pairs={{0,32},{8,40},{16,48},{24,56},{32,64},{40,72},{48,80},{56,88},{64,... | collective-permute-start | bytes 786440 | tf_op jit(solution)/shard_map/ppermute | solution.py:403
  55.8 3.6 %copy-start.1 = (bf16[4,256,128]{2,1,0:T(8,128)(2,1)}, bf16[4,256,128]{2,1,0:T(8,128)(2,1)S(1)}, u32[]{:S(2)}) copy-start(bf16[4,256,128]{2,1,0:T(8,128)(2,1)S(1)} %collective-permute-done.5.p3) | copy-start | bytes 786436
  55.8 3.6 %copy-start.2 = (bf16[4,256,128]{2,1,0:T(8,128)(2,1)}, bf16[4,256,128]{2,1,0:T(8,128)(2,1)S(1)}, u32[]{:S(2)}) copy-start(bf16[4,256,128]{2,1,0:T(8,128)(2,1)S(1)} %collective-permute-done.4.p2) | copy-start | bytes 786436
  59.4 0.7 copy-start.3
  75.2 7.2 %collective-permute-start.8 = (bf16[4,128,128]{2,1,0:T(8,128)(2,1)}, bf16[4,128,128]{2,1,0:T(8,128)(2,1)S(1)}, u32[]{:S(2)}, u32[]{:S(2)}) collective-permute-start(bf16[4,128,128]{2,1,0:T(8,128)(2,1)} %get-tuple-element.88.own), channel_id=1, source_target_pairs={{0,24},{8,0},{16,8},{24,16},{32,56},{40,32},{48,40},{56,48},{64,88... | collective-permute-start | bytes 393224 | tf_op jit(solution)/shard_map/ppermute | solution.py:403
  75.3 8.0 %collective-permute-start.7 = (bf16[4,128,128]{2,1,0:T(8,128)(2,1)}, bf16[4,128,128]{2,1,0:T(8,128)(2,1)S(1)}, u32[]{:S(2)}, u32[]{:S(2)}) collective-permute-start(bf16[4,128,128]{2,1,0:T(8,128)(2,1)} %get-tuple-element.88.own), channel_id=1, source_target_pairs={{0,16},{8,24},{16,0},{24,8},{32,48},{40,56},{48,32},{56,40},{64,80... | collective-permute-start | bytes 393224 | tf_op jit(solution)/shard_map/ppermute | solution.py:403
  76.3 9.0 %collective-permute-start.6 = (bf16[4,128,128]{2,1,0:T(8,128)(2,1)}, bf16[4,128,128]{2,1,0:T(8,128)(2,1)S(1)}, u32[]{:S(2)}, u32[]{:S(2)}) collective-permute-start(bf16[4,128,128]{2,1,0:T(8,128)(2,1)} %get-tuple-element.88.own), channel_id=1, source_target_pairs={{0,8},{8,16},{16,24},{24,0},{32,40},{40,48},{48,56},{56,32},{64,72... | collective-permute-start | bytes 393224 | tf_op jit(solution)/shard_map/ppermute | solution.py:403
  82.5 2.9 %copy-start.7 = (bf16[4,128,128]{2,1,0:T(8,128)(2,1)}, bf16[4,128,128]{2,1,0:T(8,128)(2,1)S(1)}, u32[]{:S(2)}) copy-start(bf16[4,128,128]{2,1,0:T(8,128)(2,1)S(1)} %collective-permute-done.8.p3) | copy-start | bytes 393220
  83.4 2.0 %copy-start.8 = (bf16[4,128,128]{2,1,0:T(8,128)(2,1)}, bf16[4,128,128]{2,1,0:T(8,128)(2,1)S(1)}, u32[]{:S(2)}) copy-start(bf16[4,128,128]{2,1,0:T(8,128)(2,1)S(1)} %collective-permute-done.7.p2) | copy-start | bytes 393220
  85.3 0.7 copy-start.9
  88.9 8.4 %collective-permute-start.11 = (bf16[4,128,128]{2,1,0:T(8,128)(2,1)}, bf16[4,128,128]{2,1,0:T(8,128)(2,1)S(1)}, u32[]{:S(2)}, u32[]{:S(2)}) collective-permute-start(bf16[4,128,128]{2,1,0:T(8,128)(2,1)} %get-tuple-element.92.own), channel_id=1, source_target_pairs={{0,96},{8,104},{16,112},{24,120},{32,0},{40,8},{48,16},{56,24},{64... | collective-permute-start | bytes 393224 | tf_op jit(solution)/shard_map/ppermute | solution.py:403
  88.9 8.4 %collective-permute-start.10 = (bf16[4,128,128]{2,1,0:T(8,128)(2,1)}, bf16[4,128,128]{2,1,0:T(8,128)(2,1)S(1)}, u32[]{:S(2)}, u32[]{:S(2)}) collective-permute-start(bf16[4,128,128]{2,1,0:T(8,128)(2,1)} %get-tuple-element.92.own), channel_id=1, source_target_pairs={{0,64},{8,72},{16,80},{24,88},{32,96},{40,104},{48,112},{56,120},{... | collective-permute-start | bytes 393224 | tf_op jit(solution)/shard_map/ppermute | solution.py:403
  89.5 9.3 %collective-permute-start.9 = (bf16[4,128,128]{2,1,0:T(8,128)(2,1)}, bf16[4,128,128]{2,1,0:T(8,128)(2,1)S(1)}, u32[]{:S(2)}, u32[]{:S(2)}) collective-permute-start(bf16[4,128,128]{2,1,0:T(8,128)(2,1)} %get-tuple-element.92.own), channel_id=1, source_target_pairs={{0,32},{8,40},{16,48},{24,56},{32,64},{40,72},{48,80},{56,88},{64,... | collective-permute-start | bytes 393224 | tf_op jit(solution)/shard_map/ppermute | solution.py:403
  97.3 1.5 %copy-start.10 = (bf16[4,128,128]{2,1,0:T(8,128)(2,1)}, bf16[4,128,128]{2,1,0:T(8,128)(2,1)S(1)}, u32[]{:S(2)}) copy-start(bf16[4,128,128]{2,1,0:T(8,128)(2,1)S(1)} %collective-permute-done.11.p3) | copy-start | bytes 393220
  97.3 1.5 %copy-start.11 = (bf16[4,128,128]{2,1,0:T(8,128)(2,1)}, bf16[4,128,128]{2,1,0:T(8,128)(2,1)S(1)}, u32[]{:S(2)}) copy-start(bf16[4,128,128]{2,1,0:T(8,128)(2,1)S(1)} %collective-permute-done.10.p2) | copy-start | bytes 393220
  98.8 0.7 copy-start.12
Sparse Core Ops, SparseCore 0:
  9.7 36.7 all-gather.1

commit v3 on v2

--- a/solution.py
+++ b/solution.py
@@ -70,9 +70,19 @@
     return [f(*xs) for xs in zip(*lists)]
 
 
+def spread(me, array, outs):
+    for shift, out in enumerate(outs):
+        out[...] = array[lax.rem(me + shift, RING)].astype(out.dtype)
+
+
+def collect(me, array, arrived):
+    for shift, other in enumerate(arrived):
+        array[lax.rem(me + RING - shift, RING)] = other[...].astype(array.dtype)
+
+
 def kernel_a1(
-    heads, resets, k_ref, v_ref, d_ref, b_ref, w_ref,
-    g_ref, wb_ref, kd_ref, kt_ref, y_ref, n_ref, pre_ref, mb_ref, state,
+    heads, place, resets, k_ref, v_ref, d_ref, b_ref, w_ref,
+    g_ref, wb_ref, kd_ref, kt_ref, y_ref, n_ref, pre_ref, o0, o1, o2, o3, state,
 ):
     step = pl.program_id(0)
 
@@ -119,8 +129,7 @@
 
     @pl.when(step == pl.num_programs(0) - 1)
     def _():
-        for h in range(heads):
-            mb_ref[h] = rs[h].astype(bf16)
+        spread(place[1], state, (o0, o1, o2, o3))
 
 
 def kernel_a2(heads, q_ref, k_ref, g_ref, qd_ref, ki_ref, a_ref, at_ref):
@@ -142,14 +151,15 @@
 
 
 def kernel_b(
-    heads, v_ref, kd_ref, qd_ref, y_ref, wb_ref, a_ref, at_ref, pre_ref, gate_ref, up_ref, gain_ref, s_ref,
-    e_ref, vp_ref, u_ref, do_ref, du_ref, dt_ref, dg_ref, r_ref, total,
+    heads, place, v_ref, kd_ref, qd_ref, y_ref, wb_ref, a_ref, at_ref, pre_ref, gate_ref, up_ref, gain_ref,
+    s0, s1, s2, s3, e_ref, vp_ref, u_ref, do_ref, du_ref, dt_ref, dg_ref, r0, r1, r2, r3, total, s_ref,
 ):
     step = pl.program_id(0)
 
     @pl.when(step == 0)
     def _():
         total[...] = jnp.zeros_like(total)
+        collect(place[1], s_ref, (s0, s1, s2, s3))
 
     gain = gain_ref[...]
     sums = [total[h] for h in range(heads)]
@@ -201,8 +211,7 @@
 
     @pl.when(step == pl.num_programs(0) - 1)
     def _():
-        for h in range(heads):
-            r_ref[h] = sums[h].astype(bf16)
+        spread(place[1], total, (r0, r1, r2, r3))
 
 
 def kernel_c1(heads, q_ref, g_ref, ki_ref, u_ref, do_ref, e_ref, dq_ref, pq_ref):
@@ -245,15 +254,15 @@
 
 
 def kernel_c2(
-    heads, resets, k_ref, g_ref, b_ref, wb_ref, kt_ref, n_ref, e_ref, vp_ref, u_ref, du_ref, dt_ref,
-    pq_ref, kk_ref, gin_ref, dk_ref, dv_ref, dd_ref, db_ref, state,
+    heads, place, resets, k_ref, g_ref, b_ref, wb_ref, kt_ref, n_ref, e_ref, vp_ref, u_ref, du_ref, dt_ref,
+    pq_ref, kk_ref, g0, g1, g2, g3, dk_ref, dv_ref, dd_ref, db_ref, state,
 ):
     step = pl.program_id(0)
-    place = pl.num_programs(0) - 1 - step
+    turn = pl.num_programs(0) - 1 - step
 
     @pl.when(step == 0)
     def _():
-        state[...] = gin_ref[...].astype(f32)
+        collect(place[1], state, (g0, g1, g2, g3))
 
     weights = twice(True)
     ones = jnp.ones((16, 128), bf16)
@@ -261,7 +270,7 @@
     gbs = {}
     now = [state[h] for h in range(heads)]
     for c in reversed(range(STEP)):
-        keep = (place * STEP + c != resets[0]).astype(f32)
+        keep = (turn * STEP + c != resets[0]).astype(f32)
         for h in range(heads):
             grads[c, h] = now[h]
             gbs[c, h] = now[h].astype(bf16)
@@ -313,85 +322,79 @@
             db_ref[h : h + 1, half(c)] = db / b_ref[h : h + 1, half(c)]
 
 
-def gather_slots(me, own, others, slots):
-    slots[me] = own[...]
-    for shift, other in enumerate(others, 1):
-        slots[lax.rem(me + RING - shift, RING)] = other[...]
-
-
 def identity_pair():
     row = lax.broadcasted_iota(jnp.int32, (256, 128), 0)
     col = lax.broadcasted_iota(jnp.int32, (256, 128), 1)
-    return (row == col + 128).astype(f32)
+    return (row == col + 128).astype(bf16)
 
 
 def after(pair, r):
-    moved = nn(r.astype(bf16), pair[128:256])
+    moved = nn(r, pair[128:256])
     return jnp.concatenate([moved[0:128] + pair[0:128].astype(f32), moved[128:256]], axis=0)
 
 
-def kernel_f1(heads, place, own, p1, p2, p3, total_ref, before_ref, slots):
-    me = place[1]
-    gather_slots(me, own, (p1, p2, p3), slots)
-    start = identity_pair()
-    rs = [slots[0, h].astype(f32) for h in range(heads)]
-    befores = [jnp.where(me == 0, start, r) for r in rs]
+def kernel_f1(heads, place, p0, p1, p2, p3, total_ref, before_ref, slots):
+    collect(place[1], slots, (p0, p1, p2, p3))
+    before_ref[0] = identity_pair()
+    r = slots[0]
     for z in range(1, RING):
-        befores = [jnp.where(z < me, after(slots[z, h], r), b) for h, (r, b) in enumerate(zip(rs, befores))]
-        rs = [after(slots[z, h], r) for h, r in enumerate(rs)]
-    for h in range(heads):
-        total_ref[h] = rs[h].astype(bf16)
-        before_ref[h] = befores[h].astype(bf16)
-
-
-def kernel_f2(heads, place, own, p1, p2, p3, before, s_ref, slots):
-    me = place[0]
-    gather_slots(me, own, (p1, p2, p3), slots)
-    ss = [jnp.where(me > 0, slots[0, h, 0:128].astype(f32), 0.0) for h in range(heads)]
-    for i in range(1, RING - 1):
-        moved = [
-            nn(s.astype(bf16), slots[i, h, 128:256]) + slots[i, h, 0:128].astype(f32) for h, s in enumerate(ss)
-        ]
-        ss = [jnp.where(i < me, m, s) for m, s in zip(moved, ss)]
-    ss = [nn(s.astype(bf16), before[h, 128:256]) + before[h, 0:128].astype(f32) for h, s in enumerate(ss)]
-    for h in range(heads):
-        s_ref[h] = ss[h].astype(bf16)
-
-
-def kernel_m(heads, place, zslots, m_ref):
-    me = place[1]
+        before_ref[z] = r
+        r = after(slots[z], r).astype(bf16)
+    total_ref[...] = r
+
+
+def kernel_m(heads, slots, m_ref):
     row = lax.broadcasted_iota(jnp.int32, (128, 128), 0)
     col = lax.broadcasted_iota(jnp.int32, (128, 128), 1)
-    ms = [jnp.where(me < RING - 1, zslots[RING - 1, h, 128:256].astype(f32), (row == col).astype(f32)) for h in range(heads)]
+    m_ref[RING - 1] = (row == col).astype(bf16)
+    m = slots[RING - 1, 128:256]
+    m_ref[RING - 2] = m
+    for z in reversed(range(1, RING - 1)):
+        m = nn(slots[z, 128:256], m).astype(bf16)
+        m_ref[z - 1] = m
+
+
+def kernel_f2(heads, place, p0, p1, p2, p3, before, o0, o1, o2, o3, slots, states):
+    me = place[0]
+    collect(me, slots, (p0, p1, p2, p3))
+    s = jnp.where(me > 0, slots[0, 0:128].astype(f32), 0.0)
+    for i in range(1, RING - 1):
+        moved = nn(s.astype(bf16), slots[i, 128:256]) + slots[i, 0:128].astype(f32)
+        s = jnp.where(i < me, moved, s)
+    sb = s.astype(bf16)
+    moved = [nn(sb, before[z, 128:256]) for z in range(RING)]
+    for z in range(RING):
+        states[z] = (moved[z] + before[z, 0:128].astype(f32)).astype(bf16)
+    spread(place[1], states, (o0, o1, o2, o3))
+
+
+def kernel_r1(heads, place, p0, p1, p2, p3, before, total_ref, slots):
+    collect(place[1], slots, (p0, p1, p2, p3))
+    parts = [nt(slots[z], before[z, 128:256]) for z in range(1, RING)]
+    total_ref[...] = (slots[0].astype(f32) + sum(parts)).astype(bf16)
+
+
+def kernel_r3(heads, slots, zslots, later_ref):
+    later_ref[RING - 1] = jnp.zeros((128, 128), bf16)
+    g = slots[RING - 1]
+    later_ref[RING - 2] = g
+    for z in reversed(range(1, RING - 1)):
+        g = (nt(g, zslots[z, 128:256]) + slots[z].astype(f32)).astype(bf16)
+        later_ref[z - 1] = g
+
+
+def kernel_r2(heads, place, p0, p1, p2, p3, later, later_m, yslots, o0, o1, o2, o3, slots, grads):
+    me = place[0]
+    collect(me, slots, (p0, p1, p2, p3))
+    g = jnp.where(me < RING - 1, slots[RING - 1].astype(f32), 0.0)
     for i in reversed(range(1, RING - 1)):
-        moved = [nn(zslots[i, h, 128:256], m.astype(bf16)) for h, m in enumerate(ms)]
-        ms = [jnp.where(i > me, x, m) for x, m in zip(moved, ms)]
-    for h in range(heads):
-        m_ref[h] = ms[h].astype(bf16)
-
-
-def kernel_r1(heads, place, own, p1, p2, p3, zslots, total_ref, later_ref, slots):
-    me = place[1]
-    gather_slots(me, own, (p1, p2, p3), slots)
-    gs = [slots[RING - 1, h].astype(f32) for h in range(heads)]
-    laters = [jnp.where(me < RING - 1, g, 0.0) for g in gs]
-    for z in reversed(range(RING - 1)):
-        gs = [nt(g.astype(bf16), zslots[z, h, 128:256]) + slots[z, h].astype(f32) for h, g in enumerate(gs)]
-        laters = [jnp.where(z > me, g, x) for g, x in zip(gs, laters)]
-    for h in range(heads):
-        total_ref[h] = gs[h].astype(bf16)
-        later_ref[h] = laters[h].astype(bf16)
-
-
-def kernel_r2(heads, place, own, p1, p2, p3, later, later_m, yslots, g_ref, slots):
-    me = place[0]
-    gather_slots(me, own, (p1, p2, p3), slots)
-    gs = [jnp.where(me < RING - 1, slots[RING - 1, h].astype(f32), 0.0) for h in range(heads)]
-    for i in reversed(range(1, RING - 1)):
-        moved = [nt(g.astype(bf16), yslots[i, h, 128:256]) + slots[i, h].astype(f32) for h, g in enumerate(gs)]
-        gs = [jnp.where(i > me, m, g) for m, g in zip(moved, gs)]
-    for h in range(heads):
-        g_ref[h] = (nt(gs[h].astype(bf16), later_m[h]) + later[h].astype(f32)).astype(bf16)
+        moved = nt(g.astype(bf16), yslots[i, 128:256]) + slots[i].astype(f32)
+        g = jnp.where(i > me, moved, g)
+    gb = g.astype(bf16)
+    moved = [nt(gb, later_m[z]) for z in range(RING)]
+    for z in range(RING):
+        grads[z] = (moved[z] + later[z].astype(f32)).astype(bf16)
+    spread(place[1], grads, (o0, o1, o2, o3))
 
 
 def permute(x, distance, outer):
@@ -404,10 +407,12 @@
 
 
 def three(x, outer):
-    return [permute(x, distance, outer) for distance in (1, 2, 3)]
-
-
-VMEM_LIMIT = 60 * 2**20
+    arrays = [x] * RING if outer else x
+    return [arrays[0]] + [permute(arrays[distance], distance, outer) for distance in (1, 2, 3)]
+
+
+BIG = 54 * 2**20
+SMALL = 8 * 2**20
 SMEM = pl.BlockSpec(memory_space=pltpu.SMEM)
 VMEM = pl.BlockSpec(memory_space=pltpu.VMEM)
 
@@ -427,7 +432,7 @@
         out_specs=out_specs,
         scratch_shapes=scratch,
         compiler_params=pltpu.CompilerParams(
-            vmem_limit_bytes=VMEM_LIMIT,
+            vmem_limit_bytes=BIG if grid else SMALL,
             **({"dimension_semantics": ("arbitrary",)} if grid else {}),
         ),
         cost_estimate=pl.CostEstimate(flops=flops, bytes_accessed=total, transcendentals=0),
@@ -455,8 +460,8 @@
             wy=pl.BlockSpec((STEP, GROUP, heads * GROUP), lambda i: (at(i), 0, 0)),
             state=pl.BlockSpec((STEP, heads, 128, 128), lambda i: (at(i), 0, 0, 0)),
             pair=pl.BlockSpec((STEP, heads, 256, 128), lambda i: (at(i), 0, 0, 0)),
-            whole=pl.BlockSpec((heads, 128, 128), lambda i: (0, 0, 0)),
-            whole2=pl.BlockSpec((heads, 256, 128), lambda i: (0, 0, 0)),
+            whole=pl.BlockSpec((128, 128), lambda i: (0, 0)),
+            whole2=pl.BlockSpec((256, 128), lambda i: (0, 0)),
             gain=pl.BlockSpec((1, 128), lambda i: (0, 0)),
         )
 
@@ -466,17 +471,19 @@
     small_b = shape((count, GROUP, heads * GROUP), bf16)
     state_b = shape((count, heads, 128, 128), bf16)
     pair_b = shape((count, heads, 256, 128), bf16)
-    one_b = shape((heads, 128, 128), bf16)
-    two_b = shape((heads, 256, 128), bf16)
+    one_b = shape((128, 128), bf16)
+    two_b = shape((256, 128), bf16)
+    ones_b = shape((RING, 128, 128), bf16)
+    twos_b = shape((RING, 256, 128), bf16)
     unit = count * heads * 2 * 64 * 128 * 128
 
-    gamma, wb, kd, kt, y, n, pre, mb = call(
+    gamma, wb, kd, kt, y, n, pre, *mb = call(
         kernel_a1, "a1", heads,
-        [SMEM, s["tok"], s["tok"], s["tok"], s["beta"], s["wy"]],
-        [s["tok"], s["wy"], s["tok"], s["tok"], s["tok"], s["state"], s["pair"], s["whole2"]],
-        [tok_f, small_b, tok_b, tok_b, tok_b, state_b, pair_b, two_b],
+        [SMEM, SMEM, s["tok"], s["tok"], s["tok"], s["beta"], s["wy"]],
+        [s["tok"], s["wy"], s["tok"], s["tok"], s["tok"], s["state"], s["pair"]] + [s["whole2"]] * 4,
+        [tok_f, small_b, tok_b, tok_b, tok_b, state_b, pair_b] + [two_b] * 4,
         [pltpu.VMEM((heads, 256, 128), f32)], (steps,), 8 * unit,
-        resets, keys, values, decay, beta, wy_inverse,
+        place, resets, keys, values, decay, beta, wy_inverse,
     )
     zs = three(mb, False)
     qd, ki, a, at = call(
@@ -487,59 +494,61 @@
         [], (steps,), 2 * unit, queries, keys, gamma,
     )
     zs, qd = lax.optimization_barrier((zs, qd))
-    slots_b = shape((RING, heads, 256, 128), bf16)
     group, before, zslots = call(
-        kernel_f1, "f1", heads, [SMEM] + [VMEM] * 4, [VMEM] * 3, [two_b, two_b, slots_b], [], (),
-        unit // 4, place, mb, *zs,
+        kernel_f1, "f1", heads, [SMEM] + [VMEM] * 4, [VMEM] * 3, [two_b, twos_b, twos_b], [], (),
+        unit // 8, place, *zs,
     )
     ys = three(group, True)
-    (later_m,) = call(kernel_m, "m", heads, [SMEM, VMEM], [VMEM], [one_b], [], (), unit // 8, place, zslots)
+    (later_m,) = call(kernel_m, "m", heads, [VMEM], [VMEM], [ones_b], [], (), unit // 16, zslots)
+    ys, later_m = lax.optimization_barrier((ys, later_m))
+    *states, yslots = call(
+        kernel_f2, "f2", heads, [SMEM] + [VMEM] * 5, [VMEM] * 5, [one_b] * 4 + [twos_b],
+        [pltpu.VMEM((RING, 128, 128), bf16)], (), unit // 8, place, *ys, before,
+    )
+    state_in = three(states, False)
     upstream = lax.dot_general(
         gathered, out_proj, (((1,), (1,)), ((), ())), preferred_element_type=f32
     ).astype(bf16)
-    ys, upstream, later_m = lax.optimization_barrier((ys, upstream, later_m))
-    state_in, yslots = call(
-        kernel_f2, "f2", heads, [SMEM] + [VMEM] * 5, [VMEM] * 2, [one_b, slots_b], [], (),
-        unit // 4, place, group, *ys, before,
-    )
-    e, vp, u, do, du, dt, dgate, r = call(
+    state_in, upstream = lax.optimization_barrier((state_in, upstream))
+    e, vp, u, do, du, dt, dgate, *r = call(
         kernel_b, "b", heads,
-        [s["tok"], s["tok"], s["tok"], s["tok"], s["wy"], s["wy"], s["wy"], s["pair"], s["tok"], s["tok"], s["gain"], s["whole"]],
-        [s["state"], s["tok"], s["tok"], s["tok"], s["tok"], s["state"], s["tok"], s["whole"]],
-        [state_b, tok_b, tok_b, tok_b, tok_b, state_b, tok_b, one_b],
-        [pltpu.VMEM((heads, 128, 128), f32)], (steps,), 12 * unit,
-        values, kd, qd, y, wb, a, at, pre, out_gate, upstream, norm_gain.reshape(1, 128), state_in,
+        [SMEM, s["tok"], s["tok"], s["tok"], s["tok"], s["wy"], s["wy"], s["wy"], s["pair"], s["tok"], s["tok"], s["gain"]] + [s["whole"]] * 4,
+        [s["state"], s["tok"], s["tok"], s["tok"], s["tok"], s["state"], s["tok"]] + [s["whole"]] * 4,
+        [state_b, tok_b, tok_b, tok_b, tok_b, state_b, tok_b] + [one_b] * 4,
+        [pltpu.VMEM((heads, 128, 128), f32), pltpu.VMEM((heads, 128, 128), bf16)], (steps,), 12 * unit,
+        place, values, kd, qd, y, wb, a, at, pre, out_gate, upstream, norm_gain.reshape(1, 128), *state_in,
     )
     zr = three(r, False)
     (kk,) = call(
         kernel_c0, "c0", heads, [s["tok"]] * 4, [s["tok"]], [tok_b], [], (steps,), 2 * unit, gamma, qd, u, do,
     )
     zr, kk = lax.optimization_barrier((zr, kk))
-    rslots_b = shape((RING, heads, 128, 128), bf16)
-    rgroup, later, _ = call(
-        kernel_r1, "r1", heads, [SMEM] + [VMEM] * 5, [VMEM] * 3, [one_b, one_b, rslots_b], [], (),
-        unit // 4, place, r, *zr, zslots,
+    rgroup, rslots = call(
+        kernel_r1, "r1", heads, [SMEM] + [VMEM] * 5, [VMEM] * 2, [one_b, ones_b], [], (),
+        unit // 16, place, *zr, before,
     )
     yr = three(rgroup, True)
+    (later,) = call(kernel_r3, "r3", heads, [VMEM] * 2, [VMEM], [ones_b], [], (), unit // 16, rslots, zslots)
     dq, pq = call(
         kernel_c1, "c1", heads,
         [s["tok"]] * 5 + [s["state"]],
         [s["tok"], s["tok"]], [tok_b, tok_f],
         [], (steps,), 4 * unit, queries, gamma, ki, u, do, e,
     )
-    yr, pq = lax.optimization_barrier((yr, pq))
-    grad_in, _ = call(
-        kernel_r2, "r2", heads, [SMEM] + [VMEM] * 7, [VMEM] * 2, [one_b, rslots_b], [], (),
-        unit // 4, place, rgroup, *yr, later, later_m, yslots,
-    )
+    yr, pq, later = lax.optimization_barrier((yr, pq, later))
+    *grads, _ = call(
+        kernel_r2, "r2", heads, [SMEM] + [VMEM] * 7, [VMEM] * 5, [one_b] * 4 + [ones_b],
+        [pltpu.VMEM((RING, 128, 128), bf16)], (), unit // 16, place, *yr, later, later_m, yslots,
+    )
+    grad_in = three(grads, False)
     t = specs(True)
     dk, dv, dd, db = call(
         kernel_c2, "c2", heads,
-        [SMEM, t["tok"], t["tok"], t["beta"], t["wy"], t["tok"], t["state"], t["state"], t["tok"], t["tok"], t["tok"], t["state"], t["tok"], t["tok"], t["whole"]],
+        [SMEM, SMEM, t["tok"], t["tok"], t["beta"], t["wy"], t["tok"], t["state"], t["state"], t["tok"], t["tok"], t["tok"], t["state"], t["tok"], t["tok"]] + [t["whole"]] * 4,
         [t["tok"], t["tok"], t["tok"], t["beta"]],
         [tok_b, tok_b, tok_f, shape((heads, tokens), f32)],
         [pltpu.VMEM((heads, 128, 128), f32)], (steps,), 10 * unit,
-        resets, keys, gamma, beta, wb, kt, n, e, vp, u, du, dt, pq, kk, grad_in,
+        place, resets, keys, gamma, beta, wb, kt, n, e, vp, u, du, dt, pq, kk, *grad_in,
     )
     return dq, dk, dv, dd, db, dgate
 

time: 122 us -> 117 us (0.959)
  starting transfers between devices: 14.5 us -> 28.1 us
  waiting for transfers between devices: 17.9 us -> 8.29 us
  Pallas kernels: 64.1 us -> 55.7 us
    ppermute x12 -> x18, starting transfers between devices: 14.5 us -> 28.1 us  [permute(): return lax.ppermute(x, 'seq', pairs)]
    ppermute x12 -> x18, waiting for transfers between devices: 17.2 us -> 7.61 us  [permute(): return lax.ppermute(x, 'seq', pairs)]
    pallas_call x11 -> x12, Pallas kernels: 64.1 us -> 55.7 us  [call(): pl.pallas_call(functools.partial(body, heads), out_shape=out_shape, grid=...]
  transfers between devices with their start and end apart: 13 -> 19, of which waited for: 7 -> 5; matrix products, arithmetic and copies ran while one was open for 5% -> 6% of each run, Pallas kernels for 26% -> 25%
where the time goes in v3:
time: 117 us; the launch traced here: 116 us
  Pallas kernels  55.7 us (48%)
  starting transfers between devices  28.1 us (24%)
  between operations  14.9 us (13%)
  waiting for transfers between devices  8.29 us (7%)
  matrix products  5.99 us (5%)
  local copies, waits for them, and re-layouts  2.43 us (2%)
    pallas_call x12, Pallas kernels, call(): pl.pallas_call(functools.partial(body, heads), out_shape=out_shape, grid=...  55.7 us
    ppermute x18, starting transfers between devices, permute(): return lax.ppermute(x, 'seq', pairs)  28.1 us
    ppermute x18, waiting for transfers between devices, permute(): return lax.ppermute(x, 'seq', pairs)  7.61 us
    dot_general x1, matrix products, per_device(): lax.dot_general(gathered, out_proj, (((1,), (1,)), ((), ())), preferred_e...  5.99 us
    unnamed x26, local copies, waits for them, and re-layouts  2.43 us
  transfers between devices with their start and end apart: 19, of which 5 were waited for; matrix products, arithmetic and copies ran while one was open for 6% of the time, Pallas kernels for 25%

profile of v3, /device:TPU:0, one launch (start us, length us, event | category | flops | bytes accessed | tf_op | source)
XLA Modules:
  0.0 116.0 jit_solution(9249508467297051210)
XLA Ops:
  7.2 0.7 all-gather.2.cloned.1.call-update
  9.2 10.1 %a1.1 = (f32[1024,512]{1,0:T(8,128)}, bf16[16,64,256]{2,1,0:T(8,128)(2,1)}, bf16[1024,512]{1,0:T(8,128)(2,1)}, bf16[1024,512]{1,0:T(8,128)(2,1)}, bf16[1024,512]...) custom-call(s32[2]{0:T(128)} %pad_add_fusion.place, ...), custom_call_target="tpu_custom_call" | custom-call | flops 1073741824 | bytes 17580044 | tf_op jit(solution)/shard_map/a1/pallas_call | solution.py:427
  19.3 2.1 %collective-permute-start = (bf16[256,128]{1,0:T(8,128)(2,1)}, bf16[256,128]{1,0:T(8,128)(2,1)S(1)}, u32[]{:S(2)}, u32[]{:S(2)}) collective-permute-start(bf16[256,128]{1,0:T(8,128)(2,1)} %get-tuple-element.82), channel_id=1, source_target_pairs={{0,8},{8,16},{16,24},{24,0},{32,40},{40,48},{48,56},{56,32},{64,72... | collective-permute-start | bytes 196616 | tf_op jit(solution)/shard_map/ppermute | solution.py:406
  21.4 3.6 %collective-permute-start.1 = (bf16[256,128]{1,0:T(8,128)(2,1)}, bf16[256,128]{1,0:T(8,128)(2,1)S(1)}, u32[]{:S(2)}, u32[]{:S(2)}) collective-permute-start(bf16[256,128]{1,0:T(8,128)(2,1)} %get-tuple-element.83), channel_id=1, source_target_pairs={{0,16},{8,24},{16,0},{24,8},{32,48},{40,56},{48,32},{56,40},{64,80... | collective-permute-start | bytes 196616 | tf_op jit(solution)/shard_map/ppermute | solution.py:406
  25.0 1.0 collective-permute-start.2
  26.0 5.4 %a2.1 = (bf16[1024,512]{1,0:T(8,128)(2,1)}, bf16[1024,512]{1,0:T(8,128)(2,1)}, bf16[16,64,256]{2,1,0:T(8,128)(2,1)}, bf16[16,64,256]{2,1,0:T(8,128)(2,1)}) custom-call(bf16[1024,512]{1,0:T(8,128)(2,1)} %q_ref.3, bf16[1024,512]{1,0:T(8,128)(2,1)} %k_ref.5, f32[1024,512]{1,0:T(8,128)} %get-tuple-element.78.g_ref), custom_call_target="tpu_custom_call" | custom-call | flops 268435456 | bytes 7340032 | tf_op jit(solution)/shard_map/a2/pallas_call | solution.py:427
  31.4 1.0 f1.1
  32.4 3.1 %collective-permute-start.5 = (bf16[256,128]{1,0:T(8,128)(2,1)S(1)}, bf16[256,128]{1,0:T(8,128)(2,1)S(1)}, u32[]{:S(2)}, u32[]{:S(2)}) collective-permute-start(bf16[256,128]{1,0:T(8,128)(2,1)S(1)} %get-tuple-element.98.p0), channel_id=1, source_target_pairs={{0,96},{8,104},{16,112},{24,120},{32,0},{40,8},{48,16},{56,24},{64... | collective-permute-start | bytes 196616 | tf_op jit(solution)/shard_map/ppermute | solution.py:406
  36.1 1.0 collective-permute-start.3
  37.4 3.9 %collective-permute-done.4.p2 = bf16[256,128]{1,0:T(8,128)(2,1)S(1)} collective-permute-done((bf16[256,128]{1,0:T(8,128)(2,1)S(1)}, bf16[256,128]{1,0:T(8,128)(2,1)S(1)}, u32[]{:S(2)}, u32[]{:S(2)}) %collective-permute-start.4) | collective-permute-done | bytes 65568 | tf_op jit(solution)/shard_map/ppermute | solution.py:406
  41.3 0.7 collective-permute-done.3.p1
  42.0 1.0 f2.1
  43.6 1.0 collective-permute-start.6
  44.6 0.7 collective-permute-start.7
  45.3 2.0 %collective-permute-start.8 = (bf16[128,128]{1,0:T(8,128)(2,1)S(1)}, bf16[128,128]{1,0:T(8,128)(2,1)S(1)}, u32[]{:S(2)}, u32[]{:S(2)}) collective-permute-start(bf16[128,128]{1,0:T(8,128)(2,1)S(1)} %get-tuple-element.106), channel_id=1, source_target_pairs={{0,24},{8,0},{16,8},{24,16},{32,56},{40,32},{48,40},{56,48},{64,88... | collective-permute-start | bytes 98312 | tf_op jit(solution)/shard_map/ppermute | solution.py:406
  47.3 6.0 %convolution_convert_fusion.up_ref = bf16[1024,512]{1,0:T(8,128)(2,1)} fusion(bf16[1024,2304]{0,1:T(8,128)(2,1)} %all-gather.2.cloned.1.call-done, bf16[512,2304]{1,0:T(8,128)(2,1)S(1)} %copy-done), kind=kOutput, calls=%fused_computation | convolution fusion | flops 2416443392 | bytes 8126464 | tf_op jit(solution)/shard_map/dot_general | solution.py:509
  53.9 12.5 %b.1 = (bf16[16,4,128,128]{3,2,1,0:T(8,128)(2,1)}, bf16[1024,512]{1,0:T(8,128)(2,1)}, bf16[1024,512]{1,0:T(8,128)(2,1)}, bf16[1024,512]{1,0:T(8,128)(2,1)}, bf16...) custom-call(s32[2]{0:T(128)} %pad_add_fusion.place, ...), custom_call_target="tpu_custom_call" | custom-call | flops 1610612736 | bytes 21758472 | tf_op jit(solution)/shard_map/b/pallas_call | solution.py:427
  66.5 0.8 collective-permute-start.9
  67.3 2.9 %collective-permute-start.10 = (bf16[128,128]{1,0:T(8,128)(2,1)}, bf16[128,128]{1,0:T(8,128)(2,1)S(1)}, u32[]{:S(2)}, u32[]{:S(2)}) collective-permute-start(bf16[128,128]{1,0:T(8,128)(2,1)} %get-tuple-element.123), channel_id=1, source_target_pairs={{0,16},{8,24},{16,0},{24,8},{32,48},{40,56},{48,32},{56,40},{64,80... | collective-permute-start | bytes 98312 | tf_op jit(solution)/shard_map/ppermute | solution.py:406
  70.1 1.5 %collective-permute-start.11 = (bf16[128,128]{1,0:T(8,128)(2,1)}, bf16[128,128]{1,0:T(8,128)(2,1)S(1)}, u32[]{:S(2)}, u32[]{:S(2)}) collective-permute-start(bf16[128,128]{1,0:T(8,128)(2,1)} %get-tuple-element.124), channel_id=1, source_target_pairs={{0,24},{8,0},{16,8},{24,16},{32,56},{40,32},{48,40},{56,48},{64,88... | collective-permute-start | bytes 98312 | tf_op jit(solution)/shard_map/ppermute | solution.py:406
  71.6 4.8 %c0.1.kk_ref = bf16[1024,512]{1,0:T(8,128)(2,1)} custom-call(f32[1024,512]{1,0:T(8,128)} %get-tuple-element.78.g_ref, bf16[1024,512]{1,0:T(8,128)(2,1)} %get-tuple-element.86.qd_ref, bf16[1024,512]{1,0:T(8,128)(2,1)} %get-tuple-element.112.u_ref, bf16[1024,512]{1,0:T(8,128)(2,1)} %get-tuple-element.113.do_ref), custom_call_target="tpu_custom_call" | custom-call | flops 268435456 | bytes 6291456 | tf_op jit(solution)/shard_map/c0/pallas_call | solution.py:427
  76.5 0.7 r1.1
  77.2 2.9 %collective-permute-start.14 = (bf16[128,128]{1,0:T(8,128)(2,1)S(1)}, bf16[128,128]{1,0:T(8,128)(2,1)S(1)}, u32[]{:S(2)}, u32[]{:S(2)}) collective-permute-start(bf16[128,128]{1,0:T(8,128)(2,1)S(1)} %get-tuple-element.134.p0), channel_id=1, source_target_pairs={{0,96},{8,104},{16,112},{24,120},{32,0},{40,8},{48,16},{56,24},{64... | collective-permute-start | bytes 98312 | tf_op jit(solution)/shard_map/ppermute | solution.py:406
  80.1 0.8 collective-permute-start.13
  80.9 0.9 collective-permute-start.12
  81.8 6.4 %c1.1 = (bf16[1024,512]{1,0:T(8,128)(2,1)}, f32[1024,512]{1,0:T(8,128)}) custom-call(bf16[1024,512]{1,0:T(8,128)(2,1)} %q_ref.3, f32[1024,512]{1,0:T(8,128)} %get-tuple-element.78.g_ref, bf16[1024,512]{1,0:T(8,128)(2,1)} %get-tuple-element.79.ki_ref, bf16[1024,512]{1,0:T(8,128)(2,1)} %get-tuple-element.112.u_ref, ...), custom_call_target="tpu_custom_call" | custom-call | flops 536870912 | bytes 11534336 | tf_op jit(solution)/shard_map/c1/pallas_call | solution.py:427
  88.5 1.5 %r2.1 = (bf16[128,128]{1,0:T(8,128)(2,1)S(1)}, bf16[128,128]{1,0:T(8,128)(2,1)S(1)}, bf16[128,128]{1,0:T(8,128)(2,1)S(1)}, bf16[128,128]{1,0:T(8,128)(2,1)S(1)}, bf16[4,128,128]{2,1,0:T(8,128)(2,1)}) custom-call(s32[2]{0:T(128)S(1)} %copy-done.6, bf16[128,128]{1,0:T(8,128)(2,1)S(1)} %get-tuple-element.134.p0, ...), custom_call_target="tpu_custom_call" | custom-call | flops 8388608 | bytes 917512 | tf_op jit(solution)/shard_map/r2/pallas_call | solution.py:427
  91.3 1.3 %collective-permute-start.16 = (bf16[128,128]{1,0:T(8,128)(2,1)S(1)}, bf16[128,128]{1,0:T(8,128)(2,1)S(1)}, u32[]{:S(2)}, u32[]{:S(2)}) collective-permute-start(bf16[128,128]{1,0:T(8,128)(2,1)S(1)} %get-tuple-element.143), channel_id=1, source_target_pairs={{0,16},{8,24},{16,0},{24,8},{32,48},{40,56},{48,32},{56,40},{64,80... | collective-permute-start | bytes 98312 | tf_op jit(solution)/shard_map/ppermute | solution.py:406
  92.6 1.4 %collective-permute-start.17 = (bf16[128,128]{1,0:T(8,128)(2,1)S(1)}, bf16[128,128]{1,0:T(8,128)(2,1)S(1)}, u32[]{:S(2)}, u32[]{:S(2)}) collective-permute-start(bf16[128,128]{1,0:T(8,128)(2,1)S(1)} %get-tuple-element.144), channel_id=1, source_target_pairs={{0,24},{8,0},{16,8},{24,16},{32,56},{40,32},{48,40},{56,48},{64,88... | collective-permute-start | bytes 98312 | tf_op jit(solution)/shard_map/ppermute | solution.py:406
  93.9 1.8 %collective-permute-done.15.g1 = bf16[128,128]{1,0:T(8,128)(2,1)S(1)} collective-permute-done((bf16[128,128]{1,0:T(8,128)(2,1)S(1)}, bf16[128,128]{1,0:T(8,128)(2,1)S(1)}, u32[]{:S(2)}, u32[]{:S(2)}) %collective-permute-start.15) | collective-permute-done | bytes 32800 | tf_op jit(solution)/shard_map/ppermute | solution.py:406
  95.7 1.0 collective-permute-done.16.g2
  97.5 11.6 %c2.1 = (bf16[1024,512]{1,0:T(8,128)(2,1)}, bf16[1024,512]{1,0:T(8,128)(2,1)}, f32[1024,512]{1,0:T(8,128)}, f32[4,1024]{1,0:T(4,128)}) custom-call(s32[2]{0:T(128)} %pad_add_fusion.place, s32[1]{0:T(128)S(6)} %copy.17.resets, bf16[1024,512]{1,0:T(8,128)(2,1)} %k_ref.5, f32[1024,512]{1,0:T(8,128)} %get-tuple-element.78.g_ref, f32[4,1024]{1,0:T(4,128)} %b_ref.3, ...), custom_call_target="tpu_custom_call" | custom-call | flops 1342177280 | bytes 21659660 | tf_op jit(solution)/shard_map/c2/pallas_call | solution.py:427
  (47 shorter events, 5.2 us)
Async XLA Ops:
  7.2 40.1 %copy-start = (bf16[512,2304]{1,0:T(8,128)(2,1)S(1)}, bf16[512,2304]{1,0:T(8,128)(2,1)}, u32[]{:S(2)}) copy-start(bf16[512,2304]{1,0:T(8,128)(2,1)} %param.19) | copy-start | bytes 7077892
  7.2 40.1 %all-gather.2.cloned.1.call-start = ((), (), s32[]{:S(2)}) async-start(), calls=%async_computation | async-start | bytes 5308416 | tf_op jit(solution)/shard_map/all_gather | solution.py:453
  19.3 12.1 %copy-start.1 = (bf16[256,128]{1,0:T(8,128)(2,1)S(1)}, bf16[256,128]{1,0:T(8,128)(2,1)}, u32[]{:S(2)}) copy-start(bf16[256,128]{1,0:T(8,128)(2,1)} %get-tuple-element.92.p0) | copy-start | bytes 196612
  19.3 12.1 %copy-start.5 = (s32[2]{0:T(128)S(1)}, s32[2]{0:T(128)}, u32[]{:S(2)}) copy-start(s32[2]{0:T(128)} %pad_add_fusion.place) | copy-start | bytes 28
  19.3 12.1 %collective-permute-start = (bf16[256,128]{1,0:T(8,128)(2,1)}, bf16[256,128]{1,0:T(8,128)(2,1)S(1)}, u32[]{:S(2)}, u32[]{:S(2)}) collective-permute-start(bf16[256,128]{1,0:T(8,128)(2,1)} %get-tuple-element.82), channel_id=1, source_target_pairs={{0,8},{8,16},{16,24},{24,0},{32,40},{40,48},{48,56},{56,32},{64,72... | collective-permute-start | bytes 196616 | tf_op jit(solution)/shard_map/ppermute | solution.py:406
  21.4 10.0 %collective-permute-start.1 = (bf16[256,128]{1,0:T(8,128)(2,1)}, bf16[256,128]{1,0:T(8,128)(2,1)S(1)}, u32[]{:S(2)}, u32[]{:S(2)}) collective-permute-start(bf16[256,128]{1,0:T(8,128)(2,1)} %get-tuple-element.83), channel_id=1, source_target_pairs={{0,16},{8,24},{16,0},{24,8},{32,48},{40,56},{48,32},{56,40},{64,80... | collective-permute-start | bytes 196616 | tf_op jit(solution)/shard_map/ppermute | solution.py:406
  25.0 6.4 %collective-permute-start.2 = (bf16[256,128]{1,0:T(8,128)(2,1)}, bf16[256,128]{1,0:T(8,128)(2,1)S(1)}, u32[]{:S(2)}, u32[]{:S(2)}) collective-permute-start(bf16[256,128]{1,0:T(8,128)(2,1)} %get-tuple-element.84), channel_id=1, source_target_pairs={{0,24},{8,0},{16,8},{24,16},{32,56},{40,32},{48,40},{56,48},{64,88... | collective-permute-start | bytes 196616 | tf_op jit(solution)/shard_map/ppermute | solution.py:406
  32.4 5.0 %collective-permute-start.5 = (bf16[256,128]{1,0:T(8,128)(2,1)S(1)}, bf16[256,128]{1,0:T(8,128)(2,1)S(1)}, u32[]{:S(2)}, u32[]{:S(2)}) collective-permute-start(bf16[256,128]{1,0:T(8,128)(2,1)S(1)} %get-tuple-element.98.p0), channel_id=1, source_target_pairs={{0,96},{8,104},{16,112},{24,120},{32,0},{40,8},{48,16},{56,24},{64... | collective-permute-start | bytes 196616 | tf_op jit(solution)/shard_map/ppermute | solution.py:406
  35.5 5.8 %collective-permute-start.4 = (bf16[256,128]{1,0:T(8,128)(2,1)S(1)}, bf16[256,128]{1,0:T(8,128)(2,1)S(1)}, u32[]{:S(2)}, u32[]{:S(2)}) collective-permute-start(bf16[256,128]{1,0:T(8,128)(2,1)S(1)} %get-tuple-element.98.p0), channel_id=1, source_target_pairs={{0,64},{8,72},{16,80},{24,88},{32,96},{40,104},{48,112},{56,120},{... | collective-permute-start | bytes 196616 | tf_op jit(solution)/shard_map/ppermute | solution.py:406
  36.1 5.8 %collective-permute-start.3 = (bf16[256,128]{1,0:T(8,128)(2,1)S(1)}, bf16[256,128]{1,0:T(8,128)(2,1)S(1)}, u32[]{:S(2)}, u32[]{:S(2)}) collective-permute-start(bf16[256,128]{1,0:T(8,128)(2,1)S(1)} %get-tuple-element.98.p0), channel_id=1, source_target_pairs={{0,32},{8,40},{16,48},{24,56},{32,64},{40,72},{48,80},{56,88},{64,... | collective-permute-start | bytes 196616 | tf_op jit(solution)/shard_map/ppermute | solution.py:406
  43.0 0.6 copy-start.2
  43.6 9.7 %collective-permute-start.6 = (bf16[128,128]{1,0:T(8,128)(2,1)S(1)}, bf16[128,128]{1,0:T(8,128)(2,1)S(1)}, u32[]{:S(2)}, u32[]{:S(2)}) collective-permute-start(bf16[128,128]{1,0:T(8,128)(2,1)S(1)} %get-tuple-element.104), channel_id=1, source_target_pairs={{0,8},{8,16},{16,24},{24,0},{32,40},{40,48},{48,56},{56,32},{64,72... | collective-permute-start | bytes 98312 | tf_op jit(solution)/shard_map/ppermute | solution.py:406
  44.6 8.7 %collective-permute-start.7 = (bf16[128,128]{1,0:T(8,128)(2,1)S(1)}, bf16[128,128]{1,0:T(8,128)(2,1)S(1)}, u32[]{:S(2)}, u32[]{:S(2)}) collective-permute-start(bf16[128,128]{1,0:T(8,128)(2,1)S(1)} %get-tuple-element.105), channel_id=1, source_target_pairs={{0,16},{8,24},{16,0},{24,8},{32,48},{40,56},{48,32},{56,40},{64,80... | collective-permute-start | bytes 98312 | tf_op jit(solution)/shard_map/ppermute | solution.py:406
  45.3 8.0 %collective-permute-start.8 = (bf16[128,128]{1,0:T(8,128)(2,1)S(1)}, bf16[128,128]{1,0:T(8,128)(2,1)S(1)}, u32[]{:S(2)}, u32[]{:S(2)}) collective-permute-start(bf16[128,128]{1,0:T(8,128)(2,1)S(1)} %get-tuple-element.106), channel_id=1, source_target_pairs={{0,24},{8,0},{16,8},{24,16},{32,56},{40,32},{48,40},{56,48},{64,88... | collective-permute-start | bytes 98312 | tf_op jit(solution)/shard_map/ppermute | solution.py:406
  53.3 0.6 copy-start.7
  53.3 0.6 copy-start.9
  53.3 0.6 copy-start.11
  66.5 10.0 %collective-permute-start.9 = (bf16[128,128]{1,0:T(8,128)(2,1)}, bf16[128,128]{1,0:T(8,128)(2,1)S(1)}, u32[]{:S(2)}, u32[]{:S(2)}) collective-permute-start(bf16[128,128]{1,0:T(8,128)(2,1)} %get-tuple-element.122), channel_id=1, source_target_pairs={{0,8},{8,16},{16,24},{24,0},{32,40},{40,48},{48,56},{56,32},{64,72... | collective-permute-start | bytes 98312 | tf_op jit(solution)/shard_map/ppermute | solution.py:406
  67.3 9.2 %collective-permute-start.10 = (bf16[128,128]{1,0:T(8,128)(2,1)}, bf16[128,128]{1,0:T(8,128)(2,1)S(1)}, u32[]{:S(2)}, u32[]{:S(2)}) collective-permute-start(bf16[128,128]{1,0:T(8,128)(2,1)} %get-tuple-element.123), channel_id=1, source_target_pairs={{0,16},{8,24},{16,0},{24,8},{32,48},{40,56},{48,32},{56,40},{64,80... | collective-permute-start | bytes 98312 | tf_op jit(solution)/shard_map/ppermute | solution.py:406
  70.1 6.3 %collective-permute-start.11 = (bf16[128,128]{1,0:T(8,128)(2,1)}, bf16[128,128]{1,0:T(8,128)(2,1)S(1)}, u32[]{:S(2)}, u32[]{:S(2)}) collective-permute-start(bf16[128,128]{1,0:T(8,128)(2,1)} %get-tuple-element.124), channel_id=1, source_target_pairs={{0,24},{8,0},{16,8},{24,16},{32,56},{40,32},{48,40},{56,48},{64,88... | collective-permute-start | bytes 98312 | tf_op jit(solution)/shard_map/ppermute | solution.py:406
  71.6 4.8 %copy-start.4 = (bf16[128,128]{1,0:T(8,128)(2,1)S(1)}, bf16[128,128]{1,0:T(8,128)(2,1)}, u32[]{:S(2)}) copy-start(bf16[128,128]{1,0:T(8,128)(2,1)} %get-tuple-element.125.p0) | copy-start | bytes 98308
  71.6 4.8 %copy-start.6 = (s32[2]{0:T(128)S(1)}, s32[2]{0:T(128)}, u32[]{:S(2)}) copy-start(s32[2]{0:T(128)} %pad_add_fusion.place) | copy-start | bytes 28
  77.2 11.3 %collective-permute-start.14 = (bf16[128,128]{1,0:T(8,128)(2,1)S(1)}, bf16[128,128]{1,0:T(8,128)(2,1)S(1)}, u32[]{:S(2)}, u32[]{:S(2)}) collective-permute-start(bf16[128,128]{1,0:T(8,128)(2,1)S(1)} %get-tuple-element.134.p0), channel_id=1, source_target_pairs={{0,96},{8,104},{16,112},{24,120},{32,0},{40,8},{48,16},{56,24},{64... | collective-permute-start | bytes 98312 | tf_op jit(solution)/shard_map/ppermute | solution.py:406
  80.1 8.4 %collective-permute-start.13 = (bf16[128,128]{1,0:T(8,128)(2,1)S(1)}, bf16[128,128]{1,0:T(8,128)(2,1)S(1)}, u32[]{:S(2)}, u32[]{:S(2)}) collective-permute-start(bf16[128,128]{1,0:T(8,128)(2,1)S(1)} %get-tuple-element.134.p0), channel_id=1, source_target_pairs={{0,64},{8,72},{16,80},{24,88},{32,96},{40,104},{48,112},{56,120},{... | collective-permute-start | bytes 98312 | tf_op jit(solution)/shard_map/ppermute | solution.py:406
  80.9 7.6 %collective-permute-start.12 = (bf16[128,128]{1,0:T(8,128)(2,1)S(1)}, bf16[128,128]{1,0:T(8,128)(2,1)S(1)}, u32[]{:S(2)}, u32[]{:S(2)}) collective-permute-start(bf16[128,128]{1,0:T(8,128)(2,1)S(1)} %get-tuple-element.134.p0), channel_id=1, source_target_pairs={{0,32},{8,40},{16,48},{24,56},{32,64},{40,72},{48,80},{56,88},{64,... | collective-permute-start | bytes 98312 | tf_op jit(solution)/shard_map/ppermute | solution.py:406
  90.0 0.6 copy-start.3
  90.6 5.1 %collective-permute-start.15 = (bf16[128,128]{1,0:T(8,128)(2,1)S(1)}, bf16[128,128]{1,0:T(8,128)(2,1)S(1)}, u32[]{:S(2)}, u32[]{:S(2)}) collective-permute-start(bf16[128,128]{1,0:T(8,128)(2,1)S(1)} %get-tuple-element.142), channel_id=1, source_target_pairs={{0,8},{8,16},{16,24},{24,0},{32,40},{40,48},{48,56},{56,32},{64,72... | collective-permute-start | bytes 98312 | tf_op jit(solution)/shard_map/ppermute | solution.py:406
  91.3 5.4 %collective-permute-start.16 = (bf16[128,128]{1,0:T(8,128)(2,1)S(1)}, bf16[128,128]{1,0:T(8,128)(2,1)S(1)}, u32[]{:S(2)}, u32[]{:S(2)}) collective-permute-start(bf16[128,128]{1,0:T(8,128)(2,1)S(1)} %get-tuple-element.143), channel_id=1, source_target_pairs={{0,16},{8,24},{16,0},{24,8},{32,48},{40,56},{48,32},{56,40},{64,80... | collective-permute-start | bytes 98312 | tf_op jit(solution)/shard_map/ppermute | solution.py:406
  92.6 4.4 %collective-permute-start.17 = (bf16[128,128]{1,0:T(8,128)(2,1)S(1)}, bf16[128,128]{1,0:T(8,128)(2,1)S(1)}, u32[]{:S(2)}, u32[]{:S(2)}) collective-permute-start(bf16[128,128]{1,0:T(8,128)(2,1)S(1)} %get-tuple-element.144), channel_id=1, source_target_pairs={{0,24},{8,0},{16,8},{24,16},{32,56},{40,32},{48,40},{56,48},{64,88... | collective-permute-start | bytes 98312 | tf_op jit(solution)/shard_map/ppermute | solution.py:406
  95.7 1.2 %copy-start.8 = (bf16[128,128]{1,0:T(8,128)(2,1)}, bf16[128,128]{1,0:T(8,128)(2,1)S(1)}, u32[]{:S(2)}) copy-start(bf16[128,128]{1,0:T(8,128)(2,1)S(1)} %collective-permute-done.15.g1) | copy-start | bytes 98308
  96.7 0.6 copy-start.10
  96.9 0.6 copy-start.12
Sparse Core Ops, SparseCore 0:
  9.7 36.7 all-gather.1

commit v4 on v3

--- a/solution.py
+++ b/solution.py
@@ -12,7 +12,7 @@
 GROUP = 64
 EPS = 1e-6
 SCALE = DK**-0.5
-STEP = 4
+STEP = dict(a1=4, a2=8, b=4, c0=8, c1=8, c2=4)
 UNITS = dict(a1=16, a2=16, b=16, c0=16, c1=16, c2=16)
 RING = 4
 
@@ -61,8 +61,9 @@
     return slice(64 * h, 64 * h + 64)
 
 
-def units(heads, size):
-    pairs = [(c, h) for c in range(STEP) for h in range(heads)]
+def units(heads, name):
+    size = UNITS[name]
+    pairs = [(c, h) for c in range(STEP[name]) for h in range(heads)]
     return [pairs[i : i + size] for i in range(0, len(pairs), size)]
 
 
@@ -78,6 +79,20 @@
 def collect(me, array, arrived):
     for shift, other in enumerate(arrived):
         array[lax.rem(me + RING - shift, RING)] = other[...].astype(array.dtype)
+
+
+def diag(x, y):
+    zx = jnp.zeros((x.shape[0], y.shape[1]), x.dtype)
+    zy = jnp.zeros((y.shape[0], x.shape[1]), x.dtype)
+    return jnp.concatenate([jnp.concatenate([x, zx], axis=1), jnp.concatenate([zy, y], axis=1)], axis=0)
+
+
+def lanes(x, y):
+    return jnp.concatenate([x, y], axis=1)
+
+
+def split(pairs):
+    return [part for p in pairs for part in (p[:, 0:128], p[:, 128:256])]
 
 
 def kernel_a1(
@@ -94,11 +109,11 @@
             state[h] = (row == col + 128).astype(f32)
 
     weights = twice(False)
-    gammas = [sum_rows(weights, d_ref[half(c), :]) for c in range(STEP)]
-    for c in range(STEP):
+    gammas = [sum_rows(weights, d_ref[half(c), :]) for c in range(STEP["a1"])]
+    for c in range(STEP["a1"]):
         g_ref[half(c), :] = gammas[c]
     rs = [state[h] for h in range(heads)]
-    for group in units(heads, UNITS["a1"]):
+    for group in units(heads, "a1"):
         gs = [gammas[c][:, cols(h)] for c, h in group]
         ks = [k_ref[half(c), cols(h)].astype(f32) for c, h in group]
         kus = each(lambda k: k * inverse_norm(k), ks)
@@ -118,7 +133,7 @@
             y_ref[half(c), cols(h)] = xy[:, 128:]
             n_ref[c, h] = n
         for (c, h), bn, n, g in zip(group, bns, ns, gs):
-            keep = (step * STEP + c != resets[0]).astype(f32)
+            keep = (step * STEP["a1"] + c != resets[0]).astype(f32)
             r = rs[h] * keep
             rb = r.astype(bf16)
             pre_ref[c, h] = rb
@@ -135,7 +150,7 @@
 def kernel_a2(heads, q_ref, k_ref, g_ref, qd_ref, ki_ref, a_ref, at_ref):
     lower = triangle(False, f32)
     upper = triangle(True, f32)
-    for group in units(heads, UNITS["a2"]):
+    for group in units(heads, "a2"):
         gs = [g_ref[half(c), cols(h)] for c, h in group]
         qs = [q_ref[half(c), cols(h)].astype(f32) for c, h in group]
         ks = [k_ref[half(c), cols(h)].astype(f32) for c, h in group]
@@ -151,7 +166,7 @@
 
 
 def kernel_b(
-    heads, place, v_ref, kd_ref, qd_ref, y_ref, wb_ref, a_ref, at_ref, pre_ref, gate_ref, up_ref, gain_ref,
+    heads, place, v_ref, kd_ref, qd_ref, y_ref, wb_ref, a_ref, at_ref, pre_ref, gate_ref, x_ref, p_ref, gain_ref,
     s0, s1, s2, s3, e_ref, vp_ref, u_ref, do_ref, du_ref, dt_ref, dg_ref, r0, r1, r2, r3, total, s_ref,
 ):
     step = pl.program_id(0)
@@ -163,24 +178,36 @@
 
     gain = gain_ref[...]
     sums = [total[h] for h in range(heads)]
-    for group in units(heads, UNITS["b"]):
-        es = [
-            (pre_ref[c, h, 0:128].astype(f32) + nn(s_ref[h], pre_ref[c, h, 128:256])).astype(bf16)
-            for c, h in group
-        ]
-        boths = [
-            nt(jnp.concatenate([kd_ref[half(c), cols(h)], qd_ref[half(c), cols(h)]], axis=0), e)
-            for e, (c, h) in zip(es, group)
-        ]
+    up = nn(p_ref[...], x_ref[...]).astype(bf16).T
+    for group in units(heads, "b"):
+        es = split([
+            nn(lanes(s_ref[h], s_ref[h + 1]), diag(pre_ref[c, h, 128:256], pre_ref[c, h + 1, 128:256]))
+            for c, h in group[::2]
+        ])
+        es = [(pre_ref[c, h, 0:128].astype(f32) + e).astype(bf16) for e, (c, h) in zip(es, group)]
+        boths = split([
+            nt(
+                jnp.concatenate([kd_ref[half(c), 128 * h : 128 * h + 256], qd_ref[half(c), 128 * h : 128 * h + 256]], axis=0),
+                diag(es[i], es[i + 1]),
+            )
+            for i, (c, h) in list(enumerate(group))[::2]
+        ])
         vps = [
             (v_ref[half(c), cols(h)].astype(f32) - both[0:64]).astype(bf16)
             for both, (c, h) in zip(boths, group)
         ]
-        us = [nn(wb_ref[c, :, half(h)], vp).astype(bf16) for vp, (c, h) in zip(vps, group)]
-        os = [both[64:128] + nn(a_ref[c, :, half(h)], u) for both, u, (c, h) in zip(boths, us, group)]
+        us = split([
+            nn(wb_ref[c, :, 64 * h : 64 * h + 128], diag(vps[i], vps[i + 1])).astype(bf16)
+            for i, (c, h) in list(enumerate(group))[::2]
+        ])
+        os = split([
+            nn(a_ref[c, :, 64 * h : 64 * h + 128], diag(us[i], us[i + 1]))
+            for i, (c, h) in list(enumerate(group))[::2]
+        ])
+        os = each(lambda both, o: both[64:128] + o, boths, os)
         rmss = each(lambda o: lax.rsqrt(jnp.mean(o * o, axis=-1, keepdims=True) + EPS), os)
         sigs = [jax.nn.sigmoid(gate_ref[half(c), cols(h)].astype(f32)) for c, h in group]
-        ws = [up_ref[half(c), cols(h)].astype(f32) * gain * sig for sig, (c, h) in zip(sigs, group)]
+        ws = [up[half(c), cols(h)].astype(f32) * gain * sig for sig, (c, h) in zip(sigs, group)]
         ons = each(lambda o, rms: o * rms, os, rmss)
         wons = each(lambda w, on: w * on, ws, ons)
         dgs = each(lambda won, sig: (won * (1.0 - sig)).astype(bf16), wons, sigs)
@@ -188,16 +215,24 @@
             lambda rms, w, on, won: (rms * (w - on * jnp.mean(won, axis=-1, keepdims=True))).astype(bf16),
             rmss, ws, ons, wons,
         )
-        dus = [nn(at_ref[c, :, half(h)], do).astype(bf16) for do, (c, h) in zip(dos, group)]
-        dts = [
+        dus = split([
+            nn(at_ref[c, :, 64 * h : 64 * h + 128], diag(dos[i], dos[i + 1])).astype(bf16)
+            for i, (c, h) in list(enumerate(group))[::2]
+        ])
+        dts = split([
             tn(
-                jnp.concatenate([do, du], axis=0),
-                jnp.concatenate([qd_ref[half(c), cols(h)], -y_ref[half(c), cols(h)]], axis=0),
+                jnp.concatenate([dos[i], dus[i], dos[i + 1], dus[i + 1]], axis=0),
+                diag(
+                    jnp.concatenate([qd_ref[half(c), cols(h)], -y_ref[half(c), cols(h)]], axis=0),
+                    jnp.concatenate([qd_ref[half(c), cols(h + 1)], -y_ref[half(c), cols(h + 1)]], axis=0),
+                ),
             ).astype(bf16)
-            for do, du, (c, h) in zip(dos, dus, group)
-        ]
-        for (c, h), dt in zip(group, dts):
-            sums[h] = sums[h] + nt(dt, pre_ref[c, h, 128:256])
+            for i, (c, h) in list(enumerate(group))[::2]
+        ])
+        for h in range(heads):
+            mine = [(dt, c) for dt, (c, x) in zip(dts, group) if x == h]
+            for (d0, c0), (d1, c1) in zip(mine[::2], mine[1::2]):
+                sums[h] = sums[h] + nt(lanes(d0, d1), lanes(pre_ref[c0, h, 128:256], pre_ref[c1, h, 128:256]))
         for (c, h), e, vp, u, do, du, dt, dg in zip(group, es, vps, us, dos, dus, dts, dgs):
             e_ref[c, h] = e
             vp_ref[half(c), cols(h)] = vp
@@ -216,7 +251,7 @@
 
 def kernel_c1(heads, q_ref, g_ref, ki_ref, u_ref, do_ref, e_ref, dq_ref, pq_ref):
     lower = triangle(False, f32)
-    for group in units(heads, UNITS["c1"]):
+    for group in units(heads, "c1"):
         us = [u_ref[half(c), cols(h)] for c, h in group]
         dos = [do_ref[half(c), cols(h)] for c, h in group]
         das = each(lambda do, u: (nt(do, u) * lower).astype(bf16), dos, us)
@@ -241,7 +276,7 @@
 
 def kernel_c0(heads, g_ref, qd_ref, u_ref, do_ref, kk_ref):
     upper = triangle(True, f32)
-    for group in units(heads, UNITS["c0"]):
+    for group in units(heads, "c0"):
         us = [u_ref[half(c), cols(h)] for c, h in group]
         dos = [do_ref[half(c), cols(h)] for c, h in group]
         dats = each(lambda do, u: (nt(u, do) * upper).astype(bf16), dos, us)
@@ -269,8 +304,8 @@
     grads = {}
     gbs = {}
     now = [state[h] for h in range(heads)]
-    for c in reversed(range(STEP)):
-        keep = (turn * STEP + c != resets[0]).astype(f32)
+    for c in reversed(range(STEP["c2"])):
+        keep = (turn * STEP["c2"] + c != resets[0]).astype(f32)
         for h in range(heads):
             grads[c, h] = now[h]
             gbs[c, h] = now[h].astype(bf16)
@@ -279,7 +314,7 @@
             now[h] = keep * (dt_ref[c, h].astype(f32) + lam * now[h] - nt(gbs[c, h], n_ref[c, h]))
     for h in range(heads):
         state[h] = now[h]
-    for group in reversed(units(heads, UNITS["c2"])):
+    for group in reversed(units(heads, "c2")):
         gb = [gbs[p] for p in group]
         dus = [
             (du_ref[half(c), cols(h)].astype(f32) + nt(kt_ref[half(c), cols(h)], x)).astype(bf16)
@@ -411,8 +446,7 @@
     return [arrays[0]] + [permute(arrays[distance], distance, outer) for distance in (1, 2, 3)]
 
 
-BIG = 54 * 2**20
-SMALL = 8 * 2**20
+LIMIT = dict(a1=54, a2=54, b=53, c0=54, c1=54, c2=53)
 SMEM = pl.BlockSpec(memory_space=pltpu.SMEM)
 VMEM = pl.BlockSpec(memory_space=pltpu.VMEM)
 
@@ -432,7 +466,7 @@
         out_specs=out_specs,
         scratch_shapes=scratch,
         compiler_params=pltpu.CompilerParams(
-            vmem_limit_bytes=BIG if grid else SMALL,
+            vmem_limit_bytes=LIMIT.get(name, 8) * 2**20,
             **({"dimension_semantics": ("arbitrary",)} if grid else {}),
         ),
         cost_estimate=pl.CostEstimate(flops=flops, bytes_accessed=total, transcendentals=0),
@@ -446,26 +480,30 @@
     tokens = queries.shape[0]
     heads = beta.shape[0]
     count = tokens // GROUP
-    steps = count // STEP
     width = heads * 128
     index = lax.axis_index("seq")
     place = jnp.stack([index // RING, index % RING]).astype(jnp.int32)
-    gathered = lax.all_gather(grad_out, "head", axis=1, tiled=True)
-
-    def specs(back):
+    gathered = lax.all_gather(grad_out.T, "head", axis=0, tiled=True)
+    model = out_proj.shape[1]
+
+    def specs(name, back=False):
+        step = STEP[name]
+        steps = count // step
         at = (lambda i: steps - 1 - i) if back else (lambda i: i)
         return dict(
-            tok=pl.BlockSpec((STEP * GROUP, width), lambda i: (at(i), 0)),
-            beta=pl.BlockSpec((heads, STEP * GROUP), lambda i: (0, at(i))),
-            wy=pl.BlockSpec((STEP, GROUP, heads * GROUP), lambda i: (at(i), 0, 0)),
-            state=pl.BlockSpec((STEP, heads, 128, 128), lambda i: (at(i), 0, 0, 0)),
-            pair=pl.BlockSpec((STEP, heads, 256, 128), lambda i: (at(i), 0, 0, 0)),
+            grid=(steps,),
+            tok=pl.BlockSpec((step * GROUP, width), lambda i: (at(i), 0)),
+            beta=pl.BlockSpec((heads, step * GROUP), lambda i: (0, at(i))),
+            wy=pl.BlockSpec((step, GROUP, heads * GROUP), lambda i: (at(i), 0, 0)),
+            state=pl.BlockSpec((step, heads, 128, 128), lambda i: (at(i), 0, 0, 0)),
+            pair=pl.BlockSpec((step, heads, 256, 128), lambda i: (at(i), 0, 0, 0)),
             whole=pl.BlockSpec((128, 128), lambda i: (0, 0)),
             whole2=pl.BlockSpec((256, 128), lambda i: (0, 0)),
+            parts=pl.BlockSpec((model, step * GROUP), lambda i: (0, at(i))),
+            proj=pl.BlockSpec((width, model), lambda i: (0, 0)),
             gain=pl.BlockSpec((1, 128), lambda i: (0, 0)),
         )
 
-    s = specs(False)
     tok_b = shape((tokens, width), bf16)
     tok_f = shape((tokens, width), f32)
     small_b = shape((count, GROUP, heads * GROUP), bf16)
@@ -477,21 +515,23 @@
     twos_b = shape((RING, 256, 128), bf16)
     unit = count * heads * 2 * 64 * 128 * 128
 
+    s = specs("a1")
     gamma, wb, kd, kt, y, n, pre, *mb = call(
         kernel_a1, "a1", heads,
         [SMEM, SMEM, s["tok"], s["tok"], s["tok"], s["beta"], s["wy"]],
         [s["tok"], s["wy"], s["tok"], s["tok"], s["tok"], s["state"], s["pair"]] + [s["whole2"]] * 4,
         [tok_f, small_b, tok_b, tok_b, tok_b, state_b, pair_b] + [two_b] * 4,
-        [pltpu.VMEM((heads, 256, 128), f32)], (steps,), 8 * unit,
+        [pltpu.VMEM((heads, 256, 128), f32)], s["grid"], 8 * unit,
         place, resets, keys, values, decay, beta, wy_inverse,
     )
     zs = three(mb, False)
+    s = specs("a2")
     qd, ki, a, at = call(
         kernel_a2, "a2", heads,
         [s["tok"], s["tok"], s["tok"]],
         [s["tok"], s["tok"], s["wy"], s["wy"]],
         [tok_b, tok_b, small_b, small_b],
-        [], (steps,), 2 * unit, queries, keys, gamma,
+        [], s["grid"], 2 * unit, queries, keys, gamma,
     )
     zs, qd = lax.optimization_barrier((zs, qd))
     group, before, zslots = call(
@@ -506,21 +546,19 @@
         [pltpu.VMEM((RING, 128, 128), bf16)], (), unit // 8, place, *ys, before,
     )
     state_in = three(states, False)
-    upstream = lax.dot_general(
-        gathered, out_proj, (((1,), (1,)), ((), ())), preferred_element_type=f32
-    ).astype(bf16)
-    state_in, upstream = lax.optimization_barrier((state_in, upstream))
+    s = specs("b")
     e, vp, u, do, du, dt, dgate, *r = call(
         kernel_b, "b", heads,
-        [SMEM, s["tok"], s["tok"], s["tok"], s["tok"], s["wy"], s["wy"], s["wy"], s["pair"], s["tok"], s["tok"], s["gain"]] + [s["whole"]] * 4,
+        [SMEM, s["tok"], s["tok"], s["tok"], s["tok"], s["wy"], s["wy"], s["wy"], s["pair"], s["tok"], s["parts"], s["proj"], s["gain"]] + [s["whole"]] * 4,
         [s["state"], s["tok"], s["tok"], s["tok"], s["tok"], s["state"], s["tok"]] + [s["whole"]] * 4,
         [state_b, tok_b, tok_b, tok_b, tok_b, state_b, tok_b] + [one_b] * 4,
-        [pltpu.VMEM((heads, 128, 128), f32), pltpu.VMEM((heads, 128, 128), bf16)], (steps,), 12 * unit,
-        place, values, kd, qd, y, wb, a, at, pre, out_gate, upstream, norm_gain.reshape(1, 128), *state_in,
+        [pltpu.VMEM((heads, 128, 128), f32), pltpu.VMEM((heads, 128, 128), bf16)], s["grid"], 12 * unit,
+        place, values, kd, qd, y, wb, a, at, pre, out_gate, gathered, out_proj, norm_gain.reshape(1, 128), *state_in,
     )
     zr = three(r, False)
+    s = specs("c0")
     (kk,) = call(
-        kernel_c0, "c0", heads, [s["tok"]] * 4, [s["tok"]], [tok_b], [], (steps,), 2 * unit, gamma, qd, u, do,
+        kernel_c0, "c0", heads, [s["tok"]] * 4, [s["tok"]], [tok_b], [], s["grid"], 2 * unit, gamma, qd, u, do,
     )
     zr, kk = lax.optimization_barrier((zr, kk))
     rgroup, rslots = call(
@@ -529,25 +567,27 @@
     )
     yr = three(rgroup, True)
     (later,) = call(kernel_r3, "r3", heads, [VMEM] * 2, [VMEM], [ones_b], [], (), unit // 16, rslots, zslots)
+    yr, later = lax.optimization_barrier((yr, later))
+    *grads, _ = call(
+        kernel_r2, "r2", heads, [SMEM] + [VMEM] * 7, [VMEM] * 5, [one_b] * 4 + [ones_b],
+        [pltpu.VMEM((RING, 128, 128), bf16)], (), unit // 16, place, *yr, later, later_m, yslots,
+    )
+    grad_in = three(grads, False)
+    s = specs("c1")
     dq, pq = call(
         kernel_c1, "c1", heads,
         [s["tok"]] * 5 + [s["state"]],
         [s["tok"], s["tok"]], [tok_b, tok_f],
-        [], (steps,), 4 * unit, queries, gamma, ki, u, do, e,
-    )
-    yr, pq, later = lax.optimization_barrier((yr, pq, later))
-    *grads, _ = call(
-        kernel_r2, "r2", heads, [SMEM] + [VMEM] * 7, [VMEM] * 5, [one_b] * 4 + [ones_b],
-        [pltpu.VMEM((RING, 128, 128), bf16)], (), unit // 16, place, *yr, later, later_m, yslots,
-    )
-    grad_in = three(grads, False)
-    t = specs(True)
+        [], s["grid"], 4 * unit, queries, gamma, ki, u, do, e,
+    )
+    grad_in, pq = lax.optimization_barrier((grad_in, pq))
+    s = specs("c2", True)
     dk, dv, dd, db = call(
         kernel_c2, "c2", heads,
-        [SMEM, SMEM, t["tok"], t["tok"], t["beta"], t["wy"], t["tok"], t["state"], t["state"], t["tok"], t["tok"], t["tok"], t["state"], t["tok"], t["tok"]] + [t["whole"]] * 4,
-        [t["tok"], t["tok"], t["tok"], t["beta"]],
+        [SMEM, SMEM, s["tok"], s["tok"], s["beta"], s["wy"], s["tok"], s["state"], s["state"], s["tok"], s["tok"], s["tok"], s["state"], s["tok"], s["tok"]] + [s["whole"]] * 4,
+        [s["tok"], s["tok"], s["tok"], s["beta"]],
         [tok_b, tok_b, tok_f, shape((heads, tokens), f32)],
-        [pltpu.VMEM((heads, 128, 128), f32)], (steps,), 10 * unit,
+        [pltpu.VMEM((heads, 128, 128), f32)], s["grid"], 10 * unit,
         place, resets, keys, gamma, beta, wb, kt, n, e, vp, u, du, dt, pq, kk, *grad_in,
     )
     return dq, dk, dv, dd, db, dgate

time: 117 us -> 110 us (0.940)
  matrix products: 5.99 us -> 0 us
  waiting for transfers between devices: 8.29 us -> 11.8 us
  local copies, waits for them, and re-layouts: 2.43 us -> 0.02 us
  starting transfers between devices: 28.1 us -> 26.7 us
    dot_general x1 -> x0, matrix products: 5.99 us -> none  [per_device(): lax.dot_general(gathered, out_proj, (((1,), (1,)), ((), ())), preferred_e...]
    ppermute x18, waiting for transfers between devices: 7.61 us -> 11.1 us  [permute(): return lax.ppermute(x, 'seq', pairs)]
    unnamed x26 -> x10, local copies, waits for them, and re-layouts: 2.43 us -> 0.02 us
    ppermute x18, starting transfers between devices: 28.1 us -> 26.6 us  [permute(): return lax.ppermute(x, 'seq', pairs)]
  transfers between devices with their start and end apart: 19 -> 19, of which waited for: 5 -> 7; matrix products, arithmetic and copies ran while one was open for 6% -> 1% of each run, Pallas kernels for 25% -> 25%
where the time goes in v4:
time: 110 us
  Pallas kernels  56 us (51%)
  starting transfers between devices  26.7 us (24%)
  between operations  14.8 us (13%)
  waiting for transfers between devices  11.8 us (11%)
    pallas_call x12, Pallas kernels, call(): pl.pallas_call(functools.partial(body, heads), out_shape=out_shape, grid=...  56 us
    ppermute x18, starting transfers between devices, permute(): return lax.ppermute(x, 'seq', pairs)  26.6 us
    ppermute x18, waiting for transfers between devices, permute(): return lax.ppermute(x, 'seq', pairs)  11.1 us
  transfers between devices with their start and end apart: 19, of which 7 were waited for; matrix products, arithmetic and copies ran while one was open for 1% of the time, Pallas kernels for 25%

profile of v4, /device:TPU:0, one launch (start us, length us, event | category | flops | bytes accessed | tf_op | source)
XLA Modules:
  0.0 109.9 jit_solution(15825908074092712042)
XLA Ops:
  7.2 0.7 all-gather.2.cloned.1.call-update
  9.2 10.2 %a1.1 = (f32[1024,512]{1,0:T(8,128)}, bf16[16,64,256]{2,1,0:T(8,128)(2,1)}, bf16[1024,512]{1,0:T(8,128)(2,1)}, bf16[1024,512]{1,0:T(8,128)(2,1)}, bf16[1024,512]...) custom-call(s32[2]{0:T(128)} %pad_add_fusion.place, ...), custom_call_target="tpu_custom_call" | custom-call | flops 1073741824 | bytes 17580044 | tf_op jit(solution)/shard_map/a1/pallas_call | solution.py:461
  19.4 2.1 %collective-permute-start = (bf16[256,128]{1,0:T(8,128)(2,1)}, bf16[256,128]{1,0:T(8,128)(2,1)S(1)}, u32[]{:S(2)}, u32[]{:S(2)}) collective-permute-start(bf16[256,128]{1,0:T(8,128)(2,1)} %get-tuple-element.81), channel_id=1, source_target_pairs={{0,8},{8,16},{16,24},{24,0},{32,40},{40,48},{48,56},{56,32},{64,72... | collective-permute-start | bytes 196616 | tf_op jit(solution)/shard_map/ppermute | solution.py:441
  21.5 3.6 %collective-permute-start.1 = (bf16[256,128]{1,0:T(8,128)(2,1)}, bf16[256,128]{1,0:T(8,128)(2,1)S(1)}, u32[]{:S(2)}, u32[]{:S(2)}) collective-permute-start(bf16[256,128]{1,0:T(8,128)(2,1)} %get-tuple-element.82), channel_id=1, source_target_pairs={{0,16},{8,24},{16,0},{24,8},{32,48},{40,56},{48,32},{56,40},{64,80... | collective-permute-start | bytes 196616 | tf_op jit(solution)/shard_map/ppermute | solution.py:441
  25.0 1.0 collective-permute-start.2
  26.1 5.2 %a2.1 = (bf16[1024,512]{1,0:T(8,128)(2,1)}, bf16[1024,512]{1,0:T(8,128)(2,1)}, bf16[16,64,256]{2,1,0:T(8,128)(2,1)}, bf16[16,64,256]{2,1,0:T(8,128)(2,1)}) custom-call(bf16[1024,512]{1,0:T(8,128)(2,1)} %q_ref.3, bf16[1024,512]{1,0:T(8,128)(2,1)} %k_ref.5, f32[1024,512]{1,0:T(8,128)} %get-tuple-element.77.g_ref), custom_call_target="tpu_custom_call" | custom-call | flops 268435456 | bytes 7340032 | tf_op jit(solution)/shard_map/a2/pallas_call | solution.py:461
  31.4 1.0 f1.1
  32.3 3.1 %collective-permute-start.5 = (bf16[256,128]{1,0:T(8,128)(2,1)S(1)}, bf16[256,128]{1,0:T(8,128)(2,1)S(1)}, u32[]{:S(2)}, u32[]{:S(2)}) collective-permute-start(bf16[256,128]{1,0:T(8,128)(2,1)S(1)} %get-tuple-element.97.p0), channel_id=1, source_target_pairs={{0,96},{8,104},{16,112},{24,120},{32,0},{40,8},{48,16},{56,24},{64... | collective-permute-start | bytes 196616 | tf_op jit(solution)/shard_map/ppermute | solution.py:441
  36.1 1.0 collective-permute-start.3
  37.3 3.9 %collective-permute-done.4.p2 = bf16[256,128]{1,0:T(8,128)(2,1)S(1)} collective-permute-done((bf16[256,128]{1,0:T(8,128)(2,1)S(1)}, bf16[256,128]{1,0:T(8,128)(2,1)S(1)}, u32[]{:S(2)}, u32[]{:S(2)}) %collective-permute-start.4) | collective-permute-done | bytes 65568 | tf_op jit(solution)/shard_map/ppermute | solution.py:441
  41.9 1.0 f2.1
  42.9 1.1 collective-permute-start.6
  44.0 0.8 collective-permute-start.7
  44.8 1.9 %collective-permute-start.8 = (bf16[128,128]{1,0:T(8,128)(2,1)S(1)}, bf16[128,128]{1,0:T(8,128)(2,1)S(1)}, u32[]{:S(2)}, u32[]{:S(2)}) collective-permute-start(bf16[128,128]{1,0:T(8,128)(2,1)S(1)} %get-tuple-element.105), channel_id=1, source_target_pairs={{0,24},{8,0},{16,8},{24,16},{32,56},{40,32},{48,40},{56,48},{64,88... | collective-permute-start | bytes 98312 | tf_op jit(solution)/shard_map/ppermute | solution.py:441
  46.7 1.3 %collective-permute-done.6.s1 = bf16[128,128]{1,0:T(8,128)(2,1)S(1)} collective-permute-done((bf16[128,128]{1,0:T(8,128)(2,1)S(1)}, bf16[128,128]{1,0:T(8,128)(2,1)S(1)}, u32[]{:S(2)}, u32[]{:S(2)}) %collective-permute-start.6) | collective-permute-done | bytes 32800 | tf_op jit(solution)/shard_map/ppermute | solution.py:441
  48.1 1.3 %collective-permute-done.7.s2 = bf16[128,128]{1,0:T(8,128)(2,1)S(1)} collective-permute-done((bf16[128,128]{1,0:T(8,128)(2,1)S(1)}, bf16[128,128]{1,0:T(8,128)(2,1)S(1)}, u32[]{:S(2)}, u32[]{:S(2)}) %collective-permute-start.7) | collective-permute-done | bytes 32800 | tf_op jit(solution)/shard_map/ppermute | solution.py:441
  49.4 14.7 %b.1 = (bf16[16,4,128,128]{3,2,1,0:T(8,128)(2,1)}, bf16[1024,512]{1,0:T(8,128)(2,1)}, bf16[1024,512]{1,0:T(8,128)(2,1)}, bf16[1024,512]{1,0:T(8,128)(2,1)}, bf16...) custom-call(s32[2]{0:T(128)S(1)} %copy-done.3, ...), custom_call_target="tpu_custom_call" | custom-call | flops 1610612736 | bytes 27787784 | tf_op jit(solution)/shard_map/b/pallas_call | solution.py:461
  64.2 1.6 %collective-permute-start.9 = (bf16[128,128]{1,0:T(8,128)(2,1)S(1)}, bf16[128,128]{1,0:T(8,128)(2,1)S(1)}, u32[]{:S(2)}, u32[]{:S(2)}) collective-permute-start(bf16[128,128]{1,0:T(8,128)(2,1)S(1)} %get-tuple-element.116), channel_id=1, source_target_pairs={{0,8},{8,16},{16,24},{24,0},{32,40},{40,48},{48,56},{56,32},{64,72... | collective-permute-start | bytes 98312 | tf_op jit(solution)/shard_map/ppermute | solution.py:441
  65.8 2.5 %collective-permute-start.10 = (bf16[128,128]{1,0:T(8,128)(2,1)S(1)}, bf16[128,128]{1,0:T(8,128)(2,1)S(1)}, u32[]{:S(2)}, u32[]{:S(2)}) collective-permute-start(bf16[128,128]{1,0:T(8,128)(2,1)S(1)} %get-tuple-element.117), channel_id=1, source_target_pairs={{0,16},{8,24},{16,0},{24,8},{32,48},{40,56},{48,32},{56,40},{64,80... | collective-permute-start | bytes 98312 | tf_op jit(solution)/shard_map/ppermute | solution.py:441
  68.9 3.9 %c0.1.kk_ref = bf16[1024,512]{1,0:T(8,128)(2,1)} custom-call(f32[1024,512]{1,0:T(8,128)} %get-tuple-element.77.g_ref, bf16[1024,512]{1,0:T(8,128)(2,1)} %get-tuple-element.85.qd_ref, bf16[1024,512]{1,0:T(8,128)(2,1)} %get-tuple-element.106.u_ref, bf16[1024,512]{1,0:T(8,128)(2,1)} %get-tuple-element.107.do_ref), custom_call_target="tpu_custom_call" | custom-call | flops 268435456 | bytes 6291456 | tf_op jit(solution)/shard_map/c0/pallas_call | solution.py:461
  72.8 0.7 r1.1
  73.6 1.0 collective-permute-start.14
  74.5 0.8 collective-permute-start.13
  75.3 1.0 collective-permute-start.12
  76.7 0.9 collective-permute-done.14.p3
  77.5 2.4 %collective-permute-done.13.p2 = bf16[128,128]{1,0:T(8,128)(2,1)S(1)} collective-permute-done((bf16[128,128]{1,0:T(8,128)(2,1)S(1)}, bf16[128,128]{1,0:T(8,128)(2,1)S(1)}, u32[]{:S(2)}, u32[]{:S(2)}) %collective-permute-start.13) | collective-permute-done | bytes 32800 | tf_op jit(solution)/shard_map/ppermute | solution.py:441
  80.5 1.5 %r2.1 = (bf16[128,128]{1,0:T(8,128)(2,1)S(1)}, bf16[128,128]{1,0:T(8,128)(2,1)S(1)}, bf16[128,128]{1,0:T(8,128)(2,1)S(1)}, bf16[128,128]{1,0:T(8,128)(2,1)S(1)}, bf16[4,128,128]{2,1,0:T(8,128)(2,1)}) custom-call(s32[2]{0:T(128)S(1)} %copy-done.3, bf16[128,128]{1,0:T(8,128)(2,1)S(1)} %get-tuple-element.125.p0, ...), custom_call_target="tpu_custom_call" | custom-call | flops 8388608 | bytes 917512 | tf_op jit(solution)/shard_map/r2/pallas_call | solution.py:461
  82.0 1.2 %collective-permute-start.15 = (bf16[128,128]{1,0:T(8,128)(2,1)S(1)}, bf16[128,128]{1,0:T(8,128)(2,1)S(1)}, u32[]{:S(2)}, u32[]{:S(2)}) collective-permute-start(bf16[128,128]{1,0:T(8,128)(2,1)S(1)} %get-tuple-element.133), channel_id=1, source_target_pairs={{0,8},{8,16},{16,24},{24,0},{32,40},{40,48},{48,56},{56,32},{64,72... | collective-permute-start | bytes 98312 | tf_op jit(solution)/shard_map/ppermute | solution.py:441
  83.1 1.5 %collective-permute-start.16 = (bf16[128,128]{1,0:T(8,128)(2,1)S(1)}, bf16[128,128]{1,0:T(8,128)(2,1)S(1)}, u32[]{:S(2)}, u32[]{:S(2)}) collective-permute-start(bf16[128,128]{1,0:T(8,128)(2,1)S(1)} %get-tuple-element.134), channel_id=1, source_target_pairs={{0,16},{8,24},{16,0},{24,8},{32,48},{40,56},{48,32},{56,40},{64,80... | collective-permute-start | bytes 98312 | tf_op jit(solution)/shard_map/ppermute | solution.py:441
  84.6 1.2 %collective-permute-start.17 = (bf16[128,128]{1,0:T(8,128)(2,1)S(1)}, bf16[128,128]{1,0:T(8,128)(2,1)S(1)}, u32[]{:S(2)}, u32[]{:S(2)}) collective-permute-start(bf16[128,128]{1,0:T(8,128)(2,1)S(1)} %get-tuple-element.135), channel_id=1, source_target_pairs={{0,24},{8,0},{16,8},{24,16},{32,56},{40,32},{48,40},{56,48},{64,88... | collective-permute-start | bytes 98312 | tf_op jit(solution)/shard_map/ppermute | solution.py:441
  85.9 5.6 %c1.1 = (bf16[1024,512]{1,0:T(8,128)(2,1)}, f32[1024,512]{1,0:T(8,128)}) custom-call(bf16[1024,512]{1,0:T(8,128)(2,1)} %q_ref.3, f32[1024,512]{1,0:T(8,128)} %get-tuple-element.77.g_ref, bf16[1024,512]{1,0:T(8,128)(2,1)} %get-tuple-element.78.ki_ref, bf16[1024,512]{1,0:T(8,128)(2,1)} %get-tuple-element.106.u_ref, ...), custom_call_target="tpu_custom_call" | custom-call | flops 536870912 | bytes 11534336 | tf_op jit(solution)/shard_map/c1/pallas_call | solution.py:461
  91.5 11.5 %c2.1 = (bf16[1024,512]{1,0:T(8,128)(2,1)}, bf16[1024,512]{1,0:T(8,128)(2,1)}, f32[1024,512]{1,0:T(8,128)}, f32[4,1024]{1,0:T(4,128)}) custom-call(s32[2]{0:T(128)S(1)} %copy-done.3, s32[1]{0:T(128)S(6)} %copy.17.resets, bf16[1024,512]{1,0:T(8,128)(2,1)} %k_ref.5, f32[1024,512]{1,0:T(8,128)} %get-tuple-element.77.g_ref, f32[4,1024]{1,0:T(4,128)S(1)} %copy-done.1, ...), custom_call_target="tpu_custom_call" | custom-call | flops 1342177280 | bytes 21659660 | tf_op jit(solution)/shard_map/c2/pallas_call | solution.py:461
  (30 shorter events, 3.8 us)
Async XLA Ops:
  7.2 42.2 %all-gather.2.cloned.1.call-start = ((), (), s32[]{:S(2)}) async-start(), calls=%async_computation | async-start | bytes 5308416 | tf_op jit(solution)/shard_map/all_gather | solution.py:486
  19.4 11.9 %collective-permute-start = (bf16[256,128]{1,0:T(8,128)(2,1)}, bf16[256,128]{1,0:T(8,128)(2,1)S(1)}, u32[]{:S(2)}, u32[]{:S(2)}) collective-permute-start(bf16[256,128]{1,0:T(8,128)(2,1)} %get-tuple-element.81), channel_id=1, source_target_pairs={{0,8},{8,16},{16,24},{24,0},{32,40},{40,48},{48,56},{56,32},{64,72... | collective-permute-start | bytes 196616 | tf_op jit(solution)/shard_map/ppermute | solution.py:441
  21.5 9.9 %collective-permute-start.1 = (bf16[256,128]{1,0:T(8,128)(2,1)}, bf16[256,128]{1,0:T(8,128)(2,1)S(1)}, u32[]{:S(2)}, u32[]{:S(2)}) collective-permute-start(bf16[256,128]{1,0:T(8,128)(2,1)} %get-tuple-element.82), channel_id=1, source_target_pairs={{0,16},{8,24},{16,0},{24,8},{32,48},{40,56},{48,32},{56,40},{64,80... | collective-permute-start | bytes 196616 | tf_op jit(solution)/shard_map/ppermute | solution.py:441
  25.0 6.3 %collective-permute-start.2 = (bf16[256,128]{1,0:T(8,128)(2,1)}, bf16[256,128]{1,0:T(8,128)(2,1)S(1)}, u32[]{:S(2)}, u32[]{:S(2)}) collective-permute-start(bf16[256,128]{1,0:T(8,128)(2,1)} %get-tuple-element.83), channel_id=1, source_target_pairs={{0,24},{8,0},{16,8},{24,16},{32,56},{40,32},{48,40},{56,48},{64,88... | collective-permute-start | bytes 196616 | tf_op jit(solution)/shard_map/ppermute | solution.py:441
  26.1 5.3 %copy-start.2 = (bf16[256,128]{1,0:T(8,128)(2,1)S(1)}, bf16[256,128]{1,0:T(8,128)(2,1)}, u32[]{:S(2)}) copy-start(bf16[256,128]{1,0:T(8,128)(2,1)} %get-tuple-element.91.p0) | copy-start | bytes 196612
  26.1 5.3 %copy-start.3 = (s32[2]{0:T(128)S(1)}, s32[2]{0:T(128)}, u32[]{:S(2)}) copy-start(s32[2]{0:T(128)} %pad_add_fusion.place) | copy-start | bytes 28
  26.1 23.3 %copy-start = (bf16[16,64,256]{2,1,0:T(8,128)(2,1)S(1)}, bf16[16,64,256]{2,1,0:T(8,128)(2,1)}, u32[]{:S(2)}) copy-start(bf16[16,64,256]{2,1,0:T(8,128)(2,1)} %get-tuple-element.87.wb_ref) | copy-start | bytes 1572868
  26.1 23.4 %copy-start.4 = (f32[128]{0:T(128)S(1)}, f32[128]{0:T(128)}, u32[]{:S(2)}) copy-start(f32[128]{0:T(128)} %param.18) | copy-start | bytes 1540
  32.3 5.0 %collective-permute-start.5 = (bf16[256,128]{1,0:T(8,128)(2,1)S(1)}, bf16[256,128]{1,0:T(8,128)(2,1)S(1)}, u32[]{:S(2)}, u32[]{:S(2)}) collective-permute-start(bf16[256,128]{1,0:T(8,128)(2,1)S(1)} %get-tuple-element.97.p0), channel_id=1, source_target_pairs={{0,96},{8,104},{16,112},{24,120},{32,0},{40,8},{48,16},{56,24},{64... | collective-permute-start | bytes 196616 | tf_op jit(solution)/shard_map/ppermute | solution.py:441
  35.4 5.8 %collective-permute-start.4 = (bf16[256,128]{1,0:T(8,128)(2,1)S(1)}, bf16[256,128]{1,0:T(8,128)(2,1)S(1)}, u32[]{:S(2)}, u32[]{:S(2)}) collective-permute-start(bf16[256,128]{1,0:T(8,128)(2,1)S(1)} %get-tuple-element.97.p0), channel_id=1, source_target_pairs={{0,64},{8,72},{16,80},{24,88},{32,96},{40,104},{48,112},{56,120},{... | collective-permute-start | bytes 196616 | tf_op jit(solution)/shard_map/ppermute | solution.py:441
  36.1 5.8 %collective-permute-start.3 = (bf16[256,128]{1,0:T(8,128)(2,1)S(1)}, bf16[256,128]{1,0:T(8,128)(2,1)S(1)}, u32[]{:S(2)}, u32[]{:S(2)}) collective-permute-start(bf16[256,128]{1,0:T(8,128)(2,1)S(1)} %get-tuple-element.97.p0), channel_id=1, source_target_pairs={{0,32},{8,40},{16,48},{24,56},{32,64},{40,72},{48,80},{56,88},{64,... | collective-permute-start | bytes 196616 | tf_op jit(solution)/shard_map/ppermute | solution.py:441
  42.9 5.2 %collective-permute-start.6 = (bf16[128,128]{1,0:T(8,128)(2,1)S(1)}, bf16[128,128]{1,0:T(8,128)(2,1)S(1)}, u32[]{:S(2)}, u32[]{:S(2)}) collective-permute-start(bf16[128,128]{1,0:T(8,128)(2,1)S(1)} %get-tuple-element.103), channel_id=1, source_target_pairs={{0,8},{8,16},{16,24},{24,0},{32,40},{40,48},{48,56},{56,32},{64,72... | collective-permute-start | bytes 98312 | tf_op jit(solution)/shard_map/ppermute | solution.py:441
  44.0 5.4 %collective-permute-start.7 = (bf16[128,128]{1,0:T(8,128)(2,1)S(1)}, bf16[128,128]{1,0:T(8,128)(2,1)S(1)}, u32[]{:S(2)}, u32[]{:S(2)}) collective-permute-start(bf16[128,128]{1,0:T(8,128)(2,1)S(1)} %get-tuple-element.104), channel_id=1, source_target_pairs={{0,16},{8,24},{16,0},{24,8},{32,48},{40,56},{48,32},{56,40},{64,80... | collective-permute-start | bytes 98312 | tf_op jit(solution)/shard_map/ppermute | solution.py:441
  44.8 4.6 %collective-permute-start.8 = (bf16[128,128]{1,0:T(8,128)(2,1)S(1)}, bf16[128,128]{1,0:T(8,128)(2,1)S(1)}, u32[]{:S(2)}, u32[]{:S(2)}) collective-permute-start(bf16[128,128]{1,0:T(8,128)(2,1)S(1)} %get-tuple-element.105), channel_id=1, source_target_pairs={{0,24},{8,0},{16,8},{24,16},{32,56},{40,32},{48,40},{56,48},{64,88... | collective-permute-start | bytes 98312 | tf_op jit(solution)/shard_map/ppermute | solution.py:441
  64.2 8.6 %collective-permute-start.9 = (bf16[128,128]{1,0:T(8,128)(2,1)S(1)}, bf16[128,128]{1,0:T(8,128)(2,1)S(1)}, u32[]{:S(2)}, u32[]{:S(2)}) collective-permute-start(bf16[128,128]{1,0:T(8,128)(2,1)S(1)} %get-tuple-element.116), channel_id=1, source_target_pairs={{0,8},{8,16},{16,24},{24,0},{32,40},{40,48},{48,56},{56,32},{64,72... | collective-permute-start | bytes 98312 | tf_op jit(solution)/shard_map/ppermute | solution.py:441
  65.8 7.0 %collective-permute-start.10 = (bf16[128,128]{1,0:T(8,128)(2,1)S(1)}, bf16[128,128]{1,0:T(8,128)(2,1)S(1)}, u32[]{:S(2)}, u32[]{:S(2)}) collective-permute-start(bf16[128,128]{1,0:T(8,128)(2,1)S(1)} %get-tuple-element.117), channel_id=1, source_target_pairs={{0,16},{8,24},{16,0},{24,8},{32,48},{40,56},{48,32},{56,40},{64,80... | collective-permute-start | bytes 98312 | tf_op jit(solution)/shard_map/ppermute | solution.py:441
  68.3 4.5 %collective-permute-start.11 = (bf16[128,128]{1,0:T(8,128)(2,1)S(1)}, bf16[128,128]{1,0:T(8,128)(2,1)S(1)}, u32[]{:S(2)}, u32[]{:S(2)}) collective-permute-start(bf16[128,128]{1,0:T(8,128)(2,1)S(1)} %get-tuple-element.118), channel_id=1, source_target_pairs={{0,24},{8,0},{16,8},{24,16},{32,56},{40,32},{48,40},{56,48},{64,88... | collective-permute-start | bytes 98312 | tf_op jit(solution)/shard_map/ppermute | solution.py:441
  73.6 4.0 %collective-permute-start.14 = (bf16[128,128]{1,0:T(8,128)(2,1)S(1)}, bf16[128,128]{1,0:T(8,128)(2,1)S(1)}, u32[]{:S(2)}, u32[]{:S(2)}) collective-permute-start(bf16[128,128]{1,0:T(8,128)(2,1)S(1)} %get-tuple-element.125.p0), channel_id=1, source_target_pairs={{0,96},{8,104},{16,112},{24,120},{32,0},{40,8},{48,16},{56,24},{64... | collective-permute-start | bytes 98312 | tf_op jit(solution)/shard_map/ppermute | solution.py:441
  74.5 5.4 %collective-permute-start.13 = (bf16[128,128]{1,0:T(8,128)(2,1)S(1)}, bf16[128,128]{1,0:T(8,128)(2,1)S(1)}, u32[]{:S(2)}, u32[]{:S(2)}) collective-permute-start(bf16[128,128]{1,0:T(8,128)(2,1)S(1)} %get-tuple-element.125.p0), channel_id=1, source_target_pairs={{0,64},{8,72},{16,80},{24,88},{32,96},{40,104},{48,112},{56,120},{... | collective-permute-start | bytes 98312 | tf_op jit(solution)/shard_map/ppermute | solution.py:441
  75.3 5.1 %collective-permute-start.12 = (bf16[128,128]{1,0:T(8,128)(2,1)S(1)}, bf16[128,128]{1,0:T(8,128)(2,1)S(1)}, u32[]{:S(2)}, u32[]{:S(2)}) collective-permute-start(bf16[128,128]{1,0:T(8,128)(2,1)S(1)} %get-tuple-element.125.p0), channel_id=1, source_target_pairs={{0,32},{8,40},{16,48},{24,56},{32,64},{40,72},{48,80},{56,88},{64,... | collective-permute-start | bytes 98312 | tf_op jit(solution)/shard_map/ppermute | solution.py:441
  82.0 9.5 %collective-permute-start.15 = (bf16[128,128]{1,0:T(8,128)(2,1)S(1)}, bf16[128,128]{1,0:T(8,128)(2,1)S(1)}, u32[]{:S(2)}, u32[]{:S(2)}) collective-permute-start(bf16[128,128]{1,0:T(8,128)(2,1)S(1)} %get-tuple-element.133), channel_id=1, source_target_pairs={{0,8},{8,16},{16,24},{24,0},{32,40},{40,48},{48,56},{56,32},{64,72... | collective-permute-start | bytes 98312 | tf_op jit(solution)/shard_map/ppermute | solution.py:441
  83.1 8.4 %collective-permute-start.16 = (bf16[128,128]{1,0:T(8,128)(2,1)S(1)}, bf16[128,128]{1,0:T(8,128)(2,1)S(1)}, u32[]{:S(2)}, u32[]{:S(2)}) collective-permute-start(bf16[128,128]{1,0:T(8,128)(2,1)S(1)} %get-tuple-element.134), channel_id=1, source_target_pairs={{0,16},{8,24},{16,0},{24,8},{32,48},{40,56},{48,32},{56,40},{64,80... | collective-permute-start | bytes 98312 | tf_op jit(solution)/shard_map/ppermute | solution.py:441
  84.6 6.9 %collective-permute-start.17 = (bf16[128,128]{1,0:T(8,128)(2,1)S(1)}, bf16[128,128]{1,0:T(8,128)(2,1)S(1)}, u32[]{:S(2)}, u32[]{:S(2)}) collective-permute-start(bf16[128,128]{1,0:T(8,128)(2,1)S(1)} %get-tuple-element.135), channel_id=1, source_target_pairs={{0,24},{8,0},{16,8},{24,16},{32,56},{40,32},{48,40},{56,48},{64,88... | collective-permute-start | bytes 98312 | tf_op jit(solution)/shard_map/ppermute | solution.py:441
  85.9 5.7 %copy-start.1 = (f32[4,1024]{1,0:T(4,128)S(1)}, f32[4,1024]{1,0:T(4,128)}, u32[]{:S(2)}) copy-start(f32[4,1024]{1,0:T(4,128)} %b_ref.3) | copy-start | bytes 49156
Sparse Core Ops, SparseCore 0:
  9.7 36.7 all-gather.1

commit v5 on v4

--- a/solution.py
+++ b/solution.py
@@ -12,7 +12,7 @@
 GROUP = 64
 EPS = 1e-6
 SCALE = DK**-0.5
-STEP = dict(a1=4, a2=8, b=4, c0=8, c1=8, c2=4)
+STEP = dict(a1=4, a2=8, b=4, c0=8, c1=4, c2=4)
 UNITS = dict(a1=16, a2=16, b=16, c0=16, c1=16, c2=16)
 RING = 4
 
@@ -71,6 +71,14 @@
     return [f(*xs) for xs in zip(*lists)]
 
 
+def outer():
+    return lax.axis_index("seq") // RING
+
+
+def inner():
+    return lax.rem(lax.axis_index("seq"), RING)
+
+
 def spread(me, array, outs):
     for shift, out in enumerate(outs):
         out[...] = array[lax.rem(me + shift, RING)].astype(out.dtype)
@@ -96,7 +104,7 @@
 
 
 def kernel_a1(
-    heads, place, resets, k_ref, v_ref, d_ref, b_ref, w_ref,
+    heads, resets, k_ref, v_ref, d_ref, b_ref, w_ref,
     g_ref, wb_ref, kd_ref, kt_ref, y_ref, n_ref, pre_ref, o0, o1, o2, o3, state,
 ):
     step = pl.program_id(0)
@@ -144,7 +152,7 @@
 
     @pl.when(step == pl.num_programs(0) - 1)
     def _():
-        spread(place[1], state, (o0, o1, o2, o3))
+        spread(inner(), state, (o0, o1, o2, o3))
 
 
 def kernel_a2(heads, q_ref, k_ref, g_ref, qd_ref, ki_ref, a_ref, at_ref):
@@ -166,7 +174,7 @@
 
 
 def kernel_b(
-    heads, place, v_ref, kd_ref, qd_ref, y_ref, wb_ref, a_ref, at_ref, pre_ref, gate_ref, x_ref, p_ref, gain_ref,
+    heads, v_ref, kd_ref, qd_ref, y_ref, wb_ref, a_ref, at_ref, pre_ref, gate_ref, x_ref, p_ref, gain_ref,
     s0, s1, s2, s3, e_ref, vp_ref, u_ref, do_ref, du_ref, dt_ref, dg_ref, r0, r1, r2, r3, total, s_ref,
 ):
     step = pl.program_id(0)
@@ -174,7 +182,7 @@
     @pl.when(step == 0)
     def _():
         total[...] = jnp.zeros_like(total)
-        collect(place[1], s_ref, (s0, s1, s2, s3))
+        collect(inner(), s_ref, (s0, s1, s2, s3))
 
     gain = gain_ref[...]
     sums = [total[h] for h in range(heads)]
@@ -246,10 +254,11 @@
 
     @pl.when(step == pl.num_programs(0) - 1)
     def _():
-        spread(place[1], total, (r0, r1, r2, r3))
-
-
-def kernel_c1(heads, q_ref, g_ref, ki_ref, u_ref, do_ref, e_ref, dq_ref, pq_ref):
+        spread(inner(), total, (r0, r1, r2, r3))
+
+
+def kernel_c1(heads, q_ref, g_ref, ki_ref, u_ref, do_ref, e_ref, *outs):
+    dq_ref, pq_ref = outs[-2:]
     lower = triangle(False, f32)
     for group in units(heads, "c1"):
         us = [u_ref[half(c), cols(h)] for c, h in group]
@@ -289,7 +298,7 @@
 
 
 def kernel_c2(
-    heads, place, resets, k_ref, g_ref, b_ref, wb_ref, kt_ref, n_ref, e_ref, vp_ref, u_ref, du_ref, dt_ref,
+    heads, resets, k_ref, g_ref, b_ref, wb_ref, kt_ref, n_ref, e_ref, vp_ref, u_ref, du_ref, dt_ref,
     pq_ref, kk_ref, g0, g1, g2, g3, dk_ref, dv_ref, dd_ref, db_ref, state,
 ):
     step = pl.program_id(0)
@@ -297,7 +306,7 @@
 
     @pl.when(step == 0)
     def _():
-        collect(place[1], state, (g0, g1, g2, g3))
+        collect(inner(), state, (g0, g1, g2, g3))
 
     weights = twice(True)
     ones = jnp.ones((16, 128), bf16)
@@ -368,8 +377,8 @@
     return jnp.concatenate([moved[0:128] + pair[0:128].astype(f32), moved[128:256]], axis=0)
 
 
-def kernel_f1(heads, place, p0, p1, p2, p3, total_ref, before_ref, slots):
-    collect(place[1], slots, (p0, p1, p2, p3))
+def kernel_f1(heads, p0, p1, p2, p3, total_ref, before_ref, slots):
+    collect(inner(), slots, (p0, p1, p2, p3))
     before_ref[0] = identity_pair()
     r = slots[0]
     for z in range(1, RING):
@@ -389,8 +398,8 @@
         m_ref[z - 1] = m
 
 
-def kernel_f2(heads, place, p0, p1, p2, p3, before, o0, o1, o2, o3, slots, states):
-    me = place[0]
+def kernel_f2(heads, p0, p1, p2, p3, before, o0, o1, o2, o3, slots, states):
+    me = outer()
     collect(me, slots, (p0, p1, p2, p3))
     s = jnp.where(me > 0, slots[0, 0:128].astype(f32), 0.0)
     for i in range(1, RING - 1):
@@ -400,11 +409,11 @@
     moved = [nn(sb, before[z, 128:256]) for z in range(RING)]
     for z in range(RING):
         states[z] = (moved[z] + before[z, 0:128].astype(f32)).astype(bf16)
-    spread(place[1], states, (o0, o1, o2, o3))
-
-
-def kernel_r1(heads, place, p0, p1, p2, p3, before, total_ref, slots):
-    collect(place[1], slots, (p0, p1, p2, p3))
+    spread(inner(), states, (o0, o1, o2, o3))
+
+
+def kernel_r1(heads, p0, p1, p2, p3, before, total_ref, slots):
+    collect(inner(), slots, (p0, p1, p2, p3))
     parts = [nt(slots[z], before[z, 128:256]) for z in range(1, RING)]
     total_ref[...] = (slots[0].astype(f32) + sum(parts)).astype(bf16)
 
@@ -418,8 +427,8 @@
         later_ref[z - 1] = g
 
 
-def kernel_r2(heads, place, p0, p1, p2, p3, later, later_m, yslots, o0, o1, o2, o3, slots, grads):
-    me = place[0]
+def kernel_r2(heads, p0, p1, p2, p3, later, later_m, yslots, o0, o1, o2, o3, slots, grads):
+    me = outer()
     collect(me, slots, (p0, p1, p2, p3))
     g = jnp.where(me < RING - 1, slots[RING - 1].astype(f32), 0.0)
     for i in reversed(range(1, RING - 1)):
@@ -429,7 +438,7 @@
     moved = [nt(gb, later_m[z]) for z in range(RING)]
     for z in range(RING):
         grads[z] = (moved[z] + later[z].astype(f32)).astype(bf16)
-    spread(place[1], grads, (o0, o1, o2, o3))
+    spread(inner(), grads, (o0, o1, o2, o3))
 
 
 def permute(x, distance, outer):
@@ -455,7 +464,7 @@
     return jax.ShapeDtypeStruct(dims, dtype)
 
 
-def call(body, name, heads, in_specs, out_specs, out_shape, scratch, grid, flops, *args):
+def call(body, name, heads, in_specs, out_specs, out_shape, scratch, grid, flops, *args, into=()):
     total = sum(a.size * a.dtype.itemsize for a in args)
     total += sum(o.size * o.dtype.itemsize for o in out_shape)
     return pl.pallas_call(
@@ -465,13 +474,14 @@
         in_specs=in_specs,
         out_specs=out_specs,
         scratch_shapes=scratch,
+        input_output_aliases={len(args) + i: i for i in range(len(into))},
         compiler_params=pltpu.CompilerParams(
             vmem_limit_bytes=LIMIT.get(name, 8) * 2**20,
             **({"dimension_semantics": ("arbitrary",)} if grid else {}),
         ),
         cost_estimate=pl.CostEstimate(flops=flops, bytes_accessed=total, transcendentals=0),
         name=name,
-    )(*args)
+    )(*args, *into)
 
 
 def per_device(
@@ -481,8 +491,6 @@
     heads = beta.shape[0]
     count = tokens // GROUP
     width = heads * 128
-    index = lax.axis_index("seq")
-    place = jnp.stack([index // RING, index % RING]).astype(jnp.int32)
     gathered = lax.all_gather(grad_out.T, "head", axis=0, tiled=True)
     model = out_proj.shape[1]
 
@@ -518,11 +526,11 @@
     s = specs("a1")
     gamma, wb, kd, kt, y, n, pre, *mb = call(
         kernel_a1, "a1", heads,
-        [SMEM, SMEM, s["tok"], s["tok"], s["tok"], s["beta"], s["wy"]],
+        [SMEM, s["tok"], s["tok"], s["tok"], s["beta"], s["wy"]],
         [s["tok"], s["wy"], s["tok"], s["tok"], s["tok"], s["state"], s["pair"]] + [s["whole2"]] * 4,
         [tok_f, small_b, tok_b, tok_b, tok_b, state_b, pair_b] + [two_b] * 4,
         [pltpu.VMEM((heads, 256, 128), f32)], s["grid"], 8 * unit,
-        place, resets, keys, values, decay, beta, wy_inverse,
+        resets, keys, values, decay, beta, wy_inverse,
     )
     zs = three(mb, False)
     s = specs("a2")
@@ -535,25 +543,25 @@
     )
     zs, qd = lax.optimization_barrier((zs, qd))
     group, before, zslots = call(
-        kernel_f1, "f1", heads, [SMEM] + [VMEM] * 4, [VMEM] * 3, [two_b, twos_b, twos_b], [], (),
-        unit // 8, place, *zs,
+        kernel_f1, "f1", heads, [VMEM] * 4, [VMEM] * 3, [two_b, twos_b, twos_b], [], (),
+        unit // 8, *zs,
     )
     ys = three(group, True)
     (later_m,) = call(kernel_m, "m", heads, [VMEM], [VMEM], [ones_b], [], (), unit // 16, zslots)
     ys, later_m = lax.optimization_barrier((ys, later_m))
     *states, yslots = call(
-        kernel_f2, "f2", heads, [SMEM] + [VMEM] * 5, [VMEM] * 5, [one_b] * 4 + [twos_b],
-        [pltpu.VMEM((RING, 128, 128), bf16)], (), unit // 8, place, *ys, before,
+        kernel_f2, "f2", heads, [VMEM] * 5, [VMEM] * 5, [one_b] * 4 + [twos_b],
+        [pltpu.VMEM((RING, 128, 128), bf16)], (), unit // 8, *ys, before,
     )
     state_in = three(states, False)
     s = specs("b")
     e, vp, u, do, du, dt, dgate, *r = call(
         kernel_b, "b", heads,
-        [SMEM, s["tok"], s["tok"], s["tok"], s["tok"], s["wy"], s["wy"], s["wy"], s["pair"], s["tok"], s["parts"], s["proj"], s["gain"]] + [s["whole"]] * 4,
+        [s["tok"], s["tok"], s["tok"], s["tok"], s["wy"], s["wy"], s["wy"], s["pair"], s["tok"], s["parts"], s["proj"], s["gain"]] + [s["whole"]] * 4,
         [s["state"], s["tok"], s["tok"], s["tok"], s["tok"], s["state"], s["tok"]] + [s["whole"]] * 4,
         [state_b, tok_b, tok_b, tok_b, tok_b, state_b, tok_b] + [one_b] * 4,
         [pltpu.VMEM((heads, 128, 128), f32), pltpu.VMEM((heads, 128, 128), bf16)], s["grid"], 12 * unit,
-        place, values, kd, qd, y, wb, a, at, pre, out_gate, gathered, out_proj, norm_gain.reshape(1, 128), *state_in,
+        values, kd, qd, y, wb, a, at, pre, out_gate, gathered, out_proj, norm_gain.reshape(1, 128), *state_in,
     )
     zr = three(r, False)
     s = specs("c0")
@@ -562,33 +570,40 @@
     )
     zr, kk = lax.optimization_barrier((zr, kk))
     rgroup, rslots = call(
-        kernel_r1, "r1", heads, [SMEM] + [VMEM] * 5, [VMEM] * 2, [one_b, ones_b], [], (),
-        unit // 16, place, *zr, before,
+        kernel_r1, "r1", heads, [VMEM] * 5, [VMEM] * 2, [one_b, ones_b], [], (),
+        unit // 16, *zr, before,
     )
     yr = three(rgroup, True)
     (later,) = call(kernel_r3, "r3", heads, [VMEM] * 2, [VMEM], [ones_b], [], (), unit // 16, rslots, zslots)
-    yr, later = lax.optimization_barrier((yr, later))
+
+    def gradient_q(part, into):
+        steps = count // STEP["c1"] // 2
+        tok = pl.BlockSpec((STEP["c1"] * GROUP, width), lambda i: (i + part * steps, 0))
+        state = pl.BlockSpec((STEP["c1"], heads, 128, 128), lambda i: (i + part * steps, 0, 0, 0))
+        return call(
+            kernel_c1, "c1", heads,
+            [tok] * 5 + [state] + [pl.BlockSpec(memory_space=pl.ANY)] * len(into),
+            [tok, tok], [tok_b, tok_f],
+            [], (steps,), 2 * unit, queries, gamma, ki, u, do, e, into=into,
+        )
+
+    dq, pq = gradient_q(0, ())
+    yr, later, pq = lax.optimization_barrier((yr, later, pq))
     *grads, _ = call(
-        kernel_r2, "r2", heads, [SMEM] + [VMEM] * 7, [VMEM] * 5, [one_b] * 4 + [ones_b],
-        [pltpu.VMEM((RING, 128, 128), bf16)], (), unit // 16, place, *yr, later, later_m, yslots,
+        kernel_r2, "r2", heads, [VMEM] * 7, [VMEM] * 5, [one_b] * 4 + [ones_b],
+        [pltpu.VMEM((RING, 128, 128), bf16)], (), unit // 16, *yr, later, later_m, yslots,
     )
     grad_in = three(grads, False)
-    s = specs("c1")
-    dq, pq = call(
-        kernel_c1, "c1", heads,
-        [s["tok"]] * 5 + [s["state"]],
-        [s["tok"], s["tok"]], [tok_b, tok_f],
-        [], s["grid"], 4 * unit, queries, gamma, ki, u, do, e,
-    )
+    dq, pq = gradient_q(1, (dq, pq))
     grad_in, pq = lax.optimization_barrier((grad_in, pq))
     s = specs("c2", True)
     dk, dv, dd, db = call(
         kernel_c2, "c2", heads,
-        [SMEM, SMEM, s["tok"], s["tok"], s["beta"], s["wy"], s["tok"], s["state"], s["state"], s["tok"], s["tok"], s["tok"], s["state"], s["tok"], s["tok"]] + [s["whole"]] * 4,
+        [SMEM, s["tok"], s["tok"], s["beta"], s["wy"], s["tok"], s["state"], s["state"], s["tok"], s["tok"], s["tok"], s["state"], s["tok"], s["tok"]] + [s["whole"]] * 4,
         [s["tok"], s["tok"], s["tok"], s["beta"]],
         [tok_b, tok_b, tok_f, shape((heads, tokens), f32)],
         [pltpu.VMEM((heads, 128, 128), f32)], s["grid"], 10 * unit,
-        place, resets, keys, gamma, beta, wb, kt, n, e, vp, u, du, dt, pq, kk, *grad_in,
+        resets, keys, gamma, beta, wb, kt, n, e, vp, u, du, dt, pq, kk, *grad_in,
     )
     return dq, dk, dv, dd, db, dgate
 

time: 110 us -> 106 us (0.964)
  waiting for transfers between devices: 11.8 us -> 8.2 us
    ppermute x18, waiting for transfers between devices: 11.1 us -> 7.52 us  [permute(): return lax.ppermute(x, 'seq', pairs)]
    pallas_call x12 -> x13, Pallas kernels: 56 us -> 55.5 us  [call(): pl.pallas_call(functools.partial(body, heads), out_shape=out_shape, grid=...]
  transfers between devices with their start and end apart: 19 -> 19, of which waited for: 7 -> 5; matrix products, arithmetic and copies ran while one was open for 1% -> 0% of each run, Pallas kernels for 25% -> 27%
where the time goes in v5:
time: 106 us
  Pallas kernels  55.5 us (52%)
  starting transfers between devices  27.7 us (26%)
  between operations  14.8 us (14%)
  waiting for transfers between devices  8.2 us (8%)
    pallas_call x13, Pallas kernels, call(): pl.pallas_call(functools.partial(body, heads), out_shape=out_shape, grid=...  55.5 us
    ppermute x18, starting transfers between devices, permute(): return lax.ppermute(x, 'seq', pairs)  27.7 us
    ppermute x18, waiting for transfers between devices, permute(): return lax.ppermute(x, 'seq', pairs)  7.52 us
  transfers between devices with their start and end apart: 19, of which 5 were waited for; matrix products, arithmetic and copies ran while one was open for 0% of the time, Pallas kernels for 27%

profile of v5, /device:TPU:0, one launch (start us, length us, event | category | flops | bytes accessed | tf_op | source)
XLA Modules:
  0.0 106.2 jit_solution(15250472430826715591)
XLA Ops:
  7.2 0.7 all-gather.2.cloned.1.call-update
  8.5 10.2 %a1.1 = (f32[1024,512]{1,0:T(8,128)}, bf16[16,64,256]{2,1,0:T(8,128)(2,1)}, bf16[1024,512]{1,0:T(8,128)(2,1)}, bf16[1024,512]{1,0:T(8,128)(2,1)}, bf16[1024,512]...) custom-call(s32[1]{0:T(128)S(6)} %copy.21.resets, ...), custom_call_target="tpu_custom_call" | custom-call | flops 1073741824 | bytes 17580036 | tf_op jit(solution)/shard_map/a1/pallas_call | solution.py:470
  18.7 2.1 %collective-permute-start = (bf16[256,128]{1,0:T(8,128)(2,1)}, bf16[256,128]{1,0:T(8,128)(2,1)S(1)}, u32[]{:S(2)}, u32[]{:S(2)}) collective-permute-start(bf16[256,128]{1,0:T(8,128)(2,1)} %get-tuple-element.84), channel_id=1, source_target_pairs={{0,8},{8,16},{16,24},{24,0},{32,40},{40,48},{48,56},{56,32},{64,72... | collective-permute-start | bytes 196616 | tf_op jit(solution)/shard_map/ppermute | solution.py:450
  20.8 3.6 %collective-permute-start.1 = (bf16[256,128]{1,0:T(8,128)(2,1)}, bf16[256,128]{1,0:T(8,128)(2,1)S(1)}, u32[]{:S(2)}, u32[]{:S(2)}) collective-permute-start(bf16[256,128]{1,0:T(8,128)(2,1)} %get-tuple-element.85), channel_id=1, source_target_pairs={{0,16},{8,24},{16,0},{24,8},{32,48},{40,56},{48,32},{56,40},{64,80... | collective-permute-start | bytes 196616 | tf_op jit(solution)/shard_map/ppermute | solution.py:450
  24.4 1.0 collective-permute-start.2
  25.4 5.2 %a2.1 = (bf16[1024,512]{1,0:T(8,128)(2,1)}, bf16[1024,512]{1,0:T(8,128)(2,1)}, bf16[16,64,256]{2,1,0:T(8,128)(2,1)}, bf16[16,64,256]{2,1,0:T(8,128)(2,1)}) custom-call(bf16[1024,512]{1,0:T(8,128)(2,1)} %q_ref.5, bf16[1024,512]{1,0:T(8,128)(2,1)} %k_ref.5, f32[1024,512]{1,0:T(8,128)} %get-tuple-element.80.g_ref), custom_call_target="tpu_custom_call" | custom-call | flops 268435456 | bytes 7340032 | tf_op jit(solution)/shard_map/a2/pallas_call | solution.py:470
  31.1 3.1 %collective-permute-start.5 = (bf16[256,128]{1,0:T(8,128)(2,1)S(1)}, bf16[256,128]{1,0:T(8,128)(2,1)S(1)}, u32[]{:S(2)}, u32[]{:S(2)}) collective-permute-start(bf16[256,128]{1,0:T(8,128)(2,1)S(1)} %get-tuple-element.100.p0), channel_id=1, source_target_pairs={{0,96},{8,104},{16,112},{24,120},{32,0},{40,8},{48,16},{56,24},{64... | collective-permute-start | bytes 196616 | tf_op jit(solution)/shard_map/ppermute | solution.py:450
  34.2 0.6 collective-permute-start.4
  34.8 1.0 collective-permute-start.3
  36.1 3.9 %collective-permute-done.4.p2 = bf16[256,128]{1,0:T(8,128)(2,1)S(1)} collective-permute-done((bf16[256,128]{1,0:T(8,128)(2,1)S(1)}, bf16[256,128]{1,0:T(8,128)(2,1)S(1)}, u32[]{:S(2)}, u32[]{:S(2)}) %collective-permute-start.4) | collective-permute-done | bytes 65568 | tf_op jit(solution)/shard_map/ppermute | solution.py:450
  40.0 0.7 collective-permute-done.3.p1
  40.7 0.5 f2.1
  41.1 1.1 %collective-permute-start.6 = (bf16[128,128]{1,0:T(8,128)(2,1)S(1)}, bf16[128,128]{1,0:T(8,128)(2,1)S(1)}, u32[]{:S(2)}, u32[]{:S(2)}) collective-permute-start(bf16[128,128]{1,0:T(8,128)(2,1)S(1)} %get-tuple-element.106), channel_id=1, source_target_pairs={{0,8},{8,16},{16,24},{24,0},{32,40},{40,48},{48,56},{56,32},{64,72... | collective-permute-start | bytes 98312 | tf_op jit(solution)/shard_map/ppermute | solution.py:450
  42.2 0.9 collective-permute-start.7
  43.1 1.9 %collective-permute-start.8 = (bf16[128,128]{1,0:T(8,128)(2,1)S(1)}, bf16[128,128]{1,0:T(8,128)(2,1)S(1)}, u32[]{:S(2)}, u32[]{:S(2)}) collective-permute-start(bf16[128,128]{1,0:T(8,128)(2,1)S(1)} %get-tuple-element.108), channel_id=1, source_target_pairs={{0,24},{8,0},{16,8},{24,16},{32,56},{40,32},{48,40},{56,48},{64,88... | collective-permute-start | bytes 98312 | tf_op jit(solution)/shard_map/ppermute | solution.py:450
  45.0 1.3 %collective-permute-done.6.s1 = bf16[128,128]{1,0:T(8,128)(2,1)S(1)} collective-permute-done((bf16[128,128]{1,0:T(8,128)(2,1)S(1)}, bf16[128,128]{1,0:T(8,128)(2,1)S(1)}, u32[]{:S(2)}, u32[]{:S(2)}) %collective-permute-start.6) | collective-permute-done | bytes 32800 | tf_op jit(solution)/shard_map/ppermute | solution.py:450
  46.3 1.3 %collective-permute-done.7.s2 = bf16[128,128]{1,0:T(8,128)(2,1)S(1)} collective-permute-done((bf16[128,128]{1,0:T(8,128)(2,1)S(1)}, bf16[128,128]{1,0:T(8,128)(2,1)S(1)}, u32[]{:S(2)}, u32[]{:S(2)}) %collective-permute-start.7) | collective-permute-done | bytes 32800 | tf_op jit(solution)/shard_map/ppermute | solution.py:450
  47.7 14.8 %b.1 = (bf16[16,4,128,128]{3,2,1,0:T(8,128)(2,1)}, bf16[1024,512]{1,0:T(8,128)(2,1)}, bf16[1024,512]{1,0:T(8,128)(2,1)}, bf16[1024,512]{1,0:T(8,128)(2,1)}, bf16...) custom-call(bf16[1024,512]{1,0:T(8,128)(2,1)} %v_ref.3, ...), custom_call_target="tpu_custom_call" | custom-call | flops 1610612736 | bytes 27787776 | tf_op jit(solution)/shard_map/b/pallas_call | solution.py:470
  62.5 1.6 %collective-permute-start.9 = (bf16[128,128]{1,0:T(8,128)(2,1)S(1)}, bf16[128,128]{1,0:T(8,128)(2,1)S(1)}, u32[]{:S(2)}, u32[]{:S(2)}) collective-permute-start(bf16[128,128]{1,0:T(8,128)(2,1)S(1)} %get-tuple-element.114), channel_id=1, source_target_pairs={{0,8},{8,16},{16,24},{24,0},{32,40},{40,48},{48,56},{56,32},{64,72... | collective-permute-start | bytes 98312 | tf_op jit(solution)/shard_map/ppermute | solution.py:450
  64.1 2.5 %collective-permute-start.10 = (bf16[128,128]{1,0:T(8,128)(2,1)S(1)}, bf16[128,128]{1,0:T(8,128)(2,1)S(1)}, u32[]{:S(2)}, u32[]{:S(2)}) collective-permute-start(bf16[128,128]{1,0:T(8,128)(2,1)S(1)} %get-tuple-element.115), channel_id=1, source_target_pairs={{0,16},{8,24},{16,0},{24,8},{32,48},{40,56},{48,32},{56,40},{64,80... | collective-permute-start | bytes 98312 | tf_op jit(solution)/shard_map/ppermute | solution.py:450
  66.6 0.6 collective-permute-start.11
  67.2 3.9 %c0.1.kk_ref = bf16[1024,512]{1,0:T(8,128)(2,1)} custom-call(f32[1024,512]{1,0:T(8,128)} %get-tuple-element.80.g_ref, bf16[1024,512]{1,0:T(8,128)(2,1)} %get-tuple-element.88.qd_ref, bf16[1024,512]{1,0:T(8,128)(2,1)} %get-tuple-element.109.u_ref, bf16[1024,512]{1,0:T(8,128)(2,1)} %get-tuple-element.110.do_ref), custom_call_target="tpu_custom_call" | custom-call | flops 268435456 | bytes 6291456 | tf_op jit(solution)/shard_map/c0/pallas_call | solution.py:470
  71.3 2.7 %collective-permute-start.14 = (bf16[128,128]{1,0:T(8,128)(2,1)S(1)}, bf16[128,128]{1,0:T(8,128)(2,1)S(1)}, u32[]{:S(2)}, u32[]{:S(2)}) collective-permute-start(bf16[128,128]{1,0:T(8,128)(2,1)S(1)} %get-tuple-element.131.p0), channel_id=1, source_target_pairs={{0,96},{8,104},{16,112},{24,120},{32,0},{40,8},{48,16},{56,24},{64... | collective-permute-start | bytes 98312 | tf_op jit(solution)/shard_map/ppermute | solution.py:450
  74.0 0.8 collective-permute-start.13
  74.8 0.9 collective-permute-start.12
  75.7 3.7 %c1.2 = (bf16[1024,512]{1,0:T(8,128)(2,1)}, f32[1024,512]{1,0:T(8,128)}) custom-call(bf16[1024,512]{1,0:T(8,128)(2,1)} %q_ref.5, f32[1024,512]{1,0:T(8,128)} %get-tuple-element.80.g_ref, bf16[1024,512]{1,0:T(8,128)(2,1)} %get-tuple-element.81.ki_ref, bf16[1024,512]{1,0:T(8,128)(2,1)} %get-tuple-element.109.u_ref, ...), custom_call_target="tpu_custom_call" | custom-call | flops 268435456 | bytes 11534336 | tf_op jit(solution)/shard_map/c1/pallas_call | solution.py:470
  80.0 1.0 r2.1
  80.9 0.7 collective-permute-start.15
  81.6 2.0 %collective-permute-start.16 = (bf16[128,128]{1,0:T(8,128)(2,1)S(1)}, bf16[128,128]{1,0:T(8,128)(2,1)S(1)}, u32[]{:S(2)}, u32[]{:S(2)}) collective-permute-start(bf16[128,128]{1,0:T(8,128)(2,1)S(1)} %get-tuple-element.140), channel_id=1, source_target_pairs={{0,16},{8,24},{16,0},{24,8},{32,48},{40,56},{48,32},{56,40},{64,80... | collective-permute-start | bytes 98312 | tf_op jit(solution)/shard_map/ppermute | solution.py:450
  83.6 0.7 collective-permute-start.17
  84.3 3.7 %c1.3 = (bf16[1024,512]{1,0:T(8,128)(2,1)}, f32[1024,512]{1,0:T(8,128)}) custom-call(bf16[1024,512]{1,0:T(8,128)(2,1)} %q_ref.5, f32[1024,512]{1,0:T(8,128)} %get-tuple-element.80.g_ref, bf16[1024,512]{1,0:T(8,128)(2,1)} %get-tuple-element.81.ki_ref, bf16[1024,512]{1,0:T(8,128)(2,1)} %get-tuple-element.109.u_ref, ...), custom_call_target="tpu_custom_call", output_to_operand_aliasing={{0}: (6, {}), {1}: (7, {})} | custom-call | flops 268435456 | bytes 11534336 | tf_op jit(solution)/shard_map/c1/pallas_call | solution.py:470
  88.0 11.3 %c2.1 = (bf16[1024,512]{1,0:T(8,128)(2,1)}, bf16[1024,512]{1,0:T(8,128)(2,1)}, f32[1024,512]{1,0:T(8,128)}, f32[4,1024]{1,0:T(4,128)}) custom-call(s32[1]{0:T(128)S(6)} %copy.21.resets, bf16[1024,512]{1,0:T(8,128)(2,1)} %k_ref.5, f32[1024,512]{1,0:T(8,128)} %get-tuple-element.80.g_ref, f32[4,1024]{1,0:T(4,128)S(1)} %copy-done.2, ...), custom_call_target="tpu_custom_call" | custom-call | flops 1342177280 | bytes 21659652 | tf_op jit(solution)/shard_map/c2/pallas_call | solution.py:470
  (28 shorter events, 1.5 us)
Async XLA Ops:
  7.2 40.5 %all-gather.2.cloned.1.call-start = ((), (), s32[]{:S(2)}) async-start(), calls=%async_computation | async-start | bytes 5308416 | tf_op jit(solution)/shard_map/all_gather | solution.py:494
  18.7 11.9 %collective-permute-start = (bf16[256,128]{1,0:T(8,128)(2,1)}, bf16[256,128]{1,0:T(8,128)(2,1)S(1)}, u32[]{:S(2)}, u32[]{:S(2)}) collective-permute-start(bf16[256,128]{1,0:T(8,128)(2,1)} %get-tuple-element.84), channel_id=1, source_target_pairs={{0,8},{8,16},{16,24},{24,0},{32,40},{40,48},{48,56},{56,32},{64,72... | collective-permute-start | bytes 196616 | tf_op jit(solution)/shard_map/ppermute | solution.py:450
  20.8 9.9 %collective-permute-start.1 = (bf16[256,128]{1,0:T(8,128)(2,1)}, bf16[256,128]{1,0:T(8,128)(2,1)S(1)}, u32[]{:S(2)}, u32[]{:S(2)}) collective-permute-start(bf16[256,128]{1,0:T(8,128)(2,1)} %get-tuple-element.85), channel_id=1, source_target_pairs={{0,16},{8,24},{16,0},{24,8},{32,48},{40,56},{48,32},{56,40},{64,80... | collective-permute-start | bytes 196616 | tf_op jit(solution)/shard_map/ppermute | solution.py:450
  24.4 6.3 %collective-permute-start.2 = (bf16[256,128]{1,0:T(8,128)(2,1)}, bf16[256,128]{1,0:T(8,128)(2,1)S(1)}, u32[]{:S(2)}, u32[]{:S(2)}) collective-permute-start(bf16[256,128]{1,0:T(8,128)(2,1)} %get-tuple-element.86), channel_id=1, source_target_pairs={{0,24},{8,0},{16,8},{24,16},{32,56},{40,32},{48,40},{56,48},{64,88... | collective-permute-start | bytes 196616 | tf_op jit(solution)/shard_map/ppermute | solution.py:450
  25.4 5.3 %copy-start.1 = (bf16[256,128]{1,0:T(8,128)(2,1)S(1)}, bf16[256,128]{1,0:T(8,128)(2,1)}, u32[]{:S(2)}) copy-start(bf16[256,128]{1,0:T(8,128)(2,1)} %get-tuple-element.94.p0) | copy-start | bytes 196612
  25.4 22.3 %copy-start = (bf16[16,64,256]{2,1,0:T(8,128)(2,1)S(1)}, bf16[16,64,256]{2,1,0:T(8,128)(2,1)}, u32[]{:S(2)}) copy-start(bf16[16,64,256]{2,1,0:T(8,128)(2,1)} %get-tuple-element.90.wb_ref) | copy-start | bytes 1572868
  25.4 22.3 %copy-start.3 = (f32[128]{0:T(128)S(1)}, f32[128]{0:T(128)}, u32[]{:S(2)}) copy-start(f32[128]{0:T(128)} %param.18) | copy-start | bytes 1540
  31.1 5.0 %collective-permute-start.5 = (bf16[256,128]{1,0:T(8,128)(2,1)S(1)}, bf16[256,128]{1,0:T(8,128)(2,1)S(1)}, u32[]{:S(2)}, u32[]{:S(2)}) collective-permute-start(bf16[256,128]{1,0:T(8,128)(2,1)S(1)} %get-tuple-element.100.p0), channel_id=1, source_target_pairs={{0,96},{8,104},{16,112},{24,120},{32,0},{40,8},{48,16},{56,24},{64... | collective-permute-start | bytes 196616 | tf_op jit(solution)/shard_map/ppermute | solution.py:450
  34.2 5.8 %collective-permute-start.4 = (bf16[256,128]{1,0:T(8,128)(2,1)S(1)}, bf16[256,128]{1,0:T(8,128)(2,1)S(1)}, u32[]{:S(2)}, u32[]{:S(2)}) collective-permute-start(bf16[256,128]{1,0:T(8,128)(2,1)S(1)} %get-tuple-element.100.p0), channel_id=1, source_target_pairs={{0,64},{8,72},{16,80},{24,88},{32,96},{40,104},{48,112},{56,120},{... | collective-permute-start | bytes 196616 | tf_op jit(solution)/shard_map/ppermute | solution.py:450
  34.8 5.8 %collective-permute-start.3 = (bf16[256,128]{1,0:T(8,128)(2,1)S(1)}, bf16[256,128]{1,0:T(8,128)(2,1)S(1)}, u32[]{:S(2)}, u32[]{:S(2)}) collective-permute-start(bf16[256,128]{1,0:T(8,128)(2,1)S(1)} %get-tuple-element.100.p0), channel_id=1, source_target_pairs={{0,32},{8,40},{16,48},{24,56},{32,64},{40,72},{48,80},{56,88},{64,... | collective-permute-start | bytes 196616 | tf_op jit(solution)/shard_map/ppermute | solution.py:450
  41.1 5.2 %collective-permute-start.6 = (bf16[128,128]{1,0:T(8,128)(2,1)S(1)}, bf16[128,128]{1,0:T(8,128)(2,1)S(1)}, u32[]{:S(2)}, u32[]{:S(2)}) collective-permute-start(bf16[128,128]{1,0:T(8,128)(2,1)S(1)} %get-tuple-element.106), channel_id=1, source_target_pairs={{0,8},{8,16},{16,24},{24,0},{32,40},{40,48},{48,56},{56,32},{64,72... | collective-permute-start | bytes 98312 | tf_op jit(solution)/shard_map/ppermute | solution.py:450
  42.2 5.4 %collective-permute-start.7 = (bf16[128,128]{1,0:T(8,128)(2,1)S(1)}, bf16[128,128]{1,0:T(8,128)(2,1)S(1)}, u32[]{:S(2)}, u32[]{:S(2)}) collective-permute-start(bf16[128,128]{1,0:T(8,128)(2,1)S(1)} %get-tuple-element.107), channel_id=1, source_target_pairs={{0,16},{8,24},{16,0},{24,8},{32,48},{40,56},{48,32},{56,40},{64,80... | collective-permute-start | bytes 98312 | tf_op jit(solution)/shard_map/ppermute | solution.py:450
  43.1 4.6 %collective-permute-start.8 = (bf16[128,128]{1,0:T(8,128)(2,1)S(1)}, bf16[128,128]{1,0:T(8,128)(2,1)S(1)}, u32[]{:S(2)}, u32[]{:S(2)}) collective-permute-start(bf16[128,128]{1,0:T(8,128)(2,1)S(1)} %get-tuple-element.108), channel_id=1, source_target_pairs={{0,24},{8,0},{16,8},{24,16},{32,56},{40,32},{48,40},{56,48},{64,88... | collective-permute-start | bytes 98312 | tf_op jit(solution)/shard_map/ppermute | solution.py:450
  62.5 8.6 %collective-permute-start.9 = (bf16[128,128]{1,0:T(8,128)(2,1)S(1)}, bf16[128,128]{1,0:T(8,128)(2,1)S(1)}, u32[]{:S(2)}, u32[]{:S(2)}) collective-permute-start(bf16[128,128]{1,0:T(8,128)(2,1)S(1)} %get-tuple-element.114), channel_id=1, source_target_pairs={{0,8},{8,16},{16,24},{24,0},{32,40},{40,48},{48,56},{56,32},{64,72... | collective-permute-start | bytes 98312 | tf_op jit(solution)/shard_map/ppermute | solution.py:450
  64.1 7.0 %collective-permute-start.10 = (bf16[128,128]{1,0:T(8,128)(2,1)S(1)}, bf16[128,128]{1,0:T(8,128)(2,1)S(1)}, u32[]{:S(2)}, u32[]{:S(2)}) collective-permute-start(bf16[128,128]{1,0:T(8,128)(2,1)S(1)} %get-tuple-element.115), channel_id=1, source_target_pairs={{0,16},{8,24},{16,0},{24,8},{32,48},{40,56},{48,32},{56,40},{64,80... | collective-permute-start | bytes 98312 | tf_op jit(solution)/shard_map/ppermute | solution.py:450
  66.6 4.6 %collective-permute-start.11 = (bf16[128,128]{1,0:T(8,128)(2,1)S(1)}, bf16[128,128]{1,0:T(8,128)(2,1)S(1)}, u32[]{:S(2)}, u32[]{:S(2)}) collective-permute-start(bf16[128,128]{1,0:T(8,128)(2,1)S(1)} %get-tuple-element.116), channel_id=1, source_target_pairs={{0,24},{8,0},{16,8},{24,16},{32,56},{40,32},{48,40},{56,48},{64,88... | collective-permute-start | bytes 98312 | tf_op jit(solution)/shard_map/ppermute | solution.py:450
  71.3 8.4 %collective-permute-start.14 = (bf16[128,128]{1,0:T(8,128)(2,1)S(1)}, bf16[128,128]{1,0:T(8,128)(2,1)S(1)}, u32[]{:S(2)}, u32[]{:S(2)}) collective-permute-start(bf16[128,128]{1,0:T(8,128)(2,1)S(1)} %get-tuple-element.131.p0), channel_id=1, source_target_pairs={{0,96},{8,104},{16,112},{24,120},{32,0},{40,8},{48,16},{56,24},{64... | collective-permute-start | bytes 98312 | tf_op jit(solution)/shard_map/ppermute | solution.py:450
  74.0 5.7 %collective-permute-start.13 = (bf16[128,128]{1,0:T(8,128)(2,1)S(1)}, bf16[128,128]{1,0:T(8,128)(2,1)S(1)}, u32[]{:S(2)}, u32[]{:S(2)}) collective-permute-start(bf16[128,128]{1,0:T(8,128)(2,1)S(1)} %get-tuple-element.131.p0), channel_id=1, source_target_pairs={{0,64},{8,72},{16,80},{24,88},{32,96},{40,104},{48,112},{56,120},{... | collective-permute-start | bytes 98312 | tf_op jit(solution)/shard_map/ppermute | solution.py:450
  74.8 5.1 %collective-permute-start.12 = (bf16[128,128]{1,0:T(8,128)(2,1)S(1)}, bf16[128,128]{1,0:T(8,128)(2,1)S(1)}, u32[]{:S(2)}, u32[]{:S(2)}) collective-permute-start(bf16[128,128]{1,0:T(8,128)(2,1)S(1)} %get-tuple-element.131.p0), channel_id=1, source_target_pairs={{0,32},{8,40},{16,48},{24,56},{32,64},{40,72},{48,80},{56,88},{64,... | collective-permute-start | bytes 98312 | tf_op jit(solution)/shard_map/ppermute | solution.py:450
  80.9 7.1 %collective-permute-start.15 = (bf16[128,128]{1,0:T(8,128)(2,1)S(1)}, bf16[128,128]{1,0:T(8,128)(2,1)S(1)}, u32[]{:S(2)}, u32[]{:S(2)}) collective-permute-start(bf16[128,128]{1,0:T(8,128)(2,1)S(1)} %get-tuple-element.139), channel_id=1, source_target_pairs={{0,8},{8,16},{16,24},{24,0},{32,40},{40,48},{48,56},{56,32},{64,72... | collective-permute-start | bytes 98312 | tf_op jit(solution)/shard_map/ppermute | solution.py:450
  81.6 6.4 %collective-permute-start.16 = (bf16[128,128]{1,0:T(8,128)(2,1)S(1)}, bf16[128,128]{1,0:T(8,128)(2,1)S(1)}, u32[]{:S(2)}, u32[]{:S(2)}) collective-permute-start(bf16[128,128]{1,0:T(8,128)(2,1)S(1)} %get-tuple-element.140), channel_id=1, source_target_pairs={{0,16},{8,24},{16,0},{24,8},{32,48},{40,56},{48,32},{56,40},{64,80... | collective-permute-start | bytes 98312 | tf_op jit(solution)/shard_map/ppermute | solution.py:450
  83.6 4.4 %collective-permute-start.17 = (bf16[128,128]{1,0:T(8,128)(2,1)S(1)}, bf16[128,128]{1,0:T(8,128)(2,1)S(1)}, u32[]{:S(2)}, u32[]{:S(2)}) collective-permute-start(bf16[128,128]{1,0:T(8,128)(2,1)S(1)} %get-tuple-element.141), channel_id=1, source_target_pairs={{0,24},{8,0},{16,8},{24,16},{32,56},{40,32},{48,40},{56,48},{64,88... | collective-permute-start | bytes 98312 | tf_op jit(solution)/shard_map/ppermute | solution.py:450
  84.3 3.7 %copy-start.2 = (f32[4,1024]{1,0:T(4,128)S(1)}, f32[4,1024]{1,0:T(4,128)}, u32[]{:S(2)}) copy-start(f32[4,1024]{1,0:T(4,128)} %b_ref.3) | copy-start | bytes 49156
Sparse Core Ops, SparseCore 0:
  9.7 36.7 all-gather.1

commit v6 on v5

--- a/solution.py
+++ b/solution.py
@@ -55,6 +55,10 @@
 
 def cols(h):
     return slice(128 * h, 128 * h + 128)
+
+
+def wide(h):
+    return slice(128 * h, 128 * h + 256)
 
 
 def half(h):
@@ -280,7 +284,7 @@
         )
         for (c, h), dq, prod in zip(group, dqs, prods):
             dq_ref[half(c), cols(h)] = dq
-            pq_ref[half(c), cols(h)] = prod * SCALE
+            pq_ref[half(c), cols(h)] = (prod * SCALE).astype(bf16)
 
 
 def kernel_c0(heads, g_ref, qd_ref, u_ref, do_ref, kk_ref):
@@ -318,24 +322,30 @@
         for h in range(heads):
             grads[c, h] = now[h]
             gbs[c, h] = now[h].astype(bf16)
+        moved = split([
+            nt(lanes(gbs[c, h], gbs[c, h + 1]), diag(n_ref[c, h], n_ref[c, h + 1])) for h in range(0, heads, 2)
+        ])
         for h in range(heads):
             lam = jnp.exp(g_ref[64 * c + 63 : 64 * c + 64, cols(h)])
-            now[h] = keep * (dt_ref[c, h].astype(f32) + lam * now[h] - nt(gbs[c, h], n_ref[c, h]))
+            now[h] = keep * (dt_ref[c, h].astype(f32) + lam * now[h] - moved[h])
     for h in range(heads):
         state[h] = now[h]
     for group in reversed(units(heads, "c2")):
-        gb = [gbs[p] for p in group]
-        dus = [
-            (du_ref[half(c), cols(h)].astype(f32) + nt(kt_ref[half(c), cols(h)], x)).astype(bf16)
-            for x, (c, h) in zip(gb, group)
-        ]
+        firsts = list(enumerate(group))[::2]
+        both = [diag(gbs[c, h], gbs[c, h + 1]) for _, (c, h) in firsts]
+        dus = split([
+            (du_ref[half(c), wide(h)].astype(f32) + nt(kt_ref[half(c), wide(h)], x)).astype(bf16)
+            for x, (_, (c, h)) in zip(both, firsts)
+        ])
         dvs = [tn(wb_ref[c, :, half(h)], du) for du, (c, h) in zip(dus, group)]
         dvbs = each(lambda x: x.astype(bf16), dvs)
         gs = [g_ref[half(c), cols(h)] for c, h in group]
-        ktts = [
-            nn(u_ref[half(c), cols(h)], x) * jnp.exp(g[63:64, :] - g) for x, g, (c, h) in zip(gb, gs, group)
-        ]
-        kdds = [nn(dvb, e_ref[c, h]) * jnp.exp(g) for dvb, g, (c, h) in zip(dvbs, gs, group)]
+        ktts = split([nn(u_ref[half(c), wide(h)], x) for x, (_, (c, h)) in zip(both, firsts)])
+        ktts = each(lambda x, g: x * jnp.exp(g[63:64, :] - g), ktts, gs)
+        kdds = split([
+            nn(lanes(dvbs[i], dvbs[i + 1]), diag(e_ref[c, h], e_ref[c, h + 1])) for i, (c, h) in firsts
+        ])
+        kdds = each(lambda x, g: x * jnp.exp(g), kdds, gs)
         ks = [k_ref[half(c), cols(h)].astype(f32) for c, h in group]
         rks = each(inverse_norm, ks)
         kus = each(lambda k, rk: k * rk, ks, rks)
@@ -347,14 +357,15 @@
         )
         kutts = each(lambda ku, ktt: ku * ktt, kus, ktts)
         dgams = [
-            pq_ref[half(c), cols(h)] - ku * (x + kdd) for ku, kdd, x, (c, h) in zip(kus, kdds, sums, group)
+            pq_ref[half(c), cols(h)].astype(f32) - ku * (x + kdd) for ku, kdd, x, (c, h) in zip(kus, kdds, sums, group)
         ]
         dlasts = [
             jnp.sum(kutt, axis=0, keepdims=True)
             + jnp.exp(g[63:64, :]) * jnp.sum(grads[c, h] * e_ref[c, h].astype(f32), axis=0, keepdims=True)
             for kutt, g, (c, h) in zip(kutts, gs, group)
         ]
-        dds = each(lambda dgam, dlast: sum_rows(weights, dgam) + dlast, dgams, dlasts)
+        dds = split([sum_rows(weights, lanes(dgams[i], dgams[i + 1])) for i, _ in firsts])
+        dds = each(lambda x, dlast: x + dlast, dds, dlasts)
         dbs = [
             nt(ones, (dv * vp_ref[half(c), cols(h)].astype(f32)).astype(bf16))[0:1]
             for dv, (c, h) in zip(dvs, group)
@@ -583,7 +594,7 @@
         return call(
             kernel_c1, "c1", heads,
             [tok] * 5 + [state] + [pl.BlockSpec(memory_space=pl.ANY)] * len(into),
-            [tok, tok], [tok_b, tok_f],
+            [tok, tok], [tok_b, tok_b],
             [], (steps,), 2 * unit, queries, gamma, ki, u, do, e, into=into,
         )
 

time: 106 us -> 106 us (level)
  transfers between devices with their start and end apart: 19 -> 19, of which waited for: 5 -> 5; matrix products, arithmetic and copies ran while one was open for 0% -> 0% of each run, Pallas kernels for 27% -> 26%
where the time goes in v6:
time: 106 us
  Pallas kernels  55.1 us (52%)
  starting transfers between devices  27.7 us (26%)
  between operations  14.8 us (14%)
  waiting for transfers between devices  8.28 us (8%)
    pallas_call x13, Pallas kernels, call(): pl.pallas_call(functools.partial(body, heads), out_shape=out_shape, grid=...  55.1 us
    ppermute x18, starting transfers between devices, permute(): return lax.ppermute(x, 'seq', pairs)  27.7 us
    ppermute x18, waiting for transfers between devices, permute(): return lax.ppermute(x, 'seq', pairs)  7.59 us
  transfers between devices with their start and end apart: 19, of which 5 were waited for; matrix products, arithmetic and copies ran while one was open for 0% of the time, Pallas kernels for 26%

profile of v6, /device:TPU:0, one launch (start us, length us, event | category | flops | bytes accessed | tf_op | source)
XLA Modules:
  0.0 106.0 jit_solution(14269448173740014890)
XLA Ops:
  7.2 0.7 all-gather.2.cloned.1.call-update
  8.5 10.2 %a1.1 = (f32[1024,512]{1,0:T(8,128)}, bf16[16,64,256]{2,1,0:T(8,128)(2,1)}, bf16[1024,512]{1,0:T(8,128)(2,1)}, bf16[1024,512]{1,0:T(8,128)(2,1)}, bf16[1024,512]...) custom-call(s32[1]{0:T(128)S(6)} %copy.21.resets, ...), custom_call_target="tpu_custom_call" | custom-call | flops 1073741824 | bytes 17580036 | tf_op jit(solution)/shard_map/a1/pallas_call | solution.py:481
  18.7 2.1 %collective-permute-start = (bf16[256,128]{1,0:T(8,128)(2,1)}, bf16[256,128]{1,0:T(8,128)(2,1)S(1)}, u32[]{:S(2)}, u32[]{:S(2)}) collective-permute-start(bf16[256,128]{1,0:T(8,128)(2,1)} %get-tuple-element.84), channel_id=1, source_target_pairs={{0,8},{8,16},{16,24},{24,0},{32,40},{40,48},{48,56},{56,32},{64,72... | collective-permute-start | bytes 196616 | tf_op jit(solution)/shard_map/ppermute | solution.py:461
  20.8 3.6 %collective-permute-start.1 = (bf16[256,128]{1,0:T(8,128)(2,1)}, bf16[256,128]{1,0:T(8,128)(2,1)S(1)}, u32[]{:S(2)}, u32[]{:S(2)}) collective-permute-start(bf16[256,128]{1,0:T(8,128)(2,1)} %get-tuple-element.85), channel_id=1, source_target_pairs={{0,16},{8,24},{16,0},{24,8},{32,48},{40,56},{48,32},{56,40},{64,80... | collective-permute-start | bytes 196616 | tf_op jit(solution)/shard_map/ppermute | solution.py:461
  24.4 1.0 collective-permute-start.2
  25.4 5.2 %a2.1 = (bf16[1024,512]{1,0:T(8,128)(2,1)}, bf16[1024,512]{1,0:T(8,128)(2,1)}, bf16[16,64,256]{2,1,0:T(8,128)(2,1)}, bf16[16,64,256]{2,1,0:T(8,128)(2,1)}) custom-call(bf16[1024,512]{1,0:T(8,128)(2,1)} %q_ref.5, bf16[1024,512]{1,0:T(8,128)(2,1)} %k_ref.5, f32[1024,512]{1,0:T(8,128)} %get-tuple-element.80.g_ref), custom_call_target="tpu_custom_call" | custom-call | flops 268435456 | bytes 7340032 | tf_op jit(solution)/shard_map/a2/pallas_call | solution.py:481
  31.1 3.1 %collective-permute-start.5 = (bf16[256,128]{1,0:T(8,128)(2,1)S(1)}, bf16[256,128]{1,0:T(8,128)(2,1)S(1)}, u32[]{:S(2)}, u32[]{:S(2)}) collective-permute-start(bf16[256,128]{1,0:T(8,128)(2,1)S(1)} %get-tuple-element.100.p0), channel_id=1, source_target_pairs={{0,96},{8,104},{16,112},{24,120},{32,0},{40,8},{48,16},{56,24},{64... | collective-permute-start | bytes 196616 | tf_op jit(solution)/shard_map/ppermute | solution.py:461
  34.2 0.6 collective-permute-start.4
  34.8 1.0 collective-permute-start.3
  36.1 3.9 %collective-permute-done.4.p2 = bf16[256,128]{1,0:T(8,128)(2,1)S(1)} collective-permute-done((bf16[256,128]{1,0:T(8,128)(2,1)S(1)}, bf16[256,128]{1,0:T(8,128)(2,1)S(1)}, u32[]{:S(2)}, u32[]{:S(2)}) %collective-permute-start.4) | collective-permute-done | bytes 65568 | tf_op jit(solution)/shard_map/ppermute | solution.py:461
  40.0 0.7 collective-permute-done.3.p1
  40.7 0.5 f2.1
  41.1 1.1 %collective-permute-start.6 = (bf16[128,128]{1,0:T(8,128)(2,1)S(1)}, bf16[128,128]{1,0:T(8,128)(2,1)S(1)}, u32[]{:S(2)}, u32[]{:S(2)}) collective-permute-start(bf16[128,128]{1,0:T(8,128)(2,1)S(1)} %get-tuple-element.106), channel_id=1, source_target_pairs={{0,8},{8,16},{16,24},{24,0},{32,40},{40,48},{48,56},{56,32},{64,72... | collective-permute-start | bytes 98312 | tf_op jit(solution)/shard_map/ppermute | solution.py:461
  42.2 0.9 collective-permute-start.7
  43.1 1.9 %collective-permute-start.8 = (bf16[128,128]{1,0:T(8,128)(2,1)S(1)}, bf16[128,128]{1,0:T(8,128)(2,1)S(1)}, u32[]{:S(2)}, u32[]{:S(2)}) collective-permute-start(bf16[128,128]{1,0:T(8,128)(2,1)S(1)} %get-tuple-element.108), channel_id=1, source_target_pairs={{0,24},{8,0},{16,8},{24,16},{32,56},{40,32},{48,40},{56,48},{64,88... | collective-permute-start | bytes 98312 | tf_op jit(solution)/shard_map/ppermute | solution.py:461
  45.0 1.3 %collective-permute-done.6.s1 = bf16[128,128]{1,0:T(8,128)(2,1)S(1)} collective-permute-done((bf16[128,128]{1,0:T(8,128)(2,1)S(1)}, bf16[128,128]{1,0:T(8,128)(2,1)S(1)}, u32[]{:S(2)}, u32[]{:S(2)}) %collective-permute-start.6) | collective-permute-done | bytes 32800 | tf_op jit(solution)/shard_map/ppermute | solution.py:461
  46.3 1.3 %collective-permute-done.7.s2 = bf16[128,128]{1,0:T(8,128)(2,1)S(1)} collective-permute-done((bf16[128,128]{1,0:T(8,128)(2,1)S(1)}, bf16[128,128]{1,0:T(8,128)(2,1)S(1)}, u32[]{:S(2)}, u32[]{:S(2)}) %collective-permute-start.7) | collective-permute-done | bytes 32800 | tf_op jit(solution)/shard_map/ppermute | solution.py:461
  47.7 14.8 %b.1 = (bf16[16,4,128,128]{3,2,1,0:T(8,128)(2,1)}, bf16[1024,512]{1,0:T(8,128)(2,1)}, bf16[1024,512]{1,0:T(8,128)(2,1)}, bf16[1024,512]{1,0:T(8,128)(2,1)}, bf16...) custom-call(bf16[1024,512]{1,0:T(8,128)(2,1)} %v_ref.3, ...), custom_call_target="tpu_custom_call" | custom-call | flops 1610612736 | bytes 27787776 | tf_op jit(solution)/shard_map/b/pallas_call | solution.py:481
  62.5 1.6 %collective-permute-start.9 = (bf16[128,128]{1,0:T(8,128)(2,1)S(1)}, bf16[128,128]{1,0:T(8,128)(2,1)S(1)}, u32[]{:S(2)}, u32[]{:S(2)}) collective-permute-start(bf16[128,128]{1,0:T(8,128)(2,1)S(1)} %get-tuple-element.114), channel_id=1, source_target_pairs={{0,8},{8,16},{16,24},{24,0},{32,40},{40,48},{48,56},{56,32},{64,72... | collective-permute-start | bytes 98312 | tf_op jit(solution)/shard_map/ppermute | solution.py:461
  64.1 2.5 %collective-permute-start.10 = (bf16[128,128]{1,0:T(8,128)(2,1)S(1)}, bf16[128,128]{1,0:T(8,128)(2,1)S(1)}, u32[]{:S(2)}, u32[]{:S(2)}) collective-permute-start(bf16[128,128]{1,0:T(8,128)(2,1)S(1)} %get-tuple-element.115), channel_id=1, source_target_pairs={{0,16},{8,24},{16,0},{24,8},{32,48},{40,56},{48,32},{56,40},{64,80... | collective-permute-start | bytes 98312 | tf_op jit(solution)/shard_map/ppermute | solution.py:461
  66.6 0.6 collective-permute-start.11
  67.2 3.9 %c0.1.kk_ref = bf16[1024,512]{1,0:T(8,128)(2,1)} custom-call(f32[1024,512]{1,0:T(8,128)} %get-tuple-element.80.g_ref, bf16[1024,512]{1,0:T(8,128)(2,1)} %get-tuple-element.88.qd_ref, bf16[1024,512]{1,0:T(8,128)(2,1)} %get-tuple-element.109.u_ref, bf16[1024,512]{1,0:T(8,128)(2,1)} %get-tuple-element.110.do_ref), custom_call_target="tpu_custom_call" | custom-call | flops 268435456 | bytes 6291456 | tf_op jit(solution)/shard_map/c0/pallas_call | solution.py:481
  71.3 2.7 %collective-permute-start.14 = (bf16[128,128]{1,0:T(8,128)(2,1)S(1)}, bf16[128,128]{1,0:T(8,128)(2,1)S(1)}, u32[]{:S(2)}, u32[]{:S(2)}) collective-permute-start(bf16[128,128]{1,0:T(8,128)(2,1)S(1)} %get-tuple-element.131.p0), channel_id=1, source_target_pairs={{0,96},{8,104},{16,112},{24,120},{32,0},{40,8},{48,16},{56,24},{64... | collective-permute-start | bytes 98312 | tf_op jit(solution)/shard_map/ppermute | solution.py:461
  74.0 0.8 collective-permute-start.13
  74.9 0.9 collective-permute-start.12
  75.7 3.6 %c1.2 = (bf16[1024,512]{1,0:T(8,128)(2,1)}, bf16[1024,512]{1,0:T(8,128)(2,1)}) custom-call(bf16[1024,512]{1,0:T(8,128)(2,1)} %q_ref.5, f32[1024,512]{1,0:T(8,128)} %get-tuple-element.80.g_ref, bf16[1024,512]{1,0:T(8,128)(2,1)} %get-tuple-element.81.ki_ref, bf16[1024,512]{1,0:T(8,128)(2,1)} %get-tuple-element.109.u_ref, ...), custom_call_target="tpu_custom_call" | custom-call | flops 268435456 | bytes 10485760 | tf_op jit(solution)/shard_map/c1/pallas_call | solution.py:481
  80.0 1.0 r2.1
  80.9 0.7 collective-permute-start.15
  81.6 2.0 %collective-permute-start.16 = (bf16[128,128]{1,0:T(8,128)(2,1)S(1)}, bf16[128,128]{1,0:T(8,128)(2,1)S(1)}, u32[]{:S(2)}, u32[]{:S(2)}) collective-permute-start(bf16[128,128]{1,0:T(8,128)(2,1)S(1)} %get-tuple-element.140), channel_id=1, source_target_pairs={{0,16},{8,24},{16,0},{24,8},{32,48},{40,56},{48,32},{56,40},{64,80... | collective-permute-start | bytes 98312 | tf_op jit(solution)/shard_map/ppermute | solution.py:461
  83.6 0.7 collective-permute-start.17
  84.3 3.6 %c1.3 = (bf16[1024,512]{1,0:T(8,128)(2,1)}, bf16[1024,512]{1,0:T(8,128)(2,1)}) custom-call(bf16[1024,512]{1,0:T(8,128)(2,1)} %q_ref.5, f32[1024,512]{1,0:T(8,128)} %get-tuple-element.80.g_ref, bf16[1024,512]{1,0:T(8,128)(2,1)} %get-tuple-element.81.ki_ref, bf16[1024,512]{1,0:T(8,128)(2,1)} %get-tuple-element.109.u_ref, ...), custom_call_target="tpu_custom_call", output_to_operand_aliasing={{0}: (6, {}), {1}: (7, {})} | custom-call | flops 268435456 | bytes 10485760 | tf_op jit(solution)/shard_map/c1/pallas_call | solution.py:481
  87.9 11.2 %c2.1 = (bf16[1024,512]{1,0:T(8,128)(2,1)}, bf16[1024,512]{1,0:T(8,128)(2,1)}, f32[1024,512]{1,0:T(8,128)}, f32[4,1024]{1,0:T(4,128)}) custom-call(s32[1]{0:T(128)S(6)} %copy.21.resets, bf16[1024,512]{1,0:T(8,128)(2,1)} %k_ref.5, f32[1024,512]{1,0:T(8,128)} %get-tuple-element.80.g_ref, f32[4,1024]{1,0:T(4,128)S(1)} %copy-done.2, ...), custom_call_target="tpu_custom_call" | custom-call | flops 1342177280 | bytes 20611076 | tf_op jit(solution)/shard_map/c2/pallas_call | solution.py:481
  (28 shorter events, 1.6 us)
Async XLA Ops:
  7.2 40.5 %all-gather.2.cloned.1.call-start = ((), (), s32[]{:S(2)}) async-start(), calls=%async_computation | async-start | bytes 5308416 | tf_op jit(solution)/shard_map/all_gather | solution.py:505
  18.7 11.9 %collective-permute-start = (bf16[256,128]{1,0:T(8,128)(2,1)}, bf16[256,128]{1,0:T(8,128)(2,1)S(1)}, u32[]{:S(2)}, u32[]{:S(2)}) collective-permute-start(bf16[256,128]{1,0:T(8,128)(2,1)} %get-tuple-element.84), channel_id=1, source_target_pairs={{0,8},{8,16},{16,24},{24,0},{32,40},{40,48},{48,56},{56,32},{64,72... | collective-permute-start | bytes 196616 | tf_op jit(solution)/shard_map/ppermute | solution.py:461
  20.8 9.9 %collective-permute-start.1 = (bf16[256,128]{1,0:T(8,128)(2,1)}, bf16[256,128]{1,0:T(8,128)(2,1)S(1)}, u32[]{:S(2)}, u32[]{:S(2)}) collective-permute-start(bf16[256,128]{1,0:T(8,128)(2,1)} %get-tuple-element.85), channel_id=1, source_target_pairs={{0,16},{8,24},{16,0},{24,8},{32,48},{40,56},{48,32},{56,40},{64,80... | collective-permute-start | bytes 196616 | tf_op jit(solution)/shard_map/ppermute | solution.py:461
  24.4 6.3 %collective-permute-start.2 = (bf16[256,128]{1,0:T(8,128)(2,1)}, bf16[256,128]{1,0:T(8,128)(2,1)S(1)}, u32[]{:S(2)}, u32[]{:S(2)}) collective-permute-start(bf16[256,128]{1,0:T(8,128)(2,1)} %get-tuple-element.86), channel_id=1, source_target_pairs={{0,24},{8,0},{16,8},{24,16},{32,56},{40,32},{48,40},{56,48},{64,88... | collective-permute-start | bytes 196616 | tf_op jit(solution)/shard_map/ppermute | solution.py:461
  25.4 5.3 %copy-start.1 = (bf16[256,128]{1,0:T(8,128)(2,1)S(1)}, bf16[256,128]{1,0:T(8,128)(2,1)}, u32[]{:S(2)}) copy-start(bf16[256,128]{1,0:T(8,128)(2,1)} %get-tuple-element.94.p0) | copy-start | bytes 196612
  25.4 22.3 %copy-start = (bf16[16,64,256]{2,1,0:T(8,128)(2,1)S(1)}, bf16[16,64,256]{2,1,0:T(8,128)(2,1)}, u32[]{:S(2)}) copy-start(bf16[16,64,256]{2,1,0:T(8,128)(2,1)} %get-tuple-element.90.wb_ref) | copy-start | bytes 1572868
  25.4 22.3 %copy-start.3 = (f32[128]{0:T(128)S(1)}, f32[128]{0:T(128)}, u32[]{:S(2)}) copy-start(f32[128]{0:T(128)} %param.18) | copy-start | bytes 1540
  31.1 5.0 %collective-permute-start.5 = (bf16[256,128]{1,0:T(8,128)(2,1)S(1)}, bf16[256,128]{1,0:T(8,128)(2,1)S(1)}, u32[]{:S(2)}, u32[]{:S(2)}) collective-permute-start(bf16[256,128]{1,0:T(8,128)(2,1)S(1)} %get-tuple-element.100.p0), channel_id=1, source_target_pairs={{0,96},{8,104},{16,112},{24,120},{32,0},{40,8},{48,16},{56,24},{64... | collective-permute-start | bytes 196616 | tf_op jit(solution)/shard_map/ppermute | solution.py:461
  34.2 5.8 %collective-permute-start.4 = (bf16[256,128]{1,0:T(8,128)(2,1)S(1)}, bf16[256,128]{1,0:T(8,128)(2,1)S(1)}, u32[]{:S(2)}, u32[]{:S(2)}) collective-permute-start(bf16[256,128]{1,0:T(8,128)(2,1)S(1)} %get-tuple-element.100.p0), channel_id=1, source_target_pairs={{0,64},{8,72},{16,80},{24,88},{32,96},{40,104},{48,112},{56,120},{... | collective-permute-start | bytes 196616 | tf_op jit(solution)/shard_map/ppermute | solution.py:461
  34.8 5.8 %collective-permute-start.3 = (bf16[256,128]{1,0:T(8,128)(2,1)S(1)}, bf16[256,128]{1,0:T(8,128)(2,1)S(1)}, u32[]{:S(2)}, u32[]{:S(2)}) collective-permute-start(bf16[256,128]{1,0:T(8,128)(2,1)S(1)} %get-tuple-element.100.p0), channel_id=1, source_target_pairs={{0,32},{8,40},{16,48},{24,56},{32,64},{40,72},{48,80},{56,88},{64,... | collective-permute-start | bytes 196616 | tf_op jit(solution)/shard_map/ppermute | solution.py:461
  41.1 5.2 %collective-permute-start.6 = (bf16[128,128]{1,0:T(8,128)(2,1)S(1)}, bf16[128,128]{1,0:T(8,128)(2,1)S(1)}, u32[]{:S(2)}, u32[]{:S(2)}) collective-permute-start(bf16[128,128]{1,0:T(8,128)(2,1)S(1)} %get-tuple-element.106), channel_id=1, source_target_pairs={{0,8},{8,16},{16,24},{24,0},{32,40},{40,48},{48,56},{56,32},{64,72... | collective-permute-start | bytes 98312 | tf_op jit(solution)/shard_map/ppermute | solution.py:461
  42.2 5.4 %collective-permute-start.7 = (bf16[128,128]{1,0:T(8,128)(2,1)S(1)}, bf16[128,128]{1,0:T(8,128)(2,1)S(1)}, u32[]{:S(2)}, u32[]{:S(2)}) collective-permute-start(bf16[128,128]{1,0:T(8,128)(2,1)S(1)} %get-tuple-element.107), channel_id=1, source_target_pairs={{0,16},{8,24},{16,0},{24,8},{32,48},{40,56},{48,32},{56,40},{64,80... | collective-permute-start | bytes 98312 | tf_op jit(solution)/shard_map/ppermute | solution.py:461
  43.1 4.6 %collective-permute-start.8 = (bf16[128,128]{1,0:T(8,128)(2,1)S(1)}, bf16[128,128]{1,0:T(8,128)(2,1)S(1)}, u32[]{:S(2)}, u32[]{:S(2)}) collective-permute-start(bf16[128,128]{1,0:T(8,128)(2,1)S(1)} %get-tuple-element.108), channel_id=1, source_target_pairs={{0,24},{8,0},{16,8},{24,16},{32,56},{40,32},{48,40},{56,48},{64,88... | collective-permute-start | bytes 98312 | tf_op jit(solution)/shard_map/ppermute | solution.py:461
  62.5 8.6 %collective-permute-start.9 = (bf16[128,128]{1,0:T(8,128)(2,1)S(1)}, bf16[128,128]{1,0:T(8,128)(2,1)S(1)}, u32[]{:S(2)}, u32[]{:S(2)}) collective-permute-start(bf16[128,128]{1,0:T(8,128)(2,1)S(1)} %get-tuple-element.114), channel_id=1, source_target_pairs={{0,8},{8,16},{16,24},{24,0},{32,40},{40,48},{48,56},{56,32},{64,72... | collective-permute-start | bytes 98312 | tf_op jit(solution)/shard_map/ppermute | solution.py:461
  64.1 7.0 %collective-permute-start.10 = (bf16[128,128]{1,0:T(8,128)(2,1)S(1)}, bf16[128,128]{1,0:T(8,128)(2,1)S(1)}, u32[]{:S(2)}, u32[]{:S(2)}) collective-permute-start(bf16[128,128]{1,0:T(8,128)(2,1)S(1)} %get-tuple-element.115), channel_id=1, source_target_pairs={{0,16},{8,24},{16,0},{24,8},{32,48},{40,56},{48,32},{56,40},{64,80... | collective-permute-start | bytes 98312 | tf_op jit(solution)/shard_map/ppermute | solution.py:461
  66.6 4.6 %collective-permute-start.11 = (bf16[128,128]{1,0:T(8,128)(2,1)S(1)}, bf16[128,128]{1,0:T(8,128)(2,1)S(1)}, u32[]{:S(2)}, u32[]{:S(2)}) collective-permute-start(bf16[128,128]{1,0:T(8,128)(2,1)S(1)} %get-tuple-element.116), channel_id=1, source_target_pairs={{0,24},{8,0},{16,8},{24,16},{32,56},{40,32},{48,40},{56,48},{64,88... | collective-permute-start | bytes 98312 | tf_op jit(solution)/shard_map/ppermute | solution.py:461
  71.3 8.3 %collective-permute-start.14 = (bf16[128,128]{1,0:T(8,128)(2,1)S(1)}, bf16[128,128]{1,0:T(8,128)(2,1)S(1)}, u32[]{:S(2)}, u32[]{:S(2)}) collective-permute-start(bf16[128,128]{1,0:T(8,128)(2,1)S(1)} %get-tuple-element.131.p0), channel_id=1, source_target_pairs={{0,96},{8,104},{16,112},{24,120},{32,0},{40,8},{48,16},{56,24},{64... | collective-permute-start | bytes 98312 | tf_op jit(solution)/shard_map/ppermute | solution.py:461
  74.0 5.6 %collective-permute-start.13 = (bf16[128,128]{1,0:T(8,128)(2,1)S(1)}, bf16[128,128]{1,0:T(8,128)(2,1)S(1)}, u32[]{:S(2)}, u32[]{:S(2)}) collective-permute-start(bf16[128,128]{1,0:T(8,128)(2,1)S(1)} %get-tuple-element.131.p0), channel_id=1, source_target_pairs={{0,64},{8,72},{16,80},{24,88},{32,96},{40,104},{48,112},{56,120},{... | collective-permute-start | bytes 98312 | tf_op jit(solution)/shard_map/ppermute | solution.py:461
  74.9 5.1 %collective-permute-start.12 = (bf16[128,128]{1,0:T(8,128)(2,1)S(1)}, bf16[128,128]{1,0:T(8,128)(2,1)S(1)}, u32[]{:S(2)}, u32[]{:S(2)}) collective-permute-start(bf16[128,128]{1,0:T(8,128)(2,1)S(1)} %get-tuple-element.131.p0), channel_id=1, source_target_pairs={{0,32},{8,40},{16,48},{24,56},{32,64},{40,72},{48,80},{56,88},{64,... | collective-permute-start | bytes 98312 | tf_op jit(solution)/shard_map/ppermute | solution.py:461
  80.9 7.0 %collective-permute-start.15 = (bf16[128,128]{1,0:T(8,128)(2,1)S(1)}, bf16[128,128]{1,0:T(8,128)(2,1)S(1)}, u32[]{:S(2)}, u32[]{:S(2)}) collective-permute-start(bf16[128,128]{1,0:T(8,128)(2,1)S(1)} %get-tuple-element.139), channel_id=1, source_target_pairs={{0,8},{8,16},{16,24},{24,0},{32,40},{40,48},{48,56},{56,32},{64,72... | collective-permute-start | bytes 98312 | tf_op jit(solution)/shard_map/ppermute | solution.py:461
  81.6 6.3 %collective-permute-start.16 = (bf16[128,128]{1,0:T(8,128)(2,1)S(1)}, bf16[128,128]{1,0:T(8,128)(2,1)S(1)}, u32[]{:S(2)}, u32[]{:S(2)}) collective-permute-start(bf16[128,128]{1,0:T(8,128)(2,1)S(1)} %get-tuple-element.140), channel_id=1, source_target_pairs={{0,16},{8,24},{16,0},{24,8},{32,48},{40,56},{48,32},{56,40},{64,80... | collective-permute-start | bytes 98312 | tf_op jit(solution)/shard_map/ppermute | solution.py:461
  83.6 4.3 %collective-permute-start.17 = (bf16[128,128]{1,0:T(8,128)(2,1)S(1)}, bf16[128,128]{1,0:T(8,128)(2,1)S(1)}, u32[]{:S(2)}, u32[]{:S(2)}) collective-permute-start(bf16[128,128]{1,0:T(8,128)(2,1)S(1)} %get-tuple-element.141), channel_id=1, source_target_pairs={{0,24},{8,0},{16,8},{24,16},{32,56},{40,32},{48,40},{56,48},{64,88... | collective-permute-start | bytes 98312 | tf_op jit(solution)/shard_map/ppermute | solution.py:461
  84.3 3.6 %copy-start.2 = (f32[4,1024]{1,0:T(4,128)S(1)}, f32[4,1024]{1,0:T(4,128)}, u32[]{:S(2)}) copy-start(f32[4,1024]{1,0:T(4,128)} %b_ref.3) | copy-start | bytes 49156
Sparse Core Ops, SparseCore 0:
  9.7 36.7 all-gather.1
